TPU v7x, 32 devices: a whole 2x2x4 slice. The times are simulated.
32 devices in a mesh: groups: 2 (over x), slab: 16 (over z, y, core).
Axes of the slice: x: 2, y: 2, z: 4, core: 2. Of those that a mesh axis runs over, the one named last changes fastest.
Arguments:
- features: bfloat16 [128, 16, 16, 128], P(('groups', 'slab')), parts along dimension 0, may hold values from -6 to 6
- filters_first: bfloat16 [3456, 128], P('slab'), may hold values from -0.109375 to 0.109375
- filters_second: bfloat16 [3456, 128], P('slab'), may hold values from -0.109375 to 0.109375
- cotangent: bfloat16 [128, 16, 16, 128], P(('groups', 'slab')), parts along dimension 0, may hold values from -0.125 to 0.125
Outputs:
- output: bfloat16 [128, 16, 16, 128], P(('groups', 'slab')), parts along dimension 0
- grad_first: float32 [6912, 128], P(('groups', 'slab')), parts along dimension 0
- grad_second: float32 [6912, 128], P(('groups', 'slab')), parts along dimension 0
There are 2 independent parts, one for each index of `groups`. A program takes and returns all parts, laid end to end along the dimension named above; an argument that names none is the same for every part. Nothing has to cross between parts.
All inputs are finite; a program needn't handle non-finite values.
Results may differ from a plain program's by a relative error of at most 0.0049.
Values may be sent and summed in bfloat16 or wider, within the bound.
No kernel may reach another device: no remote copies, remote signals or barrier semaphores. Data moves between devices by JAX's collectives and lax.ppermute only.
A program may use at most 64 MiB of HBM per device.

v0:
```python
import jax
import jax.numpy as jnp
from jax import lax
from jax.sharding import PartitionSpec as P

inv_root_two = 0.7071067811865476
inv_root_two_pi = 0.3989422804014327


def extended(block, sides, width):
    for axis, dim in sides:
        count = lax.axis_size(axis)
        forward = [(i, i + 1) for i in range(count - 1)]
        backward = [(target, source) for source, target in forward]
        low = lax.ppermute(
            lax.slice_in_dim(block, block.shape[dim] - width, None, axis=dim), axis, forward
        )
        high = lax.ppermute(lax.slice_in_dim(block, 0, width, axis=dim), axis, backward)
        block = jnp.concatenate([low, block, high], axis=dim)
    return block


def shifted(padded, offset_z, offset_y, offset_x, shape):
    piece = padded[
        offset_z : offset_z + shape[0],
        offset_y : offset_y + shape[1],
        offset_x : offset_x + shape[2],
        :,
    ]
    return piece.reshape(-1, shape[3])


def forward_conv(padded, weight, shape):
    channels = shape[3]
    total = jnp.zeros((shape[0] * shape[1] * shape[2], channels), jnp.float32)
    for offset_z in range(3):
        for offset_y in range(3):
            for offset_x in range(3):
                tap = (offset_z * 3 + offset_y) * 3 + offset_x
                block = weight[tap * channels : (tap + 1) * channels]
                total = total + jnp.dot(
                    shifted(padded, offset_z, offset_y, offset_x, shape),
                    block,
                    preferred_element_type=jnp.float32,
                )
    return total.reshape(shape)


def transpose_conv(padded, weight, shape):
    channels = shape[3]
    total = jnp.zeros((shape[0] * shape[1] * shape[2], channels), jnp.float32)
    for offset_z in range(3):
        for offset_y in range(3):
            for offset_x in range(3):
                tap = (offset_z * 3 + offset_y) * 3 + offset_x
                block = weight[tap * channels : (tap + 1) * channels]
                piece = shifted(padded, 2 - offset_z, 2 - offset_y, 2 - offset_x, shape)
                total = total + lax.dot_general(
                    piece, block, (((1,), (1,)), ((), ())), preferred_element_type=jnp.float32
                )
    return total.reshape(shape)


def weight_grad(padded, gradient, shape):
    flat = gradient.reshape(-1, shape[3])
    blocks = []
    for offset_z in range(3):
        for offset_y in range(3):
            for offset_x in range(3):
                piece = shifted(padded, offset_z, offset_y, offset_x, shape)
                blocks.append(
                    lax.dot_general(
                        piece, flat, (((0,), (0,)), ((), ())), preferred_element_type=jnp.float32
                    )
                )
    return jnp.concatenate(blocks, axis=0)


def gelu_parts(value):
    normal_cdf = 0.5 * (1.0 + lax.erf(value * inv_root_two))
    slope = normal_cdf + value * jnp.exp(-0.5 * value * value) * inv_root_two_pi
    return (value * normal_cdf, slope)


def pad_plane(value):
    return jnp.pad(value, ((0, 0), (1, 1), (1, 1), (0, 0)))


def shards(features, filters_first, filters_second, cotangent):
    shape = features.shape
    bank_first = lax.all_gather(filters_first, "slab", axis=0, tiled=True)
    padded_input = pad_plane(extended(features, (("slab", 0),), 1))
    pre = forward_conv(padded_input, bank_first, shape)
    active, slope = gelu_parts(pre)
    hidden = active.astype(jnp.bfloat16)
    bank_second = lax.all_gather(filters_second, "slab", axis=0, tiled=True)
    padded_hidden = pad_plane(extended(hidden, (("slab", 0),), 1))
    output = forward_conv(padded_hidden, bank_second, shape).astype(jnp.bfloat16)
    bank_back = lax.all_gather(filters_second, "slab", axis=0, tiled=True)
    padded_grad = pad_plane(extended(cotangent, (("slab", 0),), 1))
    grad_hidden = transpose_conv(padded_grad, bank_back, shape)
    term_second = weight_grad(padded_hidden, cotangent, shape)
    grad_second = lax.psum_scatter(term_second, "slab", scatter_dimension=0, tiled=True)
    grad_pre = (grad_hidden * slope).astype(jnp.bfloat16)
    term_first = weight_grad(padded_input, grad_pre, shape)
    grad_first = lax.psum_scatter(term_first, "slab", scatter_dimension=0, tiled=True)
    return (output, grad_first, grad_second)


def solution(mesh):
    return jax.shard_map(
        shards,
        mesh=mesh,
        in_specs=(
            P(("groups", "slab"), None, None, None),
            P("slab", None),
            P("slab", None),
            P(("groups", "slab"), None, None, None),
        ),
        out_specs=(
            P(("groups", "slab"), None, None, None),
            P(("groups", "slab"), None),
            P(("groups", "slab"), None),
        ),
        check_vma=False,
    )
```

profile of v0, /device:TPU:0, one launch (start us, length us, event | category | flops | bytes accessed | tf_op | source)
XLA Modules:
  0.0 241.7 jit_solution(6252223290264155383)
XLA Ops:
  7.2 0.9 fusion.236
  8.1 2.4 collective-permute-start
  10.5 1.3 collective-permute-start.1
  12.7 5.2 %collective-permute-start.4 = (bf16[1,16,16,128]{3,2,1,0:T(8,128)(2,1)S(1)}, bf16[1,16,16,128]{3,2,1,0:T(8,128)(2,1)S(1)}, u32[]{:S(2)}, u32[]{:S(2)}) collective-permute-start(bf16[1,16,16,128]{3,2,1,0:T(8,128)(2,1)S(1)} %get-tuple-element.79), channel_id=1, source_target_pairs={{0,1},{1,2},{2,3},{3,4},{4,5},{5,6},{6,7},{7,8},{8,9},{9,10},{10,1... | collective-permute-start | bytes 196616 | tf_op jit(solution)/shard_map/ppermute | solution.py:15
  17.9 1.3 collective-permute-start.5
  19.2 26.8 %all_gather.7 = bf16[3456,128]{1,0:T(8,128)(2,1)S(1)} all-gather(bf16[216,128]{1,0:T(8,128)(2,1)} %param.5), channel_id=1, replica_groups=mesh['groups'=2,'slab'=16] {'slab'}, dimensions={0}, use_global_device_ids=true | all-gather | bytes 940032 | tf_op jit(solution)/shard_map/all_gather | solution.py:91
  46.0 20.2 %all_gather.8 = bf16[3456,128]{1,0:T(8,128)(2,1)S(1)} all-gather(bf16[216,128]{1,0:T(8,128)(2,1)} %param.6), channel_id=1, replica_groups=mesh['groups'=2,'slab'=16] {'slab'}, dimensions={0}, use_global_device_ids=true | all-gather | bytes 940032 | tf_op jit(solution)/shard_map/all_gather | solution.py:96
  66.4 0.9 fusion.232
  68.8 1.1 fusion.228
  82.6 2.3 collective-permute-start.2
  84.8 1.5 collective-permute-start.3
  86.3 0.9 fusion.62
  87.2 0.9 fusion.61
  88.1 0.9 fusion.60
  89.0 0.9 fusion.59
  89.9 0.9 fusion.12
  90.8 0.9 fusion.58
  91.7 0.9 fusion.57
  92.6 0.9 fusion.56
  93.5 0.9 fusion.55
  94.4 0.9 fusion.54
  95.3 0.9 fusion.53
  96.2 0.9 fusion.52
  98.0 0.9 fusion.50
  98.9 0.9 fusion.49
  99.8 0.9 fusion.48
  100.7 0.9 fusion.47
  101.6 0.9 fusion.46
  102.5 0.9 fusion.45
  103.4 0.9 fusion.44
  104.3 0.9 fusion.43
  105.2 0.9 fusion.42
  106.1 0.9 fusion.11
  107.0 0.9 fusion.41
  107.9 0.9 fusion.40
  108.8 0.9 fusion.39
  109.6 0.9 fusion.38
  110.9 0.9 fusion.37
  112.0 0.9 fusion.36
  112.9 0.9 fusion.35
  113.8 0.9 fusion.34
  116.5 0.9 fusion.32
  117.4 0.9 fusion.31
  118.3 0.9 fusion.30
  119.2 0.9 fusion.29
  120.1 0.9 fusion.28
  121.0 0.9 fusion.27
  121.9 0.9 fusion.26
  123.6 0.9 fusion.24
  124.5 0.9 fusion.23
  125.4 0.9 fusion.22
  126.3 0.9 fusion.21
  127.2 0.9 fusion.20
  128.1 0.9 fusion.19
  129.0 0.9 fusion.18
  129.9 0.9 fusion.17
  131.7 0.9 fusion.16
  132.6 0.9 fusion.15
  133.5 0.9 fusion.14
  135.7 0.9 fusion.13
  136.6 1.9 fusion.230
  144.8 0.9 fusion.8
  145.7 25.7 %reduce-scatter.7.cloned.1.call-done = f32[216,128]{1,0:T(8,128)} async-done(((f32[3456,128]{1,0:T(8,128)}), f32[216,128]{1,0:T(8,128)}) %reduce-scatter.7.cloned.1.call-update) | async-done | bytes 110608
  171.4 63.5 %reduce-scatter.9.cloned.1.call-done = f32[216,128]{1,0:T(8,128)} async-done(((f32[3456,128]{1,0:T(8,128)}), f32[216,128]{1,0:T(8,128)}) %reduce-scatter.9.cloned.1.call-update) | async-done | bytes 110608
  (135 shorter events, 27.2 us)
Async XLA Ops:
  7.2 59.0 %copy-start = (bf16[4,16,16,128]{3,2,1,0:T(8,128)(2,1)S(1)}, bf16[4,16,16,128]{3,2,1,0:T(8,128)(2,1)}, u32[]{:S(2)}) copy-start(bf16[4,16,16,128]{3,2,1,0:T(8,128)(2,1)} %param.4) | copy-start | bytes 786436
  7.2 164.2 %reduce-scatter.7.cloned.1.call-start = ((), (), s32[]{:S(2)}) async-start(), calls=%async_computation.2 | async-start | bytes 1880064
  8.1 58.0 %collective-permute-start = (bf16[1,16,16,128]{3,2,1,0:T(8,128)(2,1)S(1)}, bf16[1,16,16,128]{3,2,1,0:T(8,128)(2,1)S(1)}, u32[]{:S(2)}, u32[]{:S(2)}) collective-permute-start(bf16[1,16,16,128]{3,2,1,0:T(8,128)(2,1)S(1)} %get-tuple-element.87), channel_id=1, source_target_pairs={{0,1},{1,2},{2,3},{3,4},{4,5},{5,6},{6,7},{7,8},{8,9},{9,10},{10,1... | collective-permute-start | bytes 196616 | tf_op jit(solution)/shard_map/ppermute | solution.py:15
  10.5 55.6 %collective-permute-start.1 = (bf16[1,16,16,128]{3,2,1,0:T(8,128)(2,1)S(1)}, bf16[1,16,16,128]{3,2,1,0:T(8,128)(2,1)S(1)}, u32[]{:S(2)}, u32[]{:S(2)}) collective-permute-start(bf16[1,16,16,128]{3,2,1,0:T(8,128)(2,1)S(1)} %get-tuple-element.88), channel_id=1, source_target_pairs={{1,0},{2,1},{3,2},{4,3},{5,4},{6,5},{7,6},{8,7},{9,8},{10,9},{11,1... | collective-permute-start | bytes 196616 | tf_op jit(solution)/shard_map/ppermute | solution.py:18
  12.7 54.9 %collective-permute-start.4 = (bf16[1,16,16,128]{3,2,1,0:T(8,128)(2,1)S(1)}, bf16[1,16,16,128]{3,2,1,0:T(8,128)(2,1)S(1)}, u32[]{:S(2)}, u32[]{:S(2)}) collective-permute-start(bf16[1,16,16,128]{3,2,1,0:T(8,128)(2,1)S(1)} %get-tuple-element.79), channel_id=1, source_target_pairs={{0,1},{1,2},{2,3},{3,4},{4,5},{5,6},{6,7},{7,8},{8,9},{9,10},{10,1... | collective-permute-start | bytes 196616 | tf_op jit(solution)/shard_map/ppermute | solution.py:15
  17.9 49.7 %collective-permute-start.5 = (bf16[1,16,16,128]{3,2,1,0:T(8,128)(2,1)S(1)}, bf16[1,16,16,128]{3,2,1,0:T(8,128)(2,1)S(1)}, u32[]{:S(2)}, u32[]{:S(2)}) collective-permute-start(bf16[1,16,16,128]{3,2,1,0:T(8,128)(2,1)S(1)} %get-tuple-element.80), channel_id=1, source_target_pairs={{1,0},{2,1},{3,2},{4,3},{5,4},{6,5},{7,6},{8,7},{9,8},{10,9},{11,1... | collective-permute-start | bytes 196616 | tf_op jit(solution)/shard_map/ppermute | solution.py:18
  67.4 1.0 copy-start.1
  82.6 28.0 %collective-permute-start.2 = (bf16[1,16,16,128]{3,2,1,0:T(8,128)(2,1)S(1)}, bf16[1,16,16,128]{3,2,1,0:T(8,128)(2,1)S(1)}, u32[]{:S(2)}, u32[]{:S(2)}) collective-permute-start(bf16[1,16,16,128]{3,2,1,0:T(8,128)(2,1)S(1)} %get-tuple-element.83), channel_id=1, source_target_pairs={{0,1},{1,2},{2,3},{3,4},{4,5},{5,6},{6,7},{7,8},{8,9},{9,10},{10,1... | collective-permute-start | bytes 196616 | tf_op jit(solution)/shard_map/ppermute | solution.py:15
  84.8 25.8 %collective-permute-start.3 = (bf16[1,16,16,128]{3,2,1,0:T(8,128)(2,1)S(1)}, bf16[1,16,16,128]{3,2,1,0:T(8,128)(2,1)S(1)}, u32[]{:S(2)}, u32[]{:S(2)}) collective-permute-start(bf16[1,16,16,128]{3,2,1,0:T(8,128)(2,1)S(1)} %get-tuple-element.84), channel_id=1, source_target_pairs={{1,0},{2,1},{3,2},{4,3},{5,4},{6,5},{7,6},{8,7},{9,8},{10,9},{11,1... | collective-permute-start | bytes 196616 | tf_op jit(solution)/shard_map/ppermute | solution.py:18
  110.6 124.3 %reduce-scatter.9.cloned.1.call-start = ((), (), s32[]{:S(2)}) async-start(), calls=%async_computation.3 | async-start | bytes 1880064
  140.0 1.0 copy-start.11
  140.3 1.0 copy-start.10
  140.3 1.4 copy-start.9
  141.2 1.0 copy-start.8
  141.4 1.0 copy-start.7
  141.7 1.0 copy-start.6
  142.2 1.0 copy-start.5
  142.4 1.0 copy-start.4
  143.4 1.0 copy-start.3
  143.6 1.0 copy-start.2
Sparse Core Ops, SparseCore 0:
  110.7 60.6 reduce-scatter.6
  175.7 59.1 reduce-scatter.8
where the time goes:
time: 242 us
  waiting for transfers between devices  89.2 us (37%)
  matrix products  66.5 us (27%)
  blocking collectives  47 us (19%)
  between operations  14.9 us (6%)
  starting transfers between devices  13.9 us (6%)
  local copies, waits for them, and re-layouts  9.11 us (4%)
    unnamed x4, waiting for transfers between devices  89.2 us
    dot_general x54, matrix products, weight_grad(): lax.dot_general(piece, flat, (((0,), (0,)), ((), ())), preferred_element_...  48.4 us
    all_gather x1, blocking collectives, shards(): bank_first = lax.all_gather(filters_first, 'slab', axis=0, tiled=True)  26.8 us
    all_gather x1, blocking collectives, shards(): bank_second = lax.all_gather(filters_second, 'slab', axis=0, tiled=True)  20.2 us
    dot_general x54, matrix products, forward_conv(): jnp.dot(shifted(padded, offset_z, offset_y, offset_x, shape), block, pref...  12.1 us
    ppermute x3, starting transfers between devices, extended(): lax.ppermute(lax.slice_in_dim(block, block.shape[dim] - width, None, axis...  9.78 us
    dot_general x27, matrix products, transpose_conv(): lax.dot_general(piece, block, (((1,), (1,)), ((), ())), preferred_element...  6.11 us
  transfers between devices with their start and end apart: 8, of which 2 were waited for; matrix products, arithmetic and copies ran while one was open for 25% of the time, Pallas kernels for 0%

commit v1 on v0

v1 whole, which is shorter than its diff:
```python
import functools

import jax
import jax.numpy as jnp
from jax import lax
from jax.experimental import pallas as pl
from jax.experimental.pallas import tpu as pltpu
from jax.sharding import PartitionSpec as P

inv_root_two = 0.7071067811865476
inv_root_two_pi = 0.3989422804014327

BF16 = jnp.bfloat16
F32 = jnp.float32
MIB = 1 << 20


def gelu_parts(value):
    normal_cdf = 0.5 * (1.0 + lax.erf(value * inv_root_two))
    slope = normal_cdf + value * jnp.exp(-0.5 * value * value) * inv_root_two_pi
    return (value * normal_cdf, slope)


def local_call(kernel, name, outs, args, scratch=(), flops=0, limit=24 * MIB, scalars=0):
    moved = sum(a.size * a.dtype.itemsize for a in args)
    moved += sum(o.size * o.dtype.itemsize for o in outs)
    specs = [
        pl.BlockSpec(memory_space=pltpu.SMEM if at < scalars else pltpu.VMEM)
        for at in range(len(args))
    ]
    return pl.pallas_call(
        kernel,
        out_shape=list(outs),
        in_specs=specs,
        out_specs=[pl.BlockSpec(memory_space=pltpu.VMEM) for _ in outs],
        scratch_shapes=list(scratch),
        name=name,
        compiler_params=pltpu.CompilerParams(vmem_limit_bytes=limit),
        cost_estimate=pl.CostEstimate(flops=flops, bytes_accessed=moved, transcendentals=0),
    )(*args)


def like(shape, dtype):
    return jax.ShapeDtypeStruct(shape, dtype)


def write_shifted(dst, at, plane):
    height, width, channels = plane.shape
    flat = plane.astype(F32).reshape(height * width, channels)
    column = lax.broadcasted_iota(jnp.int32, flat.shape, 0) % width
    left = jnp.where(column == 0, 0.0, pltpu.roll(flat, 1, 0))
    right = jnp.where(column == width - 1, 0.0, pltpu.roll(flat, height * width - 1, 0))
    row = jnp.zeros((1, width, 3 * channels), BF16)
    dst[at, 0:1] = row
    dst[at, height + 1 : height + 2] = row
    for block, value in enumerate((left, flat, right)):
        dst[at, 1 : height + 1, :, block * channels : (block + 1) * channels] = (
            value.astype(BF16).reshape(height, width, channels)
        )


def prepare_kernel(f_ref, g_ref, lo_ref, hi_ref, xf_ref, xg_ref, xt_ref):
    planes, height, width, channels = f_ref.shape
    for p in range(2):
        write_shifted(xf_ref, p, lo_ref[p])
        write_shifted(xf_ref, planes + 2 + p, hi_ref[p])
    write_shifted(xg_ref, 0, lo_ref[2])
    write_shifted(xg_ref, planes + 1, hi_ref[2])
    for p in range(planes):
        write_shifted(xf_ref, p + 2, f_ref[p])
        write_shifted(xg_ref, p + 1, g_ref[p])

    def transposed(p, _):
        for b in range(3):
            for c in range(3):
                window = xf_ref[p + 1, b : b + height, :, c * channels : (c + 1) * channels]
                xt_ref[p, b * 3 + c] = window.reshape(height * width, channels).T
        return 0

    lax.fori_loop(0, planes + 2, transposed, 0)


def window(ref, first, planes):
    height, width, lanes = ref.shape[1] - 2, ref.shape[2], ref.shape[3]
    return jnp.concatenate(
        [
            ref[first : first + planes, b : b + height].reshape(planes * height * width, lanes)
            for b in range(3)
        ],
        axis=1,
    )


def conv_rows(ref, first, planes, weight_ref):
    depth = weight_ref.shape[0] // 3
    total = None
    for a in range(3):
        term = jnp.dot(
            window(ref, first + a, planes),
            weight_ref[a * depth : (a + 1) * depth],
            preferred_element_type=F32,
        )
        total = term if total is None else total + term
    return total


def assemble(me, pieces, dst):
    rows = pieces[0].shape[1]
    for low, piece in enumerate(pieces):
        for d in range(piece.shape[0]):
            start = pl.multiple_of((me ^ (4 * d + low)) * rows, 8)
            dst[pl.ds(start, rows)] = piece[d]


def split_terms(me, total_ref, send_ref, keep_ref):
    count, rows, _ = keep_ref.shape
    core = me % 2
    for k in range(count):
        own = pl.multiple_of((2 * k + core) * rows, 8)
        other = pl.multiple_of((2 * k + 1 - core) * rows, 8)
        keep_ref[k] = total_ref[pl.ds(own, rows)]
        send_ref[k] = total_ref[pl.ds(other, rows)].astype(BF16)


def first_kernel(
    me_ref, w0, w1, w2, w3, xf_ref, xg_ref, bank_ref, hidden_ref, slope_ref, send_ref, keep_ref, total_ref
):
    me = me_ref[0]
    planes, height, width, channels = hidden_ref.shape
    assemble(me, (w0, w1, w2, w3), bank_ref)
    pre = conv_rows(xf_ref, 1, planes, bank_ref)
    active, slope = gelu_parts(pre)
    slope_ref[...] = slope
    hidden = active.astype(BF16)
    hidden_ref[...] = hidden.reshape(hidden_ref.shape)
    flipped = hidden.T
    for a in range(3):
        out = jnp.dot(flipped, window(xg_ref, 2 - a, planes), preferred_element_type=F32)
        for b in range(3):
            for c in range(3):
                tap = (a * 3 + b) * 3 + c
                source = (2 - b) * 3 + 2 - c
                total_ref[tap * channels : (tap + 1) * channels] = out[
                    :, source * channels : (source + 1) * channels
                ]
    split_terms(me, total_ref, send_ref, keep_ref)


def second_kernel(
    me_ref, w0, w1, w2, w3, xg_ref, xt_ref, slope_ref, bank_ref, send_ref, keep_ref, back_ref, total_ref
):
    me = me_ref[0]
    channels = slope_ref.shape[1]
    planes = xg_ref.shape[0] - 2
    cells = slope_ref.shape[0] // planes
    assemble(me, (w0, w1, w2, w3), bank_ref)
    for tap in range(27):
        a, rest = divmod(tap, 9)
        to = (2 - a) * 9 + 8 - rest
        back_ref[to * channels : (to + 1) * channels] = bank_ref[
            tap * channels : (tap + 1) * channels
        ].T
    grad_hidden = conv_rows(xg_ref, 0, planes, back_ref)
    grad_pre = (grad_hidden * slope_ref[...]).astype(BF16)
    depth = 9 * channels
    for a in range(3):
        total = None
        for z in range(planes):
            term = jnp.dot(
                xt_ref[z + a].reshape(depth, cells),
                grad_pre[z * cells : (z + 1) * cells],
                preferred_element_type=F32,
            )
            total = term if total is None else total + term
        total_ref[a * depth : (a + 1) * depth] = total
    split_terms(me, total_ref, send_ref, keep_ref)


def output_kernel(me_ref, count, xf_ref, bank_ref, hidden_ref, second_ref, out_ref, xh_ref):
    me = me_ref[0]
    planes, height, width, channels = hidden_ref.shape
    for at, first, inside in ((0, 0, me > 0), (planes + 1, planes + 1, me < count - 1)):
        active, _ = gelu_parts(conv_rows(xf_ref, first, 1, bank_ref))
        active = jnp.where(inside, active, 0.0)
        write_shifted(xh_ref, at, active.astype(BF16).reshape(height, width, channels))
    for p in range(planes):
        write_shifted(xh_ref, p + 1, hidden_ref[p])
    out = conv_rows(xh_ref, 0, planes, second_ref)
    out_ref[...] = out.astype(BF16).reshape(out_ref.shape)


def sum_pair_kernel(me_ref, keep_ref, got_ref, send_ref, own_ref):
    half = (me_ref[0] // 2) % 2
    for d in range(own_ref.shape[0]):
        own_ref[d] = keep_ref[2 * d + half] + got_ref[2 * d + half].astype(F32)
        other = 2 * d + 1 - half
        send_ref[d] = (keep_ref[other] + got_ref[other].astype(F32)).astype(BF16)


def sum_rows_kernel(me_ref, keep_ref, got_ref, own_ref, *send_refs):
    at = me_ref[0] // 4
    own_ref[...] = keep_ref[at] + got_ref[at].astype(F32)
    for d, send_ref in enumerate(send_refs, 1):
        send_ref[...] = (keep_ref[at ^ d] + got_ref[at ^ d].astype(F32)).astype(BF16)


def sum_last_kernel(keep_ref, *refs):
    total = keep_ref[...]
    for ref in refs[:-1]:
        total = total + ref[...].astype(F32)
    refs[-1][...] = total


def swap(value, count, distance):
    return lax.ppermute(value, "slab", [(i, i ^ distance) for i in range(count)])


def gather_bank(shard, count):
    own = jnp.stack([shard] + [swap(shard, count, 4 * d) for d in range(1, count // 4)])
    across = swap(own, count, 2)
    return own, swap(own, count, 1), across, swap(across, count, 1)


def scatter_terms(me, send, keep, count, rows, channels, name):
    groups = count // 4
    got = swap(send, count, 1)
    send, keep = local_call(
        sum_pair_kernel,
        name + "_pair",
        [like((groups, rows, channels), BF16), like((groups, rows, channels), F32)],
        [me, keep, got],
        scalars=1,
    )
    got = swap(send, count, 2)
    own, *sends = local_call(
        sum_rows_kernel,
        name + "_rows",
        [like((rows, channels), F32)] + [like((rows, channels), BF16)] * (groups - 1),
        [me, keep, got],
        scalars=1,
    )
    gots = [swap(value, count, 4 * d) for d, value in enumerate(sends, 1)]
    (total,) = local_call(
        sum_last_kernel, name + "_last", [like((rows, channels), F32)], [own, *gots]
    )
    return total


def shards(count, features, filters_first, filters_second, cotangent):
    planes, height, width, channels = features.shape
    cells = planes * height * width
    rows = filters_first.shape[0]
    taps = 27 * channels
    direct = count in (8, 16) and rows % 8 == 0
    me = lax.axis_index("slab").astype(jnp.int32).reshape(1)
    up = [(i, i + 1) for i in range(count - 1)]
    down = [(i + 1, i) for i in range(count - 1)]
    low = lax.ppermute(jnp.concatenate([features[-2:], cotangent[-1:]]), "slab", up)
    high = lax.ppermute(jnp.concatenate([features[:2], cotangent[:1]]), "slab", down)
    if direct:
        first = gather_bank(filters_first, count)
        second = gather_bank(filters_second, count)
        shard_rows = rows
    else:
        shard_rows = taps // 16
        first = whole_pieces(filters_first, shard_rows)
        second = whole_pieces(filters_second, shard_rows)
    place = me if direct else jnp.zeros((1,), jnp.int32)
    kept = taps // shard_rows // 2

    xf, xg, xt = local_call(
        prepare_kernel,
        "shifted_planes",
        [
            like((planes + 4, height + 2, width, 3 * channels), BF16),
            like((planes + 2, height + 2, width, 3 * channels), BF16),
            like((planes + 2, 9, channels, height * width), BF16),
        ],
        [features, cotangent, low, high],
    )
    flops = 2 * cells * taps * channels
    bank, hidden, slope, send_second, keep_second = local_call(
        first_kernel,
        "hidden_and_second_grad",
        [
            like((taps, channels), BF16),
            like(features.shape, BF16),
            like((cells, channels), F32),
            like((kept, shard_rows, channels), BF16),
            like((kept, shard_rows, channels), F32),
        ],
        [place, *first, xf, xg],
        scratch=[pltpu.VMEM((taps, channels), F32)],
        flops=2 * flops,
        scalars=1,
    )
    bank_second, send_first, keep_first = local_call(
        second_kernel,
        "first_grad",
        [
            like((taps, channels), BF16),
            like((kept, shard_rows, channels), BF16),
            like((kept, shard_rows, channels), F32),
        ],
        [place, *second, xg, xt, slope],
        scratch=[pltpu.VMEM((taps, channels), BF16), pltpu.VMEM((taps, channels), F32)],
        flops=2 * flops,
        scalars=1,
    )
    (output,) = local_call(
        lambda me_ref, *refs: output_kernel(me_ref, count, *refs),
        "output_conv",
        [like(features.shape, BF16)],
        [me, xf, bank, hidden, bank_second],
        scratch=[pltpu.VMEM((planes + 2, height + 2, width, 3 * channels), BF16)],
        flops=flops,
        scalars=1,
    )
    if direct:
        grads = [
            scatter_terms(me, send, keep, count, rows, channels, name)
            for send, keep, name in (
                (send_second, keep_second, "second"),
                (send_first, keep_first, "first"),
            )
        ]
    else:
        grads = [
            lax.psum_scatter(
                jnp.stack([keep, send.astype(F32)], 1).reshape(taps, channels),
                "slab",
                scatter_dimension=0,
                tiled=True,
            )
            for send, keep in ((send_second, keep_second), (send_first, keep_first))
        ]
    return (output, grads[1], grads[0])


def whole_pieces(shard, shard_rows):
    bank = lax.all_gather(shard, "slab", axis=0, tiled=True)
    parts = bank.reshape(-1, 4, shard_rows, bank.shape[1])
    return tuple(parts[:, low] for low in range(4))


def solution(mesh):
    return jax.shard_map(
        functools.partial(shards, mesh.shape["slab"]),
        mesh=mesh,
        in_specs=(
            P(("groups", "slab"), None, None, None),
            P("slab", None),
            P("slab", None),
            P(("groups", "slab"), None, None, None),
        ),
        out_specs=(
            P(("groups", "slab"), None, None, None),
            P(("groups", "slab"), None),
            P(("groups", "slab"), None),
        ),
        check_vma=False,
    )
```

time: 242 us -> 65.7 us (0.27)
  waiting for transfers between devices: 89.2 us -> 9.74 us
  matrix products: 66.5 us -> 0 us
  blocking collectives: 47 us -> 0 us
  starting transfers between devices: 13.9 us -> 34.3 us
  Pallas kernels: 0 us -> 16.9 us
  between operations: 14.9 us -> 0.8 us
  local copies, waits for them, and re-layouts: 9.11 us -> 1.88 us
    unnamed x4 -> x0, waiting for transfers between devices: 89.2 us -> none
    dot_general x135 -> x0, matrix products: 66.5 us -> none  [the longest x54 48.4 us: weight_grad(): lax.dot_general(piece, flat, (((0,), (0,)), ((), ())), preferred_element_...]
    all_gather x2 -> x0, blocking collectives: 47 us -> none  [the longest x1 26.8 us: shards(): bank_first = lax.all_gather(filters_first, 'slab', axis=0, tiled=True)]
    ppermute x6 -> x24, starting transfers between devices: 13.8 us -> 34.3 us  [the longest x22 31.7 us: swap(): lax.ppermute(value, 'slab', [(i, i ^ distance) for i in range(count)])]
    pallas_call x0 -> x10, Pallas kernels: none -> 16.9 us  [local_call(): pl.pallas_call(kernel, out_shape=list(outs), in_specs=specs, out_specs=[p...]
    ppermute x6 -> x24, waiting for transfers between devices: 0.02 us -> 9.74 us  [the longest x22 9.74 us: swap(): lax.ppermute(value, 'slab', [(i, i ^ distance) for i in range(count)])]
    slice x11 -> x2, local copies, waits for them, and re-layouts: 6.41 us -> 1.87 us  [the longest x1 0.99 us: shards(): features[:2]]
    unnamed x26 -> x4, local copies, waits for them, and re-layouts: 2.69 us -> 0.01 us
  transfers between devices with their start and end apart: 8 -> 24, of which waited for: 2 -> 4; matrix products, arithmetic and copies ran while one was open for 25% -> 6% of each run, Pallas kernels for 0% -> 25%
where the time goes in v1:
time: 65.7 us; the launch traced here: 65.4 us
  starting transfers between devices  34.3 us (52%)
  Pallas kernels  16.9 us (26%)
  waiting for transfers between devices  9.74 us (15%)
  local copies, waits for them, and re-layouts  1.88 us (3%)
  other arithmetic  1.73 us (3%)
  between operations  0.8 us (1%)
    ppermute x22, starting transfers between devices, swap(): lax.ppermute(value, 'slab', [(i, i ^ distance) for i in range(count)])  31.7 us
    pallas_call x10, Pallas kernels, local_call(): pl.pallas_call(kernel, out_shape=list(outs), in_specs=specs, out_specs=[p...  16.9 us
    ppermute x22, waiting for transfers between devices, swap(): lax.ppermute(value, 'slab', [(i, i ^ distance) for i in range(count)])  9.74 us
    another operation x2, other arithmetic, gather_bank(): jnp.stack([shard] + [swap(shard, count, 4 * d) for d in range(1, count //...  1.69 us
  transfers between devices with their start and end apart: 24, of which 4 were waited for; matrix products, arithmetic and copies ran while one was open for 6% of the time, Pallas kernels for 25%

profile of v1, /device:TPU:0, one launch (start us, length us, event | category | flops | bytes accessed | tf_op | source)
XLA Modules:
  0.0 65.4 jit_solution(12428254718203749068)
XLA Ops:
  0.6 0.0 copy-start.1
  0.7 3.1 %collective-permute-start.2 = (bf16[216,128]{1,0:T(8,128)(2,1)}, bf16[216,128]{1,0:T(8,128)(2,1)S(1)}, u32[]{:S(2)}, u32[]{:S(2)}) collective-permute-start(bf16[216,128]{1,0:T(8,128)(2,1)} %param.5), channel_id=1, source_target_pairs={{0,4},{1,5},{2,6},{3,7},{4,0},{5,1},{6,2},{7,3},{8,12},{9,13},{10,... | collective-permute-start | bytes 165896 | tf_op jit(solution)/shard_map/ppermute | solution.py:215
  3.7 2.6 %collective-permute-start.3 = (bf16[216,128]{1,0:T(8,128)(2,1)}, bf16[216,128]{1,0:T(8,128)(2,1)S(1)}, u32[]{:S(2)}, u32[]{:S(2)}) collective-permute-start(bf16[216,128]{1,0:T(8,128)(2,1)} %param.5), channel_id=1, source_target_pairs={{0,8},{1,9},{2,10},{3,11},{4,12},{5,13},{6,14},{7,15},{8,0},{9,1},... | collective-permute-start | bytes 165896 | tf_op jit(solution)/shard_map/ppermute | solution.py:215
  6.3 0.0 collective-permute-start.4
  6.3 0.9 %collective-permute-start.8 = (bf16[216,128]{1,0:T(8,128)(2,1)}, bf16[216,128]{1,0:T(8,128)(2,1)S(1)}, u32[]{:S(2)}, u32[]{:S(2)}) collective-permute-start(bf16[216,128]{1,0:T(8,128)(2,1)} %param.6), channel_id=1, source_target_pairs={{0,4},{1,5},{2,6},{3,7},{4,0},{5,1},{6,2},{7,3},{8,12},{9,13},{10,... | collective-permute-start | bytes 165896 | tf_op jit(solution)/shard_map/ppermute | solution.py:215
  7.2 3.5 %collective-permute-start.9 = (bf16[216,128]{1,0:T(8,128)(2,1)}, bf16[216,128]{1,0:T(8,128)(2,1)S(1)}, u32[]{:S(2)}, u32[]{:S(2)}) collective-permute-start(bf16[216,128]{1,0:T(8,128)(2,1)} %param.6), channel_id=1, source_target_pairs={{0,8},{1,9},{2,10},{3,11},{4,12},{5,13},{6,14},{7,15},{8,0},{9,1},... | collective-permute-start | bytes 165896 | tf_op jit(solution)/shard_map/ppermute | solution.py:215
  10.7 1.0 %fusion = (bf16[2,16,16,128]{3,2,1,0:T(8,128)(2,1)S(1)}, bf16[2,16,16,128]{3,2,1,0:T(8,128)(2,1)S(1)}) fusion(bf16[4,16,16,128]{3,2,1,0:T(8,128)(2,1)} %f_ref.1), kind=kLoop, calls=%fused_computation.4 | loop fusion | bytes 524288 | tf_op jit(solution)/shard_map/slice | solution.py:259
  11.7 0.9 %fusion.1 = (bf16[1,16,16,128]{3,2,1,0:T(8,128)(2,1)S(1)}, bf16[1,16,16,128]{3,2,1,0:T(8,128)(2,1)S(1)}) fusion(bf16[4,16,16,128]{3,2,1,0:T(8,128)(2,1)} %g_ref.1), kind=kLoop, calls=%fused_computation.5 | loop fusion | bytes 262144 | tf_op jit(solution)/shard_map/slice | solution.py:259
  12.6 0.0 collective-permute-done.2
  12.6 0.1 collective-permute-start.10
  12.7 0.0 collective-permute-done.3
  12.7 0.0 collective-permute-done.4
  12.7 0.8 %pad_maximum_fusion.w0 = bf16[4,216,128]{2,1,0:T(8,128)(2,1)S(1)} fusion(bf16[1,216,128]{2,1,0:T(8,128)(2,1)S(1)} %bitcast.16, bf16[1,216,128]{2,1,0:T(8,128)(2,1)S(1)} %bitcast.15, bf16[1,216,128]{2,1,0:T(8,128)(2,1)S(1)} %bitcast.14, bf16[1,216,128]{2,1,0:T(8,128)(2,1)} %bitcast.9), kind=kLoop, calls=%fused_computation | loop fusion | flops 331776 | bytes 442368 | tf_op jit(solution)/shard_map/stack | solution.py:219
  13.6 1.8 %collective-permute-start.6 = (bf16[4,216,128]{2,1,0:T(8,128)(2,1)S(1)}, bf16[4,216,128]{2,1,0:T(8,128)(2,1)S(1)}, u32[]{:S(2)}, u32[]{:S(2)}) collective-permute-start(bf16[4,216,128]{2,1,0:T(8,128)(2,1)S(1)} %pad_maximum_fusion.w0), channel_id=1, source_target_pairs={{0,2},{1,3},{2,0},{3,1},{4,6},{5,7},{6,4},{7,5},{8,10},{9,11},{10,... | collective-permute-start | bytes 663560 | tf_op jit(solution)/shard_map/ppermute | solution.py:215
  15.4 1.3 %collective-permute-start = (bf16[3,16,16,128]{3,2,1,0:T(8,128)(2,1)S(1)}, bf16[3,16,16,128]{3,2,1,0:T(8,128)(2,1)S(1)}, u32[]{:S(2)}, u32[]{:S(2)}) collective-permute-start(bf16[3,16,16,128]{3,2,1,0:T(8,128)(2,1)S(1)} %pad_maximum_fusion.2), channel_id=1, source_target_pairs={{0,1},{1,2},{2,3},{3,4},{4,5},{5,6},{6,7},{7,8},{8,9},{9,10},{10,1... | collective-permute-start | bytes 589832 | tf_op jit(solution)/shard_map/ppermute | solution.py:258
  16.7 0.0 collective-permute-done.8
  16.7 1.1 %collective-permute-start.5 = (bf16[4,216,128]{2,1,0:T(8,128)(2,1)S(1)}, bf16[4,216,128]{2,1,0:T(8,128)(2,1)S(1)}, u32[]{:S(2)}, u32[]{:S(2)}) collective-permute-start(bf16[4,216,128]{2,1,0:T(8,128)(2,1)S(1)} %pad_maximum_fusion.w0), channel_id=1, source_target_pairs={{0,1},{1,0},{2,3},{3,2},{4,5},{5,4},{6,7},{7,6},{8,9},{9,8},{10,11... | collective-permute-start | bytes 663560 | tf_op jit(solution)/shard_map/ppermute | solution.py:215
  17.8 0.0 collective-permute-done.9
  17.8 1.1 %collective-permute-done.10 = bf16[216,128]{1,0:T(8,128)(2,1)S(1)} collective-permute-done((bf16[216,128]{1,0:T(8,128)(2,1)}, bf16[216,128]{1,0:T(8,128)(2,1)S(1)}, u32[]{:S(2)}, u32[]{:S(2)}) %collective-permute-start.10) | collective-permute-done | bytes 55328 | tf_op jit(solution)/shard_map/ppermute | solution.py:215
  18.8 0.8 %pad_maximum_fusion.1.w0 = bf16[4,216,128]{2,1,0:T(8,128)(2,1)S(1)} fusion(bf16[1,216,128]{2,1,0:T(8,128)(2,1)S(1)} %bitcast.13, bf16[1,216,128]{2,1,0:T(8,128)(2,1)S(1)} %bitcast.12, bf16[1,216,128]{2,1,0:T(8,128)(2,1)S(1)} %bitcast.11, bf16[1,216,128]{2,1,0:T(8,128)(2,1)} %bitcast.10), kind=kLoop, calls=%fused_computation.1 | loop fusion | flops 331776 | bytes 442368 | tf_op jit(solution)/shard_map/stack | solution.py:219
  19.7 1.6 %collective-permute-start.12 = (bf16[4,216,128]{2,1,0:T(8,128)(2,1)S(1)}, bf16[4,216,128]{2,1,0:T(8,128)(2,1)S(1)}, u32[]{:S(2)}, u32[]{:S(2)}) collective-permute-start(bf16[4,216,128]{2,1,0:T(8,128)(2,1)S(1)} %pad_maximum_fusion.1.w0), channel_id=1, source_target_pairs={{0,2},{1,3},{2,0},{3,1},{4,6},{5,7},{6,4},{7,5},{8,10},{9,11},{10,... | collective-permute-start | bytes 663560 | tf_op jit(solution)/shard_map/ppermute | solution.py:215
  21.3 0.0 collective-permute-done.6.w2
  21.3 0.0 collective-permute-start.7
  21.3 1.3 %collective-permute-start.1 = (bf16[3,16,16,128]{3,2,1,0:T(8,128)(2,1)S(1)}, bf16[3,16,16,128]{3,2,1,0:T(8,128)(2,1)S(1)}, u32[]{:S(2)}, u32[]{:S(2)}) collective-permute-start(bf16[3,16,16,128]{3,2,1,0:T(8,128)(2,1)S(1)} %pad_maximum_fusion.3), channel_id=1, source_target_pairs={{1,0},{2,1},{3,2},{4,3},{5,4},{6,5},{7,6},{8,7},{9,8},{10,9},{11,1... | collective-permute-start | bytes 589832 | tf_op jit(solution)/shard_map/ppermute | solution.py:259
  22.6 0.0 collective-permute-done.lo_ref
  22.6 1.2 %collective-permute-start.11 = (bf16[4,216,128]{2,1,0:T(8,128)(2,1)S(1)}, bf16[4,216,128]{2,1,0:T(8,128)(2,1)S(1)}, u32[]{:S(2)}, u32[]{:S(2)}) collective-permute-start(bf16[4,216,128]{2,1,0:T(8,128)(2,1)S(1)} %pad_maximum_fusion.1.w0), channel_id=1, source_target_pairs={{0,1},{1,0},{2,3},{3,2},{4,5},{5,4},{6,7},{7,6},{8,9},{9,8},{10,11... | collective-permute-start | bytes 663560 | tf_op jit(solution)/shard_map/ppermute | solution.py:215
  23.8 2.3 %collective-permute-done.12.w2 = bf16[4,216,128]{2,1,0:T(8,128)(2,1)S(1)} collective-permute-done((bf16[4,216,128]{2,1,0:T(8,128)(2,1)S(1)}, bf16[4,216,128]{2,1,0:T(8,128)(2,1)S(1)}, u32[]{:S(2)}, u32[]{:S(2)}) %collective-permute-start.12) | collective-permute-done | bytes 221216 | tf_op jit(solution)/shard_map/ppermute | solution.py:215
  26.1 0.0 collective-permute-start.13
  26.1 0.0 collective-permute-done.1.hi_ref
  26.1 0.0 copy-done
  26.1 1.9 %shifted_planes.1 = (bf16[8,18,16,384]{3,2,1,0:T(8,128)(2,1)S(1)}, bf16[6,18,16,384]{3,2,1,0:T(8,128)(2,1)S(1)}, bf16[6,9,128,256]{3,2,1,0:T(8,128)(2,1)S(1)}) custom-call(bf16[4,16,16,128]{3,2,1,0:T(8,128)(2,1)S(1)} %copy-done, bf16[4,16,16,128]{3,2,1,0:T(8,128)(2,1)S(1)} %copy-done.1, bf16[3,16,16,128]{3,2,1,0:T(8,128)(2,1)S(1)} %collective-permute-done.lo_ref, ...), custom_call_target="tpu_custom_call" | custom-call | bytes 7553024 | tf_op jit(solution)/shard_map/shifted_planes/pallas_call | solution.py:31
  28.0 0.0 collective-permute-done.5.w1
  28.0 0.0 collective-permute-done.7.w3
  28.0 4.4 %hidden_and_second_grad.1 = (bf16[3456,128]{1,0:T(8,128)(2,1)S(1)}, bf16[4,16,16,128]{3,2,1,0:T(8,128)(2,1)S(1)}, f32[1024,128]{1,0:T(8,128)S(1)}, bf16[8,216,128]{2,1,0:T(8,128)(2,1)S(1)}, f32[8,216,128]{2,1,0:T(8,128)S(1)}) custom-call(s32[1]{0:T(128)} %bitcast.me_ref, bf16[4,216,128]{2,1,0:T(8,128)(2,1)S(1)} %pad_maximum_fusion.w0, ...), custom_call_target="tpu_custom_call" | custom-call | flops 1811939328 | bytes 6979588 | tf_op jit(solution)/shard_map/hidden_and_second_grad/pallas_call | solution.py:31
  32.4 2.8 %collective-permute-start.19 = (bf16[8,216,128]{2,1,0:T(8,128)(2,1)S(1)}, bf16[8,216,128]{2,1,0:T(8,128)(2,1)S(1)}, u32[]{:S(2)}, u32[]{:S(2)}) collective-permute-start(bf16[8,216,128]{2,1,0:T(8,128)(2,1)S(1)} %get-tuple-element.42), channel_id=1, source_target_pairs={{0,1},{1,0},{2,3},{3,2},{4,5},{5,4},{6,7},{7,6},{8,9},{9,8},{10,11... | collective-permute-start | bytes 1327112 | tf_op jit(solution)/shard_map/ppermute | solution.py:215
  35.2 0.0 collective-permute-done.11.w1
  35.2 0.0 collective-permute-done.13.w3
  35.2 5.2 %first_grad.1 = (bf16[3456,128]{1,0:T(8,128)(2,1)S(1)}, bf16[8,216,128]{2,1,0:T(8,128)(2,1)S(1)}, f32[8,216,128]{2,1,0:T(8,128)S(1)}) custom-call(s32[1]{0:T(128)} %bitcast.me_ref, bf16[4,216,128]{2,1,0:T(8,128)(2,1)S(1)} %pad_maximum_fusion.1.w0, bf16[4,216,128]{2,1,0:T(8,128)(2,1)S(1)} %collective-permute-done.11.w1, ...), custom_call_target="tpu_custom_call" | custom-call | flops 1811939328 | bytes 8486916 | tf_op jit(solution)/shard_map/first_grad/pallas_call | solution.py:31
  40.3 0.1 collective-permute-start.14
  40.4 0.0 collective-permute-done.19.got_ref
  40.4 0.1 second_pair.1
  40.5 1.6 %collective-permute-start.20 = (bf16[4,216,128]{2,1,0:T(8,128)(2,1)S(1)}, bf16[4,216,128]{2,1,0:T(8,128)(2,1)S(1)}, u32[]{:S(2)}, u32[]{:S(2)}) collective-permute-start(bf16[4,216,128]{2,1,0:T(8,128)(2,1)S(1)} %get-tuple-element.44), channel_id=1, source_target_pairs={{0,2},{1,3},{2,0},{3,1},{4,6},{5,7},{6,4},{7,5},{8,10},{9,11},{10,... | collective-permute-start | bytes 663560 | tf_op jit(solution)/shard_map/ppermute | solution.py:215
  42.1 0.0 collective-permute-done.14.got_ref
  42.2 0.1 first_pair.1
  42.3 1.6 %collective-permute-start.15 = (bf16[4,216,128]{2,1,0:T(8,128)(2,1)S(1)}, bf16[4,216,128]{2,1,0:T(8,128)(2,1)S(1)}, u32[]{:S(2)}, u32[]{:S(2)}) collective-permute-start(bf16[4,216,128]{2,1,0:T(8,128)(2,1)S(1)} %get-tuple-element.36), channel_id=1, source_target_pairs={{0,2},{1,3},{2,0},{3,1},{4,6},{5,7},{6,4},{7,5},{8,10},{9,11},{10,... | collective-permute-start | bytes 663560 | tf_op jit(solution)/shard_map/ppermute | solution.py:215
  43.9 4.9 %collective-permute-done.20.got_ref = bf16[4,216,128]{2,1,0:T(8,128)(2,1)S(1)} collective-permute-done((bf16[4,216,128]{2,1,0:T(8,128)(2,1)S(1)}, bf16[4,216,128]{2,1,0:T(8,128)(2,1)S(1)}, u32[]{:S(2)}, u32[]{:S(2)}) %collective-permute-start.20) | collective-permute-done | bytes 221216 | tf_op jit(solution)/shard_map/ppermute | solution.py:215
  48.8 0.1 second_rows.1
  48.9 1.6 %collective-permute-start.21 = (bf16[216,128]{1,0:T(8,128)(2,1)S(1)}, bf16[216,128]{1,0:T(8,128)(2,1)S(1)}, u32[]{:S(2)}, u32[]{:S(2)}) collective-permute-start(bf16[216,128]{1,0:T(8,128)(2,1)S(1)} %get-tuple-element.46), channel_id=1, source_target_pairs={{0,4},{1,5},{2,6},{3,7},{4,0},{5,1},{6,2},{7,3},{8,12},{9,13},{10,... | collective-permute-start | bytes 165896 | tf_op jit(solution)/shard_map/ppermute | solution.py:215
  50.5 3.8 %collective-permute-start.22 = (bf16[216,128]{1,0:T(8,128)(2,1)S(1)}, bf16[216,128]{1,0:T(8,128)(2,1)S(1)}, u32[]{:S(2)}, u32[]{:S(2)}) collective-permute-start(bf16[216,128]{1,0:T(8,128)(2,1)S(1)} %get-tuple-element.47), channel_id=1, source_target_pairs={{0,8},{1,9},{2,10},{3,11},{4,12},{5,13},{6,14},{7,15},{8,0},{9,1},... | collective-permute-start | bytes 165896 | tf_op jit(solution)/shard_map/ppermute | solution.py:215
  54.2 0.0 collective-permute-start.23
  54.2 0.0 collective-permute-done.15.got_ref
  54.2 0.1 first_rows.1
  54.3 0.6 collective-permute-start.16
  54.9 3.8 %collective-permute-start.17 = (bf16[216,128]{1,0:T(8,128)(2,1)S(1)}, bf16[216,128]{1,0:T(8,128)(2,1)S(1)}, u32[]{:S(2)}, u32[]{:S(2)}) collective-permute-start(bf16[216,128]{1,0:T(8,128)(2,1)S(1)} %get-tuple-element.39), channel_id=1, source_target_pairs={{0,8},{1,9},{2,10},{3,11},{4,12},{5,13},{6,14},{7,15},{8,0},{9,1},... | collective-permute-start | bytes 165896 | tf_op jit(solution)/shard_map/ppermute | solution.py:215
  58.8 0.0 collective-permute-done.21.refs_0_
  58.8 0.0 collective-permute-start.18
  58.8 3.8 %output_conv.1 = bf16[4,16,16,128]{3,2,1,0:T(8,128)(2,1)} custom-call(s32[1]{0:T(128)} %bitcast.me_ref, bf16[8,18,16,384]{3,2,1,0:T(8,128)(2,1)S(1)} %get-tuple-element.26.xf_ref.refs_0_, bf16[3456,128]{1,0:T(8,128)(2,1)S(1)} %get-tuple-element.28.refs_1_, bf16[4,16,16,128]{3,2,1,0:T(8,128)(2,1)S(1)} %get-tuple-element.29.refs_2_, ...), custom_call_target="tpu_custom_call" | custom-call | flops 905969664 | bytes 4063236 | tf_op jit(solution)/shard_map/output_conv/pallas_call | solution.py:31
  62.6 0.0 collective-permute-done.22.refs_1_
  62.6 0.0 collective-permute-done.23.refs_2_
  62.6 0.7 %second_last.1 = f32[216,128]{1,0:T(8,128)} custom-call(f32[216,128]{1,0:T(8,128)S(1)} %get-tuple-element.45.keep_ref, bf16[216,128]{1,0:T(8,128)(2,1)S(1)} %collective-permute-done.21.refs_0_, bf16[216,128]{1,0:T(8,128)(2,1)S(1)} %collective-permute-done.22.refs_1_, bf16[216,128]{1,0:T(8,128)(2,1)S(1)} %collective-permute-done.23.refs_2_), custom_call_target="tpu_custom_call" | custom-call | bytes 387072 | tf_op jit(solution)/shard_map/second_last/pallas_call | solution.py:31
  63.3 0.0 collective-permute-done.16.refs_0_
  63.3 0.0 collective-permute-done.17.refs_1_
  63.3 1.4 %collective-permute-done.18.refs_2_ = bf16[216,128]{1,0:T(8,128)(2,1)S(1)} collective-permute-done((bf16[216,128]{1,0:T(8,128)(2,1)S(1)}, bf16[216,128]{1,0:T(8,128)(2,1)S(1)}, u32[]{:S(2)}, u32[]{:S(2)}) %collective-permute-start.18) | collective-permute-done | bytes 55328 | tf_op jit(solution)/shard_map/ppermute | solution.py:215
  64.7 0.7 %first_last.1 = f32[216,128]{1,0:T(8,128)} custom-call(f32[216,128]{1,0:T(8,128)S(1)} %get-tuple-element.37.keep_ref, bf16[216,128]{1,0:T(8,128)(2,1)S(1)} %collective-permute-done.16.refs_0_, bf16[216,128]{1,0:T(8,128)(2,1)S(1)} %collective-permute-done.17.refs_1_, bf16[216,128]{1,0:T(8,128)(2,1)S(1)} %collective-permute-done.18.refs_2_), custom_call_target="tpu_custom_call" | custom-call | bytes 387072 | tf_op jit(solution)/shard_map/first_last/pallas_call | solution.py:31
  (4 shorter events, 0.0 us)
Async XLA Ops:
  0.6 25.4 %copy-start = (bf16[4,16,16,128]{3,2,1,0:T(8,128)(2,1)S(1)}, bf16[4,16,16,128]{3,2,1,0:T(8,128)(2,1)}, u32[]{:S(2)}) copy-start(bf16[4,16,16,128]{3,2,1,0:T(8,128)(2,1)} %f_ref.1) | copy-start | bytes 786436
  0.6 25.4 %copy-start.1 = (bf16[4,16,16,128]{3,2,1,0:T(8,128)(2,1)S(1)}, bf16[4,16,16,128]{3,2,1,0:T(8,128)(2,1)}, u32[]{:S(2)}) copy-start(bf16[4,16,16,128]{3,2,1,0:T(8,128)(2,1)} %g_ref.1) | copy-start | bytes 786436
  0.7 11.9 %collective-permute-start.2 = (bf16[216,128]{1,0:T(8,128)(2,1)}, bf16[216,128]{1,0:T(8,128)(2,1)S(1)}, u32[]{:S(2)}, u32[]{:S(2)}) collective-permute-start(bf16[216,128]{1,0:T(8,128)(2,1)} %param.5), channel_id=1, source_target_pairs={{0,4},{1,5},{2,6},{3,7},{4,0},{5,1},{6,2},{7,3},{8,12},{9,13},{10,... | collective-permute-start | bytes 165896 | tf_op jit(solution)/shard_map/ppermute | solution.py:215
  3.7 8.9 %collective-permute-start.3 = (bf16[216,128]{1,0:T(8,128)(2,1)}, bf16[216,128]{1,0:T(8,128)(2,1)S(1)}, u32[]{:S(2)}, u32[]{:S(2)}) collective-permute-start(bf16[216,128]{1,0:T(8,128)(2,1)} %param.5), channel_id=1, source_target_pairs={{0,8},{1,9},{2,10},{3,11},{4,12},{5,13},{6,14},{7,15},{8,0},{9,1},... | collective-permute-start | bytes 165896 | tf_op jit(solution)/shard_map/ppermute | solution.py:215
  6.3 6.4 %collective-permute-start.4 = (bf16[216,128]{1,0:T(8,128)(2,1)}, bf16[216,128]{1,0:T(8,128)(2,1)S(1)}, u32[]{:S(2)}, u32[]{:S(2)}) collective-permute-start(bf16[216,128]{1,0:T(8,128)(2,1)} %param.5), channel_id=1, source_target_pairs={{0,12},{1,13},{2,14},{3,15},{4,8},{5,9},{6,10},{7,11},{8,4},{9,5},... | collective-permute-start | bytes 165896 | tf_op jit(solution)/shard_map/ppermute | solution.py:215
  6.3 10.3 %collective-permute-start.8 = (bf16[216,128]{1,0:T(8,128)(2,1)}, bf16[216,128]{1,0:T(8,128)(2,1)S(1)}, u32[]{:S(2)}, u32[]{:S(2)}) collective-permute-start(bf16[216,128]{1,0:T(8,128)(2,1)} %param.6), channel_id=1, source_target_pairs={{0,4},{1,5},{2,6},{3,7},{4,0},{5,1},{6,2},{7,3},{8,12},{9,13},{10,... | collective-permute-start | bytes 165896 | tf_op jit(solution)/shard_map/ppermute | solution.py:215
  7.2 10.6 %collective-permute-start.9 = (bf16[216,128]{1,0:T(8,128)(2,1)}, bf16[216,128]{1,0:T(8,128)(2,1)S(1)}, u32[]{:S(2)}, u32[]{:S(2)}) collective-permute-start(bf16[216,128]{1,0:T(8,128)(2,1)} %param.6), channel_id=1, source_target_pairs={{0,8},{1,9},{2,10},{3,11},{4,12},{5,13},{6,14},{7,15},{8,0},{9,1},... | collective-permute-start | bytes 165896 | tf_op jit(solution)/shard_map/ppermute | solution.py:215
  12.6 6.2 %collective-permute-start.10 = (bf16[216,128]{1,0:T(8,128)(2,1)}, bf16[216,128]{1,0:T(8,128)(2,1)S(1)}, u32[]{:S(2)}, u32[]{:S(2)}) collective-permute-start(bf16[216,128]{1,0:T(8,128)(2,1)} %param.6), channel_id=1, source_target_pairs={{0,12},{1,13},{2,14},{3,15},{4,8},{5,9},{6,10},{7,11},{8,4},{9,5},... | collective-permute-start | bytes 165896 | tf_op jit(solution)/shard_map/ppermute | solution.py:215
  13.6 7.7 %collective-permute-start.6 = (bf16[4,216,128]{2,1,0:T(8,128)(2,1)S(1)}, bf16[4,216,128]{2,1,0:T(8,128)(2,1)S(1)}, u32[]{:S(2)}, u32[]{:S(2)}) collective-permute-start(bf16[4,216,128]{2,1,0:T(8,128)(2,1)S(1)} %pad_maximum_fusion.w0), channel_id=1, source_target_pairs={{0,2},{1,3},{2,0},{3,1},{4,6},{5,7},{6,4},{7,5},{8,10},{9,11},{10,... | collective-permute-start | bytes 663560 | tf_op jit(solution)/shard_map/ppermute | solution.py:215
  15.4 7.2 %collective-permute-start = (bf16[3,16,16,128]{3,2,1,0:T(8,128)(2,1)S(1)}, bf16[3,16,16,128]{3,2,1,0:T(8,128)(2,1)S(1)}, u32[]{:S(2)}, u32[]{:S(2)}) collective-permute-start(bf16[3,16,16,128]{3,2,1,0:T(8,128)(2,1)S(1)} %pad_maximum_fusion.2), channel_id=1, source_target_pairs={{0,1},{1,2},{2,3},{3,4},{4,5},{5,6},{6,7},{7,8},{8,9},{9,10},{10,1... | collective-permute-start | bytes 589832 | tf_op jit(solution)/shard_map/ppermute | solution.py:258
  16.7 11.3 %collective-permute-start.5 = (bf16[4,216,128]{2,1,0:T(8,128)(2,1)S(1)}, bf16[4,216,128]{2,1,0:T(8,128)(2,1)S(1)}, u32[]{:S(2)}, u32[]{:S(2)}) collective-permute-start(bf16[4,216,128]{2,1,0:T(8,128)(2,1)S(1)} %pad_maximum_fusion.w0), channel_id=1, source_target_pairs={{0,1},{1,0},{2,3},{3,2},{4,5},{5,4},{6,7},{7,6},{8,9},{9,8},{10,11... | collective-permute-start | bytes 663560 | tf_op jit(solution)/shard_map/ppermute | solution.py:215
  19.7 6.4 %collective-permute-start.12 = (bf16[4,216,128]{2,1,0:T(8,128)(2,1)S(1)}, bf16[4,216,128]{2,1,0:T(8,128)(2,1)S(1)}, u32[]{:S(2)}, u32[]{:S(2)}) collective-permute-start(bf16[4,216,128]{2,1,0:T(8,128)(2,1)S(1)} %pad_maximum_fusion.1.w0), channel_id=1, source_target_pairs={{0,2},{1,3},{2,0},{3,1},{4,6},{5,7},{6,4},{7,5},{8,10},{9,11},{10,... | collective-permute-start | bytes 663560 | tf_op jit(solution)/shard_map/ppermute | solution.py:215
  21.3 6.8 %collective-permute-start.7 = (bf16[4,216,128]{2,1,0:T(8,128)(2,1)S(1)}, bf16[4,216,128]{2,1,0:T(8,128)(2,1)S(1)}, u32[]{:S(2)}, u32[]{:S(2)}) collective-permute-start(bf16[4,216,128]{2,1,0:T(8,128)(2,1)S(1)} %collective-permute-done.6.w2), channel_id=1, source_target_pairs={{0,1},{1,0},{2,3},{3,2},{4,5},{5,4},{6,7},{7,6},{8,9},{9,8},{10,11... | collective-permute-start | bytes 663560 | tf_op jit(solution)/shard_map/ppermute | solution.py:215
  21.3 4.8 %collective-permute-start.1 = (bf16[3,16,16,128]{3,2,1,0:T(8,128)(2,1)S(1)}, bf16[3,16,16,128]{3,2,1,0:T(8,128)(2,1)S(1)}, u32[]{:S(2)}, u32[]{:S(2)}) collective-permute-start(bf16[3,16,16,128]{3,2,1,0:T(8,128)(2,1)S(1)} %pad_maximum_fusion.3), channel_id=1, source_target_pairs={{1,0},{2,1},{3,2},{4,3},{5,4},{6,5},{7,6},{8,7},{9,8},{10,9},{11,1... | collective-permute-start | bytes 589832 | tf_op jit(solution)/shard_map/ppermute | solution.py:259
  22.6 12.6 %collective-permute-start.11 = (bf16[4,216,128]{2,1,0:T(8,128)(2,1)S(1)}, bf16[4,216,128]{2,1,0:T(8,128)(2,1)S(1)}, u32[]{:S(2)}, u32[]{:S(2)}) collective-permute-start(bf16[4,216,128]{2,1,0:T(8,128)(2,1)S(1)} %pad_maximum_fusion.1.w0), channel_id=1, source_target_pairs={{0,1},{1,0},{2,3},{3,2},{4,5},{5,4},{6,7},{7,6},{8,9},{9,8},{10,11... | collective-permute-start | bytes 663560 | tf_op jit(solution)/shard_map/ppermute | solution.py:215
  26.1 9.1 %collective-permute-start.13 = (bf16[4,216,128]{2,1,0:T(8,128)(2,1)S(1)}, bf16[4,216,128]{2,1,0:T(8,128)(2,1)S(1)}, u32[]{:S(2)}, u32[]{:S(2)}) collective-permute-start(bf16[4,216,128]{2,1,0:T(8,128)(2,1)S(1)} %collective-permute-done.12.w2), channel_id=1, source_target_pairs={{0,1},{1,0},{2,3},{3,2},{4,5},{5,4},{6,7},{7,6},{8,9},{9,8},{10,11... | collective-permute-start | bytes 663560 | tf_op jit(solution)/shard_map/ppermute | solution.py:215
  32.4 8.0 %collective-permute-start.19 = (bf16[8,216,128]{2,1,0:T(8,128)(2,1)S(1)}, bf16[8,216,128]{2,1,0:T(8,128)(2,1)S(1)}, u32[]{:S(2)}, u32[]{:S(2)}) collective-permute-start(bf16[8,216,128]{2,1,0:T(8,128)(2,1)S(1)} %get-tuple-element.42), channel_id=1, source_target_pairs={{0,1},{1,0},{2,3},{3,2},{4,5},{5,4},{6,7},{7,6},{8,9},{9,8},{10,11... | collective-permute-start | bytes 1327112 | tf_op jit(solution)/shard_map/ppermute | solution.py:215
  40.3 1.9 %collective-permute-start.14 = (bf16[8,216,128]{2,1,0:T(8,128)(2,1)S(1)}, bf16[8,216,128]{2,1,0:T(8,128)(2,1)S(1)}, u32[]{:S(2)}, u32[]{:S(2)}) collective-permute-start(bf16[8,216,128]{2,1,0:T(8,128)(2,1)S(1)} %get-tuple-element.34), channel_id=1, source_target_pairs={{0,1},{1,0},{2,3},{3,2},{4,5},{5,4},{6,7},{7,6},{8,9},{9,8},{10,11... | collective-permute-start | bytes 1327112 | tf_op jit(solution)/shard_map/ppermute | solution.py:215
  40.5 8.3 %collective-permute-start.20 = (bf16[4,216,128]{2,1,0:T(8,128)(2,1)S(1)}, bf16[4,216,128]{2,1,0:T(8,128)(2,1)S(1)}, u32[]{:S(2)}, u32[]{:S(2)}) collective-permute-start(bf16[4,216,128]{2,1,0:T(8,128)(2,1)S(1)} %get-tuple-element.44), channel_id=1, source_target_pairs={{0,2},{1,3},{2,0},{3,1},{4,6},{5,7},{6,4},{7,5},{8,10},{9,11},{10,... | collective-permute-start | bytes 663560 | tf_op jit(solution)/shard_map/ppermute | solution.py:215
  42.3 12.0 %collective-permute-start.15 = (bf16[4,216,128]{2,1,0:T(8,128)(2,1)S(1)}, bf16[4,216,128]{2,1,0:T(8,128)(2,1)S(1)}, u32[]{:S(2)}, u32[]{:S(2)}) collective-permute-start(bf16[4,216,128]{2,1,0:T(8,128)(2,1)S(1)} %get-tuple-element.36), channel_id=1, source_target_pairs={{0,2},{1,3},{2,0},{3,1},{4,6},{5,7},{6,4},{7,5},{8,10},{9,11},{10,... | collective-permute-start | bytes 663560 | tf_op jit(solution)/shard_map/ppermute | solution.py:215
  48.9 9.9 %collective-permute-start.21 = (bf16[216,128]{1,0:T(8,128)(2,1)S(1)}, bf16[216,128]{1,0:T(8,128)(2,1)S(1)}, u32[]{:S(2)}, u32[]{:S(2)}) collective-permute-start(bf16[216,128]{1,0:T(8,128)(2,1)S(1)} %get-tuple-element.46), channel_id=1, source_target_pairs={{0,4},{1,5},{2,6},{3,7},{4,0},{5,1},{6,2},{7,3},{8,12},{9,13},{10,... | collective-permute-start | bytes 165896 | tf_op jit(solution)/shard_map/ppermute | solution.py:215
  50.5 12.1 %collective-permute-start.22 = (bf16[216,128]{1,0:T(8,128)(2,1)S(1)}, bf16[216,128]{1,0:T(8,128)(2,1)S(1)}, u32[]{:S(2)}, u32[]{:S(2)}) collective-permute-start(bf16[216,128]{1,0:T(8,128)(2,1)S(1)} %get-tuple-element.47), channel_id=1, source_target_pairs={{0,8},{1,9},{2,10},{3,11},{4,12},{5,13},{6,14},{7,15},{8,0},{9,1},... | collective-permute-start | bytes 165896 | tf_op jit(solution)/shard_map/ppermute | solution.py:215
  54.2 8.4 %collective-permute-start.23 = (bf16[216,128]{1,0:T(8,128)(2,1)S(1)}, bf16[216,128]{1,0:T(8,128)(2,1)S(1)}, u32[]{:S(2)}, u32[]{:S(2)}) collective-permute-start(bf16[216,128]{1,0:T(8,128)(2,1)S(1)} %get-tuple-element.48), channel_id=1, source_target_pairs={{0,12},{1,13},{2,14},{3,15},{4,8},{5,9},{6,10},{7,11},{8,4},{9,5},... | collective-permute-start | bytes 165896 | tf_op jit(solution)/shard_map/ppermute | solution.py:215
  54.3 9.0 %collective-permute-start.16 = (bf16[216,128]{1,0:T(8,128)(2,1)S(1)}, bf16[216,128]{1,0:T(8,128)(2,1)S(1)}, u32[]{:S(2)}, u32[]{:S(2)}) collective-permute-start(bf16[216,128]{1,0:T(8,128)(2,1)S(1)} %get-tuple-element.38), channel_id=1, source_target_pairs={{0,4},{1,5},{2,6},{3,7},{4,0},{5,1},{6,2},{7,3},{8,12},{9,13},{10,... | collective-permute-start | bytes 165896 | tf_op jit(solution)/shard_map/ppermute | solution.py:215
  54.9 8.4 %collective-permute-start.17 = (bf16[216,128]{1,0:T(8,128)(2,1)S(1)}, bf16[216,128]{1,0:T(8,128)(2,1)S(1)}, u32[]{:S(2)}, u32[]{:S(2)}) collective-permute-start(bf16[216,128]{1,0:T(8,128)(2,1)S(1)} %get-tuple-element.39), channel_id=1, source_target_pairs={{0,8},{1,9},{2,10},{3,11},{4,12},{5,13},{6,14},{7,15},{8,0},{9,1},... | collective-permute-start | bytes 165896 | tf_op jit(solution)/shard_map/ppermute | solution.py:215
  58.8 6.0 %collective-permute-start.18 = (bf16[216,128]{1,0:T(8,128)(2,1)S(1)}, bf16[216,128]{1,0:T(8,128)(2,1)S(1)}, u32[]{:S(2)}, u32[]{:S(2)}) collective-permute-start(bf16[216,128]{1,0:T(8,128)(2,1)S(1)} %get-tuple-element.40), channel_id=1, source_target_pairs={{0,12},{1,13},{2,14},{3,15},{4,8},{5,9},{6,10},{7,11},{8,4},{9,5},... | collective-permute-start | bytes 165896 | tf_op jit(solution)/shard_map/ppermute | solution.py:215

commit v2 on v1

v2 whole, which is shorter than its diff:
```python
import functools

import jax
import jax.numpy as jnp
from jax import lax
from jax.experimental import pallas as pl
from jax.experimental.pallas import tpu as pltpu
from jax.sharding import PartitionSpec as P

inv_root_two = 0.7071067811865476
inv_root_two_pi = 0.3989422804014327

BF16 = jnp.bfloat16
F32 = jnp.float32
LIMIT = 14 << 20


def gelu_parts(value):
    normal_cdf = 0.5 * (1.0 + lax.erf(value * inv_root_two))
    slope = normal_cdf + value * jnp.exp(-0.5 * value * value) * inv_root_two_pi
    return (value * normal_cdf, slope)


def local_call(kernel, name, outs, args, scratch=(), scalars=0, wait_for=()):
    first, last = len(args), len(args) + len(wait_for)

    def body(*refs):
        kernel(*refs[:first], *refs[last:])

    spaces = [pltpu.SMEM] * scalars + [pltpu.VMEM] * (first - scalars) + [pl.ANY] * len(wait_for)
    return pl.pallas_call(
        body,
        out_shape=list(outs),
        in_specs=[pl.BlockSpec(memory_space=space) for space in spaces],
        out_specs=[pl.BlockSpec(memory_space=pltpu.VMEM) for _ in outs],
        scratch_shapes=list(scratch),
        name=name,
        compiler_params=pltpu.CompilerParams(vmem_limit_bytes=LIMIT),
        cost_estimate=pl.CostEstimate(flops=1000, bytes_accessed=0, transcendentals=0),
    )(*args, *wait_for)


def like(shape, dtype):
    return jax.ShapeDtypeStruct(shape, dtype)


def write_shifted(dst, at, plane):
    height, width, channels = plane.shape
    flat = plane.astype(F32).reshape(height * width, channels)
    column = lax.broadcasted_iota(jnp.int32, flat.shape, 0) % width
    left = jnp.where(column == 0, 0.0, pltpu.roll(flat, 1, 0))
    right = jnp.where(column == width - 1, 0.0, pltpu.roll(flat, height * width - 1, 0))
    row = jnp.zeros((1, width, 3 * channels), BF16)
    dst[at, 0:1] = row
    dst[at, height + 1 : height + 2] = row
    for block, value in enumerate((left, flat, right)):
        dst[at, 1 : height + 1, :, block * channels : (block + 1) * channels] = (
            value.astype(BF16).reshape(height, width, channels)
        )


def prepare_kernel(me_ref, f_ref, g_ref, core_ref, chip_ref, xf_ref, xg_ref, gt_ref):
    planes, height, width, channels = f_ref.shape
    odd = me_ref[0] % 2
    for ref, below in ((core_ref, odd), (chip_ref, 1 - odd)):
        for p in range(2):
            write_shifted(xf_ref, jnp.where(below == 1, p, planes + 2 + p), ref[p])
        write_shifted(xg_ref, jnp.where(below == 1, 0, planes + 1), ref[2])
    for p in range(planes):
        write_shifted(xf_ref, p + 2, f_ref[p])
        write_shifted(xg_ref, p + 1, g_ref[p])

    def transposed(p, _):
        for b in range(3):
            for c in range(3):
                block = xg_ref[p, b : b + height, :, c * channels : (c + 1) * channels]
                gt_ref[p, b * 3 + c] = block.reshape(height * width, channels).T
        return 0

    lax.fori_loop(0, planes + 2, transposed, 0)


def load_kernel(f_hbm, g_hbm, first_hbm, second_hbm, *refs):
    f_ref, g_ref, first_ref, second_ref, sems = refs
    moves = [
        pltpu.make_async_copy(source, target, sems.at[at])
        for at, (source, target) in enumerate(
            (
                (first_hbm, first_ref.at[0]),
                (second_hbm, second_ref.at[0]),
                (f_hbm, f_ref),
                (g_hbm, g_ref),
            )
        )
    ]
    for move in moves:
        move.start()
    for move in moves:
        move.wait()


def edges_kernel(me_ref, f_ref, g_ref, core_ref, chip_ref):
    planes = f_ref.shape[0]
    odd = me_ref[0] % 2
    for ref, low in ((core_ref, odd == 1), (chip_ref, odd == 0)):
        ref[0:2] = f_ref[pl.ds(jnp.where(low, 0, planes - 2), 2)]
        ref[2:3] = g_ref[pl.ds(jnp.where(low, 0, planes - 1), 1)]


def loaded(features, first, second, cotangent):
    args = [
        pltpu.with_memory_space_constraint(a, pltpu.HBM)
        for a in (features, cotangent, first, second)
    ]
    return pl.pallas_call(
        load_kernel,
        out_shape=[
            like(features.shape, BF16),
            like(cotangent.shape, BF16),
            like((1, *first.shape), BF16),
            like((1, *second.shape), BF16),
        ],
        in_specs=[pl.BlockSpec(memory_space=pltpu.HBM) for _ in args],
        out_specs=[pl.BlockSpec(memory_space=pltpu.VMEM) for _ in range(4)],
        scratch_shapes=[pltpu.SemaphoreType.DMA((len(args),))],
        name="load",
        compiler_params=pltpu.CompilerParams(vmem_limit_bytes=LIMIT),
    )(*args)


def join_kernel(*refs):
    *parts, out_ref = refs
    at = 0
    for part in parts:
        if len(part.shape) == 2:
            out_ref[at] = part[...]
            at += 1
        else:
            out_ref[at : at + part.shape[0]] = part[...]
            at += part.shape[0]


def window(ref, first, planes):
    height, width, lanes = ref.shape[1] - 2, ref.shape[2], ref.shape[3]
    return jnp.concatenate(
        [
            ref[first : first + planes, b : b + height].reshape(planes * height * width, lanes)
            for b in range(3)
        ],
        axis=1,
    )


def conv_rows(ref, first, planes, weight_ref):
    depth = weight_ref.shape[0] // 3
    cells = (ref.shape[1] - 2) * ref.shape[2]
    taps = [weight_ref[a * depth : (a + 1) * depth] for a in range(3)]

    def term(at, count, weight):
        return jnp.dot(window(ref, first + at, count), weight, preferred_element_type=F32)

    if planes == 1:
        return sum(term(a, 1, taps[a]) for a in range(3))
    channels = taps[0].shape[1]
    middle = term(1, planes - 1, jnp.concatenate(taps[:2], axis=1))
    late = term(2, planes - 2, taps[2])
    ends = (term(0, 1, taps[0]), term(planes + 1, 1, taps[2]))
    last = term(planes, 1, jnp.concatenate(taps[1:], axis=1))
    parts = [[] for _ in range(planes)]
    parts[0].append(ends[0])
    for p in range(1, planes):
        rows = slice((p - 1) * cells, p * cells)
        parts[p].append(middle[rows, :channels])
        parts[p - 1].append(middle[rows, channels:])
    for p in range(2, planes):
        parts[p - 2].append(late[(p - 2) * cells : (p - 1) * cells])
    parts[planes - 1].append(last[:, :channels])
    parts[planes - 2].append(last[:, channels:])
    parts[planes - 1].append(ends[1])
    return jnp.concatenate([sum(terms[1:], terms[0]) for terms in parts], axis=0)


def near_far(core):
    return jnp.where(core == 0, 4, 2), jnp.where(core == 0, 2, 4)


def assemble(me, pieces, dst):
    rows = pieces[0].shape[1]
    near, far = near_far(me % 2)
    for piece, start, side in zip(
        pieces, (me, me ^ far, me ^ 1, me ^ 1 ^ near), (near, near, far, far)
    ):
        for at, owner in enumerate((start, start ^ 8, start ^ side, start ^ 8 ^ side)):
            dst[pl.ds(pl.multiple_of(owner * rows, 8), rows)] = piece[at]


def assemble_in_order(me, pieces, dst):
    dst[...] = pieces[0][...]


def split_terms(me, total_ref, send_ref, keep_ref):
    count, rows, _ = keep_ref.shape
    core = me % 2
    for k in range(count):
        own = pl.multiple_of((2 * k + core) * rows, 8)
        other = pl.multiple_of((2 * k + 1 - core) * rows, 8)
        keep_ref[k] = total_ref[pl.ds(own, rows)]
        send_ref[k] = total_ref[pl.ds(other, rows)].astype(BF16)


def first_kernel(pieces, place, me_ref, *refs):
    piece_refs, (xf_ref, xg_ref, *out_refs) = refs[:pieces], refs[pieces:]
    bank_ref, hidden_ref, slope_ref, send_ref, keep_ref, total_ref = out_refs
    me = me_ref[0]
    planes, height, width, channels = hidden_ref.shape
    place(me, piece_refs, bank_ref)
    active, slope = gelu_parts(conv_rows(xf_ref, 1, planes, bank_ref))
    slope_ref[...] = slope.T
    hidden = active.astype(BF16)
    hidden_ref[...] = hidden.reshape(hidden_ref.shape)
    flipped = hidden.T
    for a in range(3):
        out = jnp.dot(flipped, window(xg_ref, 2 - a, planes), preferred_element_type=F32)
        for rest in range(9):
            tap, source = a * 9 + rest, 8 - rest
            total_ref[tap * channels : (tap + 1) * channels] = out[
                :, source * channels : (source + 1) * channels
            ]
    split_terms(me, total_ref, send_ref, keep_ref)


def second_kernel(pieces, place, me_ref, *refs):
    piece_refs, (xf_ref, gt_ref, slope_ref, *out_refs) = refs[:pieces], refs[pieces:]
    bank_ref, send_ref, keep_ref, total_ref = out_refs
    me = me_ref[0]
    channels = slope_ref.shape[0]
    planes, _, _, cells = gt_ref.shape
    planes -= 2
    place(me, piece_refs, bank_ref)
    back = jnp.concatenate(
        [bank_ref[tap * channels : (tap + 1) * channels] for tap in reversed(range(27))], axis=1
    )
    grads = []
    for z in range(planes):
        grad_hidden = jnp.dot(
            back, gt_ref[z : z + 3].reshape(27 * channels, cells), preferred_element_type=F32
        )
        grads.append((grad_hidden * slope_ref[:, z * cells : (z + 1) * cells]).astype(BF16))
    grad_pre = jnp.concatenate(grads, axis=1)
    for a in range(3):
        out = jnp.dot(grad_pre, window(xf_ref, 1 + a, planes), preferred_element_type=F32)
        for rest in range(9):
            tap = a * 9 + rest
            total_ref[tap * channels : (tap + 1) * channels] = out[
                :, rest * channels : (rest + 1) * channels
            ].T
    split_terms(me, total_ref, send_ref, keep_ref)


def hidden_kernel(count, me_ref, xf_ref, bank_ref, hidden_ref, xh_ref):
    me = me_ref[0]
    planes, height, width, channels = hidden_ref.shape
    for at, first, inside in ((0, 0, me > 0), (planes + 1, planes + 1, me < count - 1)):
        active, _ = gelu_parts(conv_rows(xf_ref, first, 1, bank_ref))
        active = jnp.where(inside, active, 0.0)
        write_shifted(xh_ref, at, active.astype(BF16).reshape(height, width, channels))
    for p in range(planes):
        write_shifted(xh_ref, p + 1, hidden_ref[p])


def output_kernel(xh_ref, second_ref, out_ref):
    out = conv_rows(xh_ref, 0, out_ref.shape[0], second_ref)
    out_ref[...] = out.astype(BF16).reshape(out_ref.shape)


def sum_half(bit, place, keep_ref, got_ref, send_ref, own_ref):
    for at in range(own_ref.shape[0]):
        mine, other = place(at, bit), place(at, 1 - bit)
        own_ref[at] = keep_ref[mine] + got_ref[mine].astype(F32)
        send_ref[at] = (keep_ref[other] + got_ref[other].astype(F32)).astype(BF16)


def sum_pair_kernel(me_ref, *refs):
    me = me_ref[0]
    core = me % 2
    bit = jnp.where(core == 0, (me // 2) % 2, (me // 4) % 2)

    def place(at, value):
        return jnp.where(core == 0, 2 * at + value, at // 2 * 4 + 2 * value + at % 2)

    sum_half(bit, place, *refs)


def sum_near_kernel(me_ref, *refs):
    me = me_ref[0]
    bit = jnp.where(me % 2 == 0, (me // 4) % 2, (me // 2) % 2)
    sum_half(bit, lambda at, value: 2 * at + value, *refs)


def sum_far_kernel(me_ref, *refs):
    sum_half(me_ref[0] // 8, lambda at, value: value, *refs)


def sum_last_kernel(keep_first, got_first, keep_second, got_second, first_ref, second_ref):
    first_ref[...] = keep_first[0] + got_first[0].astype(F32)
    second_ref[...] = keep_second[0] + got_second[0].astype(F32)


def swap(value, count, distance):
    return lax.ppermute(value, "slab", [(i, i ^ distance) for i in range(count)])


def swap_mixed(value, count, even, odd):
    pairs = [(i, i ^ (odd if i % 2 else even)) for i in range(count)]
    return lax.ppermute(value, "slab", pairs)


def joined(parts, name, wait_for=()):
    depth = sum(part.shape[0] if part.ndim == 3 else 1 for part in parts)
    out = like((depth, *parts[0].shape[-2:]), BF16)
    return local_call(join_kernel, name, [out], parts, wait_for=wait_for)[0]


def summed(kernel, name, me, keep, got, wait_for=()):
    shape = (keep.shape[0] // 2, *keep.shape[1:])
    outs = [like(shape, BF16), like(shape, F32)]
    return local_call(kernel, name, outs, [me, keep, got], scalars=1, wait_for=wait_for)


def shards(count, features, filters_first, filters_second, cotangent):
    planes, height, width, channels = features.shape
    cells = planes * height * width
    rows = filters_first.shape[0]
    taps = 27 * channels
    direct = count == 16 and rows % 8 == 0
    me = lax.axis_index("slab").astype(jnp.int32).reshape(1)
    shard_rows = rows if direct else taps // 16
    place = me if direct else jnp.zeros((1,), jnp.int32)
    order = assemble if direct else assemble_in_order

    features, cotangent, first_shard, second_shard = loaded(
        features, filters_first, filters_second, cotangent
    )
    edge = like((3, height, width, channels), BF16)
    to_core, to_chip = local_call(
        edges_kernel, "edges", [edge, edge], [me, features, cotangent], scalars=1
    )
    from_core = swap(to_core, count, 1)
    next_chip = [(i, i + 1 if i % 2 else i - 1) for i in range(1, count - 1)]
    from_chip = lax.ppermute(to_chip, "slab", next_chip)
    xf, xg, gt = local_call(
        prepare_kernel,
        "shifted_planes",
        [
            like((planes + 4, height + 2, width, 3 * channels), BF16),
            like((planes + 2, height + 2, width, 3 * channels), BF16),
            like((planes + 2, 9, channels, height * width), BF16),
        ],
        [me, features, cotangent, from_core, from_chip],
        scalars=1,
    )
    wait_for = []
    if direct:
        far = [swap(shard, count, 8) for shard in (filters_first, filters_second)]
        two_first = joined([first_shard, far[0]], "first_two", [from_chip])
        near_first = swap_mixed(two_first, count, 4, 2)
        two_second = joined([second_shard, far[1]], "second_two")
        near_second = swap_mixed(two_second, count, 4, 2)
        four_first = joined([two_first, near_first], "first_four", [two_second, xf])
        cross_first = swap_mixed(four_first, count, 2, 4)
        four_second = joined([two_second, near_second], "second_four")
        cross_second = swap_mixed(four_second, count, 2, 4)
        wait_for = [cross_second]
        first = [four_first, cross_first, swap(four_first, count, 1), swap(cross_first, count, 1)]
        second = [
            four_second,
            cross_second,
            swap(four_second, count, 1),
            swap(cross_second, count, 1),
        ]
    else:
        first, second = (
            [lax.all_gather(shard, "slab", axis=0, tiled=True)]
            for shard in (filters_first, filters_second)
        )

    terms = [like((8, shard_rows, channels), BF16), like((8, shard_rows, channels), F32)]
    total = pltpu.VMEM((taps, channels), F32)
    bank, hidden, slope, send_second, keep_second = local_call(
        functools.partial(first_kernel, len(first), order),
        "hidden_and_second_grad",
        [
            like((taps, channels), BF16),
            like(features.shape, BF16),
            like((channels, cells), F32),
            *terms,
        ],
        [place, *first, xf, xg],
        scratch=[total],
        scalars=1,
        wait_for=wait_for,
    )
    bank_second, send_first, keep_first = local_call(
        functools.partial(second_kernel, len(second), order),
        "first_grad",
        [like((taps, channels), BF16), *terms],
        [place, *second, xf, gt, slope],
        scratch=[total],
        scalars=1,
    )
    wait_for = []
    if direct:
        got = swap(send_second, count, 1)
        send_second, keep_second = summed(sum_pair_kernel, "second_pair", me, keep_second, got)
        got_second = swap_mixed(send_second, count, 2, 4)
        got = swap(send_first, count, 1)
    (xh,) = local_call(
        functools.partial(hidden_kernel, count),
        "hidden_planes",
        [like((planes + 2, height + 2, width, 3 * channels), BF16)],
        [me, xf, bank, hidden],
        scalars=1,
        wait_for=[keep_first],
    )
    if direct:
        send_first, keep_first = summed(sum_pair_kernel, "first_pair", me, keep_first, got, [xh])
        got_first = swap_mixed(send_first, count, 2, 4)
        send_second, keep_second = summed(
            sum_near_kernel, "second_near", me, keep_second, got_second, [send_first]
        )
        got_second = swap_mixed(send_second, count, 4, 2)
        send_first, keep_first = summed(
            sum_near_kernel, "first_near", me, keep_first, got_first, [send_second]
        )
        got_first = swap_mixed(send_first, count, 4, 2)
        send_second, keep_second = summed(
            sum_far_kernel, "second_far", me, keep_second, got_second, [send_first]
        )
        got_second = swap(send_second, count, 8)
        send_first, keep_first = summed(
            sum_far_kernel, "first_far", me, keep_first, got_first, [send_second]
        )
        wait_for = [send_first]
    (output,) = local_call(
        output_kernel, "output_conv", [like(features.shape, BF16)], [xh, bank_second], wait_for=wait_for
    )
    if direct:
        out = like((rows, channels), F32)
        grad_first, grad_second = local_call(
            sum_last_kernel,
            "sum_last",
            [out, out],
            [keep_first, swap(send_first, count, 8), keep_second, got_second],
        )
    else:
        grad_first, grad_second = (
            lax.psum_scatter(
                jnp.stack([keep, send.astype(F32)], 1).reshape(taps, channels),
                "slab",
                scatter_dimension=0,
                tiled=True,
            )
            for send, keep in ((send_first, keep_first), (send_second, keep_second))
        )
    return (output, grad_first, grad_second)


def solution(mesh):
    return jax.shard_map(
        functools.partial(shards, mesh.shape["slab"]),
        mesh=mesh,
        in_specs=(
            P(("groups", "slab"), None, None, None),
            P("slab", None),
            P("slab", None),
            P(("groups", "slab"), None, None, None),
        ),
        out_specs=(
            P(("groups", "slab"), None, None, None),
            P(("groups", "slab"), None),
            P(("groups", "slab"), None),
        ),
        check_vma=False,
    )
```

time: 65.7 us -> 57.4 us (0.87)
  starting transfers between devices: 34.3 us -> 18.1 us
  waiting for transfers between devices: 9.74 us -> 24.7 us
  Pallas kernels: 16.9 us -> 13.6 us
  local copies, waits for them, and re-layouts: 1.88 us -> 0 us
  other arithmetic: 1.73 us -> 0 us
    ppermute x22 -> x11, starting transfers between devices: 31.7 us -> 11.5 us  [swap(): lax.ppermute(value, 'slab', [(i, i ^ distance) for i in range(count)])]
    ppermute x2 -> x9, waiting for transfers between devices: 0.01 us -> 15.7 us  [the longest x8 15.7 us: swap_mixed(): return lax.ppermute(value, 'slab', pairs)]
    ppermute x2 -> x9, starting transfers between devices: 2.59 us -> 6.63 us  [the longest x8 5.95 us: swap_mixed(): return lax.ppermute(value, 'slab', pairs)]
    pallas_call x10 -> x18, Pallas kernels: 16.9 us -> 13.6 us  [the longest x17 12.5 us: local_call(): pl.pallas_call(body, out_shape=list(outs), in_specs=[pl.BlockSpec(memory_...]
    slice x2 -> x0, local copies, waits for them, and re-layouts: 1.87 us -> none  [the longest x1 0.99 us: shards(): features[:2]]
    another operation x2 -> x0, other arithmetic: 1.69 us -> none  [gather_bank(): jnp.stack([shard] + [swap(shard, count, 4 * d) for d in range(1, count //...]
    ppermute x22 -> x11, waiting for transfers between devices: 9.74 us -> 9.05 us  [swap(): lax.ppermute(value, 'slab', [(i, i ^ distance) for i in range(count)])]
  transfers between devices with their start and end apart: 24 -> 20, of which waited for: 4 -> 13; matrix products, arithmetic and copies ran while one was open for 6% -> 0% of each run, Pallas kernels for 25% -> 20%
where the time goes in v2:
time: 57.4 us; the launch traced here: 57.3 us
  waiting for transfers between devices  24.7 us (43%)
  starting transfers between devices  18.1 us (32%)
  Pallas kernels  13.6 us (24%)
  between operations  0.75 us (1%)
    ppermute x8, waiting for transfers between devices, swap_mixed(): return lax.ppermute(value, 'slab', pairs)  15.7 us
    pallas_call x17, Pallas kernels, local_call(): pl.pallas_call(body, out_shape=list(outs), in_specs=[pl.BlockSpec(memory_...  12.5 us
    ppermute x11, starting transfers between devices, swap(): lax.ppermute(value, 'slab', [(i, i ^ distance) for i in range(count)])  11.5 us
    ppermute x11, waiting for transfers between devices, swap(): lax.ppermute(value, 'slab', [(i, i ^ distance) for i in range(count)])  9.05 us
    ppermute x8, starting transfers between devices, swap_mixed(): return lax.ppermute(value, 'slab', pairs)  5.95 us
  transfers between devices with their start and end apart: 20, of which 13 were waited for; matrix products, arithmetic and copies ran while one was open for 0% of the time, Pallas kernels for 20%

profile of v2, /device:TPU:0, one launch (start us, length us, event | category | flops | bytes accessed | tf_op | source)
XLA Modules:
  0.0 57.3 jit_solution(11080298167667640727)
XLA Ops:
  0.6 1.1 %load.1 = (bf16[4,16,16,128]{3,2,1,0:T(8,128)(2,1)S(1)}, bf16[4,16,16,128]{3,2,1,0:T(8,128)(2,1)S(1)}, bf16[1,216,128]{2,1,0:T(8,128)(2,1)S(1)}, bf16[1,216,128]{2,1,0:T(8,128)(2,1)S(1)}) custom-call(bf16[4,16,16,128]{3,2,1,0:T(8,128)(2,1)} %f_hbm.1, bf16[4,16,16,128]{3,2,1,0:T(8,128)(2,1)} %g_hbm.1, bf16[216,128]{1,0:T(8,128)(2,1)} %first_hbm.1, ...), custom_call_target="tpu_custom_call" | custom-call | tf_op jit(solution)/shard_map/load/pallas_call | solution.py:115
  1.8 0.7 %collective-permute-start.1 = (bf16[3,16,16,128]{3,2,1,0:T(8,128)(2,1)S(1)}, bf16[3,16,16,128]{3,2,1,0:T(8,128)(2,1)S(1)}, u32[]{:S(2)}, u32[]{:S(2)}) collective-permute-start(bf16[3,16,16,128]{3,2,1,0:T(8,128)(2,1)S(1)} %get-tuple-element.37), channel_id=1, source_target_pairs={{1,2},{2,1},{3,4},{4,3},{5,6},{6,5},{7,8},{8,7},{9,10},{10,9},{11,... | collective-permute-start | bytes 589832 | tf_op jit(solution)/shard_map/ppermute | solution.py:350
  2.5 4.4 %collective-permute-start = (bf16[3,16,16,128]{3,2,1,0:T(8,128)(2,1)S(1)}, bf16[3,16,16,128]{3,2,1,0:T(8,128)(2,1)S(1)}, u32[]{:S(2)}, u32[]{:S(2)}) collective-permute-start(bf16[3,16,16,128]{3,2,1,0:T(8,128)(2,1)S(1)} %get-tuple-element.36), channel_id=1, source_target_pairs={{0,1},{1,0},{2,3},{3,2},{4,5},{5,4},{6,7},{7,6},{8,9},{9,8},{10,11... | collective-permute-start | bytes 589832 | tf_op jit(solution)/shard_map/ppermute | solution.py:310
  6.9 2.6 %collective-permute-start.2 = (bf16[216,128]{1,0:T(8,128)(2,1)}, bf16[216,128]{1,0:T(8,128)(2,1)S(1)}, u32[]{:S(2)}, u32[]{:S(2)}) collective-permute-start(bf16[216,128]{1,0:T(8,128)(2,1)} %first_hbm.1), channel_id=1, source_target_pairs={{0,8},{1,9},{2,10},{3,11},{4,12},{5,13},{6,14},{7,15},{8,0},{9,1},... | collective-permute-start | bytes 165896 | tf_op jit(solution)/shard_map/ppermute | solution.py:310
  9.5 0.3 collective-permute-start.4
  9.8 6.6 %collective-permute-done.2.refs_1_ = bf16[216,128]{1,0:T(8,128)(2,1)S(1)} collective-permute-done((bf16[216,128]{1,0:T(8,128)(2,1)}, bf16[216,128]{1,0:T(8,128)(2,1)S(1)}, u32[]{:S(2)}, u32[]{:S(2)}) %collective-permute-start.2) | collective-permute-done | bytes 55328 | tf_op jit(solution)/shard_map/ppermute | solution.py:310
  16.4 0.0 collective-permute-done.1.refs_4_.refs_2_
  16.4 0.1 collective-permute-start.3
  16.5 0.5 collective-permute-done.4.refs_1_
  17.0 1.6 %collective-permute-start.8 = (bf16[2,216,128]{2,1,0:T(8,128)(2,1)S(1)}, bf16[2,216,128]{2,1,0:T(8,128)(2,1)S(1)}, u32[]{:S(2)}, u32[]{:S(2)}) collective-permute-start(bf16[2,216,128]{2,1,0:T(8,128)(2,1)S(1)} %second_two.1.refs_2_.refs_0_), channel_id=1, source_target_pairs={{0,4},{1,3},{2,6},{3,1},{4,0},{5,7},{6,2},{7,5},{8,12},{9,11},{10,... | collective-permute-start | bytes 331784 | tf_op jit(solution)/shard_map/ppermute | solution.py:315
  18.6 0.0 collective-permute-done.refs_3_
  18.6 1.9 %shifted_planes.1 = (bf16[8,18,16,384]{3,2,1,0:T(8,128)(2,1)S(1)}, bf16[6,18,16,384]{3,2,1,0:T(8,128)(2,1)S(1)}, bf16[6,9,128,256]{3,2,1,0:T(8,128)(2,1)S(1)}) custom-call(s32[1]{0:T(128)} %bitcast.refs_0_, bf16[4,16,16,128]{3,2,1,0:T(8,128)(2,1)S(1)} %get-tuple-element.34.refs_1_, bf16[4,16,16,128]{3,2,1,0:T(8,128)(2,1)S(1)} %get-tuple-element.35.refs_2_, ...), custom_call_target="tpu_custom_call" | custom-call | flops 1000 | tf_op jit(solution)/shard_map/shifted_planes/pallas_call | solution.py:31
  20.5 0.7 %collective-permute-done.3.refs_1_ = bf16[2,216,128]{2,1,0:T(8,128)(2,1)S(1)} collective-permute-done((bf16[2,216,128]{2,1,0:T(8,128)(2,1)S(1)}, bf16[2,216,128]{2,1,0:T(8,128)(2,1)S(1)}, u32[]{:S(2)}, u32[]{:S(2)}) %collective-permute-start.3) | collective-permute-done | bytes 110624 | tf_op jit(solution)/shard_map/ppermute | solution.py:315
  21.2 0.1 collective-permute-start.5
  21.3 1.8 %collective-permute-done.8.refs_1_ = bf16[2,216,128]{2,1,0:T(8,128)(2,1)S(1)} collective-permute-done((bf16[2,216,128]{2,1,0:T(8,128)(2,1)S(1)}, bf16[2,216,128]{2,1,0:T(8,128)(2,1)S(1)}, u32[]{:S(2)}, u32[]{:S(2)}) %collective-permute-start.8) | collective-permute-done | bytes 110624 | tf_op jit(solution)/shard_map/ppermute | solution.py:315
  23.1 0.3 collective-permute-start.9
  23.4 0.0 collective-permute-start.6
  23.4 3.8 %collective-permute-done.5.refs_2_ = bf16[4,216,128]{2,1,0:T(8,128)(2,1)S(1)} collective-permute-done((bf16[4,216,128]{2,1,0:T(8,128)(2,1)S(1)}, bf16[4,216,128]{2,1,0:T(8,128)(2,1)S(1)}, u32[]{:S(2)}, u32[]{:S(2)}) %collective-permute-start.5) | collective-permute-done | bytes 221216 | tf_op jit(solution)/shard_map/ppermute | solution.py:315
  27.2 0.0 collective-permute-start.7
  27.2 0.5 collective-permute-start.10
  27.7 1.9 %collective-permute-done.9.refs_7_.refs_2_ = bf16[4,216,128]{2,1,0:T(8,128)(2,1)S(1)} collective-permute-done((bf16[4,216,128]{2,1,0:T(8,128)(2,1)S(1)}, bf16[4,216,128]{2,1,0:T(8,128)(2,1)S(1)}, u32[]{:S(2)}, u32[]{:S(2)}) %collective-permute-start.9) | collective-permute-done | bytes 221216 | tf_op jit(solution)/shard_map/ppermute | solution.py:315
  29.6 0.0 collective-permute-start.11
  29.6 0.0 collective-permute-done.6.refs_3_
  29.6 0.0 collective-permute-done.7.refs_4_
  29.6 3.1 %hidden_and_second_grad.1 = (bf16[3456,128]{1,0:T(8,128)(2,1)S(1)}, bf16[4,16,16,128]{3,2,1,0:T(8,128)(2,1)S(1)}, f32[128,1024]{1,0:T(8,128)S(1)}, bf16[8,216,128]{2,1,0:T(8,128)(2,1)S(1)}, f32[8,216,128]{2,1,0:T(8,128)S(1)}) custom-call(s32[1]{0:T(128)} %bitcast.refs_0_, bf16[4,216,128]{2,1,0:T(8,128)(2,1)S(1)} %first_four.1.refs_1_, ...), custom_call_target="tpu_custom_call" | custom-call | flops 1000 | tf_op jit(solution)/shard_map/hidden_and_second_grad/pallas_call | solution.py:31
  32.8 0.6 collective-permute-start.14
  33.3 0.0 collective-permute-done.10.refs_3_
  33.3 0.0 collective-permute-done.11.refs_4_
  33.3 2.8 %first_grad.1 = (bf16[3456,128]{1,0:T(8,128)(2,1)S(1)}, bf16[8,216,128]{2,1,0:T(8,128)(2,1)S(1)}, f32[8,216,128]{2,1,0:T(8,128)S(1)}) custom-call(s32[1]{0:T(128)} %bitcast.refs_0_, bf16[4,216,128]{2,1,0:T(8,128)(2,1)S(1)} %second_four.1.refs_1_, bf16[4,216,128]{2,1,0:T(8,128)(2,1)S(1)} %collective-permute-done.9.refs_7_.refs_2_, ...), custom_call_target="tpu_custom_call" | custom-call | flops 1000 | tf_op jit(solution)/shard_map/first_grad/pallas_call | solution.py:31
  36.2 0.1 collective-permute-start.12
  36.3 0.0 collective-permute-done.14.refs_2_
  36.3 0.1 second_pair.1
  36.4 0.1 collective-permute-start.15
  36.5 1.3 %hidden_planes.1.refs_3_.refs_0_ = bf16[6,18,16,384]{3,2,1,0:T(8,128)(2,1)S(1)} custom-call(s32[1]{0:T(128)} %bitcast.refs_0_, bf16[8,18,16,384]{3,2,1,0:T(8,128)(2,1)S(1)} %get-tuple-element.38.refs_3_.refs_5_.refs_1_, bf16[3456,128]{1,0:T(8,128)(2,1)S(1)} %get-tuple-element.42.refs_2_, bf16[4,16,16,128]{3,2,1,0:T(8,128)(2,1)S(1)} %get-tuple-element.43.refs_3_, ...), custom_call_target="tpu_custom_call" | custom-call | flops 1000 | tf_op jit(solution)/shard_map/hidden_planes/pallas_call | solution.py:31
  37.8 0.2 collective-permute-done.12.refs_2_
  38.0 0.1 first_pair.1
  38.1 1.9 %collective-permute-start.13 = (bf16[4,216,128]{2,1,0:T(8,128)(2,1)S(1)}, bf16[4,216,128]{2,1,0:T(8,128)(2,1)S(1)}, u32[]{:S(2)}, u32[]{:S(2)}) collective-permute-start(bf16[4,216,128]{2,1,0:T(8,128)(2,1)S(1)} %get-tuple-element.50.refs_3_), channel_id=1, source_target_pairs={{0,2},{1,5},{2,0},{3,7},{4,6},{5,1},{6,4},{7,3},{8,10},{9,13},{10,... | collective-permute-start | bytes 663560 | tf_op jit(solution)/shard_map/ppermute | solution.py:315
  40.0 2.4 %collective-permute-done.15.refs_2_ = bf16[4,216,128]{2,1,0:T(8,128)(2,1)S(1)} collective-permute-done((bf16[4,216,128]{2,1,0:T(8,128)(2,1)S(1)}, bf16[4,216,128]{2,1,0:T(8,128)(2,1)S(1)}, u32[]{:S(2)}, u32[]{:S(2)}) %collective-permute-start.15) | collective-permute-done | bytes 221216 | tf_op jit(solution)/shard_map/ppermute | solution.py:315
  42.4 1.0 %collective-permute-start.17 = (bf16[2,216,128]{2,1,0:T(8,128)(2,1)S(1)}, bf16[2,216,128]{2,1,0:T(8,128)(2,1)S(1)}, u32[]{:S(2)}, u32[]{:S(2)}) collective-permute-start(bf16[2,216,128]{2,1,0:T(8,128)(2,1)S(1)} %get-tuple-element.55.refs_3_), channel_id=1, source_target_pairs={{0,4},{1,3},{2,6},{3,1},{4,0},{5,7},{6,2},{7,5},{8,12},{9,11},{10,... | collective-permute-start | bytes 331784 | tf_op jit(solution)/shard_map/ppermute | solution.py:315
  43.4 1.3 %collective-permute-done.13.refs_2_ = bf16[4,216,128]{2,1,0:T(8,128)(2,1)S(1)} collective-permute-done((bf16[4,216,128]{2,1,0:T(8,128)(2,1)S(1)}, bf16[4,216,128]{2,1,0:T(8,128)(2,1)S(1)}, u32[]{:S(2)}, u32[]{:S(2)}) %collective-permute-start.13) | collective-permute-done | bytes 221216 | tf_op jit(solution)/shard_map/ppermute | solution.py:315
  44.8 1.0 %collective-permute-start.16 = (bf16[2,216,128]{2,1,0:T(8,128)(2,1)S(1)}, bf16[2,216,128]{2,1,0:T(8,128)(2,1)S(1)}, u32[]{:S(2)}, u32[]{:S(2)}) collective-permute-start(bf16[2,216,128]{2,1,0:T(8,128)(2,1)S(1)} %get-tuple-element.57.refs_3_), channel_id=1, source_target_pairs={{0,4},{1,3},{2,6},{3,1},{4,0},{5,7},{6,2},{7,5},{8,12},{9,11},{10,... | collective-permute-start | bytes 331784 | tf_op jit(solution)/shard_map/ppermute | solution.py:315
  45.8 1.5 %collective-permute-done.17.refs_2_ = bf16[2,216,128]{2,1,0:T(8,128)(2,1)S(1)} collective-permute-done((bf16[2,216,128]{2,1,0:T(8,128)(2,1)S(1)}, bf16[2,216,128]{2,1,0:T(8,128)(2,1)S(1)}, u32[]{:S(2)}, u32[]{:S(2)}) %collective-permute-start.17) | collective-permute-done | bytes 110624 | tf_op jit(solution)/shard_map/ppermute | solution.py:315
  47.3 2.3 %collective-permute-done.16.refs_2_ = bf16[2,216,128]{2,1,0:T(8,128)(2,1)S(1)} collective-permute-done((bf16[2,216,128]{2,1,0:T(8,128)(2,1)S(1)}, bf16[2,216,128]{2,1,0:T(8,128)(2,1)S(1)}, u32[]{:S(2)}, u32[]{:S(2)}) %collective-permute-start.16) | collective-permute-done | bytes 110624 | tf_op jit(solution)/shard_map/ppermute | solution.py:315
  49.6 0.7 %collective-permute-start.18 = (bf16[1,216,128]{2,1,0:T(8,128)(2,1)S(1)}, bf16[1,216,128]{2,1,0:T(8,128)(2,1)S(1)}, u32[]{:S(2)}, u32[]{:S(2)}) collective-permute-start(bf16[1,216,128]{2,1,0:T(8,128)(2,1)S(1)} %get-tuple-element.60.refs_2_), channel_id=1, source_target_pairs={{0,8},{1,9},{2,10},{3,11},{4,12},{5,13},{6,14},{7,15},{8,0},{9,1},... | collective-permute-start | bytes 165896 | tf_op jit(solution)/shard_map/ppermute | solution.py:310
  50.3 2.3 %collective-permute-start.19 = (bf16[1,216,128]{2,1,0:T(8,128)(2,1)S(1)}, bf16[1,216,128]{2,1,0:T(8,128)(2,1)S(1)}, u32[]{:S(2)}, u32[]{:S(2)}) collective-permute-start(bf16[1,216,128]{2,1,0:T(8,128)(2,1)S(1)} %get-tuple-element.59.refs_3_), channel_id=1, source_target_pairs={{0,8},{1,9},{2,10},{3,11},{4,12},{5,13},{6,14},{7,15},{8,0},{9,1},... | collective-permute-start | bytes 165896 | tf_op jit(solution)/shard_map/ppermute | solution.py:310
  52.6 2.2 %output_conv.1 = bf16[4,16,16,128]{3,2,1,0:T(8,128)(2,1)} custom-call(bf16[6,18,16,384]{3,2,1,0:T(8,128)(2,1)S(1)} %hidden_planes.1.refs_3_.refs_0_, bf16[3456,128]{1,0:T(8,128)(2,1)S(1)} %get-tuple-element.47.refs_1_, bf16[1,216,128]{2,1,0:T(8,128)(2,1)S(1)} %get-tuple-element.60.refs_2_), custom_call_target="tpu_custom_call" | custom-call | flops 1000 | tf_op jit(solution)/shard_map/output_conv/pallas_call | solution.py:31
  54.8 0.5 collective-permute-done.18.refs_1_
  55.4 1.2 %collective-permute-done.19.refs_3_ = bf16[1,216,128]{2,1,0:T(8,128)(2,1)S(1)} collective-permute-done((bf16[1,216,128]{2,1,0:T(8,128)(2,1)S(1)}, bf16[1,216,128]{2,1,0:T(8,128)(2,1)S(1)}, u32[]{:S(2)}, u32[]{:S(2)}) %collective-permute-start.19) | collective-permute-done | bytes 55328 | tf_op jit(solution)/shard_map/ppermute | solution.py:310
  56.5 0.7 %sum_last.1 = (f32[216,128]{1,0:T(8,128)}, f32[216,128]{1,0:T(8,128)}) custom-call(f32[1,216,128]{2,1,0:T(8,128)S(1)} %get-tuple-element.61.refs_0_, bf16[1,216,128]{2,1,0:T(8,128)(2,1)S(1)} %collective-permute-done.18.refs_1_, f32[1,216,128]{2,1,0:T(8,128)S(1)} %get-tuple-element.62.refs_2_, bf16[1,216,128]{2,1,0:T(8,128)(2,1)S(1)} %collective-permute-done.19.refs_3_), custom_call_target="tpu_custom_call" | custom-call | flops 1000 | tf_op jit(solution)/shard_map/sum_last/pallas_call | solution.py:31
  (9 shorter events, 0.2 us)
Async XLA Ops:
  1.8 14.6 %collective-permute-start.1 = (bf16[3,16,16,128]{3,2,1,0:T(8,128)(2,1)S(1)}, bf16[3,16,16,128]{3,2,1,0:T(8,128)(2,1)S(1)}, u32[]{:S(2)}, u32[]{:S(2)}) collective-permute-start(bf16[3,16,16,128]{3,2,1,0:T(8,128)(2,1)S(1)} %get-tuple-element.37), channel_id=1, source_target_pairs={{1,2},{2,1},{3,4},{4,3},{5,6},{6,5},{7,8},{8,7},{9,10},{10,9},{11,... | collective-permute-start | bytes 589832 | tf_op jit(solution)/shard_map/ppermute | solution.py:350
  2.5 16.1 %collective-permute-start = (bf16[3,16,16,128]{3,2,1,0:T(8,128)(2,1)S(1)}, bf16[3,16,16,128]{3,2,1,0:T(8,128)(2,1)S(1)}, u32[]{:S(2)}, u32[]{:S(2)}) collective-permute-start(bf16[3,16,16,128]{3,2,1,0:T(8,128)(2,1)S(1)} %get-tuple-element.36), channel_id=1, source_target_pairs={{0,1},{1,0},{2,3},{3,2},{4,5},{5,4},{6,7},{7,6},{8,9},{9,8},{10,11... | collective-permute-start | bytes 589832 | tf_op jit(solution)/shard_map/ppermute | solution.py:310
  6.9 9.5 %collective-permute-start.2 = (bf16[216,128]{1,0:T(8,128)(2,1)}, bf16[216,128]{1,0:T(8,128)(2,1)S(1)}, u32[]{:S(2)}, u32[]{:S(2)}) collective-permute-start(bf16[216,128]{1,0:T(8,128)(2,1)} %first_hbm.1), channel_id=1, source_target_pairs={{0,8},{1,9},{2,10},{3,11},{4,12},{5,13},{6,14},{7,15},{8,0},{9,1},... | collective-permute-start | bytes 165896 | tf_op jit(solution)/shard_map/ppermute | solution.py:310
  9.5 7.5 %collective-permute-start.4 = (bf16[216,128]{1,0:T(8,128)(2,1)}, bf16[216,128]{1,0:T(8,128)(2,1)S(1)}, u32[]{:S(2)}, u32[]{:S(2)}) collective-permute-start(bf16[216,128]{1,0:T(8,128)(2,1)} %second_hbm.1), channel_id=1, source_target_pairs={{0,8},{1,9},{2,10},{3,11},{4,12},{5,13},{6,14},{7,15},{8,0},{9,1},... | collective-permute-start | bytes 165896 | tf_op jit(solution)/shard_map/ppermute | solution.py:310
  16.4 4.8 %collective-permute-start.3 = (bf16[2,216,128]{2,1,0:T(8,128)(2,1)S(1)}, bf16[2,216,128]{2,1,0:T(8,128)(2,1)S(1)}, u32[]{:S(2)}, u32[]{:S(2)}) collective-permute-start(bf16[2,216,128]{2,1,0:T(8,128)(2,1)S(1)} %first_two.1.refs_0_), channel_id=1, source_target_pairs={{0,4},{1,3},{2,6},{3,1},{4,0},{5,7},{6,2},{7,5},{8,12},{9,11},{10,... | collective-permute-start | bytes 331784 | tf_op jit(solution)/shard_map/ppermute | solution.py:315
  17.0 6.1 %collective-permute-start.8 = (bf16[2,216,128]{2,1,0:T(8,128)(2,1)S(1)}, bf16[2,216,128]{2,1,0:T(8,128)(2,1)S(1)}, u32[]{:S(2)}, u32[]{:S(2)}) collective-permute-start(bf16[2,216,128]{2,1,0:T(8,128)(2,1)S(1)} %second_two.1.refs_2_.refs_0_), channel_id=1, source_target_pairs={{0,4},{1,3},{2,6},{3,1},{4,0},{5,7},{6,2},{7,5},{8,12},{9,11},{10,... | collective-permute-start | bytes 331784 | tf_op jit(solution)/shard_map/ppermute | solution.py:315
  21.2 6.0 %collective-permute-start.5 = (bf16[4,216,128]{2,1,0:T(8,128)(2,1)S(1)}, bf16[4,216,128]{2,1,0:T(8,128)(2,1)S(1)}, u32[]{:S(2)}, u32[]{:S(2)}) collective-permute-start(bf16[4,216,128]{2,1,0:T(8,128)(2,1)S(1)} %first_four.1.refs_1_), channel_id=1, source_target_pairs={{0,2},{1,5},{2,0},{3,7},{4,6},{5,1},{6,4},{7,3},{8,10},{9,13},{10,... | collective-permute-start | bytes 663560 | tf_op jit(solution)/shard_map/ppermute | solution.py:315
  23.1 6.5 %collective-permute-start.9 = (bf16[4,216,128]{2,1,0:T(8,128)(2,1)S(1)}, bf16[4,216,128]{2,1,0:T(8,128)(2,1)S(1)}, u32[]{:S(2)}, u32[]{:S(2)}) collective-permute-start(bf16[4,216,128]{2,1,0:T(8,128)(2,1)S(1)} %second_four.1.refs_1_), channel_id=1, source_target_pairs={{0,2},{1,5},{2,0},{3,7},{4,6},{5,1},{6,4},{7,3},{8,10},{9,13},{10,... | collective-permute-start | bytes 663560 | tf_op jit(solution)/shard_map/ppermute | solution.py:315
  23.4 6.2 %collective-permute-start.6 = (bf16[4,216,128]{2,1,0:T(8,128)(2,1)S(1)}, bf16[4,216,128]{2,1,0:T(8,128)(2,1)S(1)}, u32[]{:S(2)}, u32[]{:S(2)}) collective-permute-start(bf16[4,216,128]{2,1,0:T(8,128)(2,1)S(1)} %first_four.1.refs_1_), channel_id=1, source_target_pairs={{0,1},{1,0},{2,3},{3,2},{4,5},{5,4},{6,7},{7,6},{8,9},{9,8},{10,11... | collective-permute-start | bytes 663560 | tf_op jit(solution)/shard_map/ppermute | solution.py:310
  27.2 2.4 %collective-permute-start.7 = (bf16[4,216,128]{2,1,0:T(8,128)(2,1)S(1)}, bf16[4,216,128]{2,1,0:T(8,128)(2,1)S(1)}, u32[]{:S(2)}, u32[]{:S(2)}) collective-permute-start(bf16[4,216,128]{2,1,0:T(8,128)(2,1)S(1)} %collective-permute-done.5.refs_2_), channel_id=1, source_target_pairs={{0,1},{1,0},{2,3},{3,2},{4,5},{5,4},{6,7},{7,6},{8,9},{9,8},{10,11... | collective-permute-start | bytes 663560 | tf_op jit(solution)/shard_map/ppermute | solution.py:310
  27.2 6.1 %collective-permute-start.10 = (bf16[4,216,128]{2,1,0:T(8,128)(2,1)S(1)}, bf16[4,216,128]{2,1,0:T(8,128)(2,1)S(1)}, u32[]{:S(2)}, u32[]{:S(2)}) collective-permute-start(bf16[4,216,128]{2,1,0:T(8,128)(2,1)S(1)} %second_four.1.refs_1_), channel_id=1, source_target_pairs={{0,1},{1,0},{2,3},{3,2},{4,5},{5,4},{6,7},{7,6},{8,9},{9,8},{10,11... | collective-permute-start | bytes 663560 | tf_op jit(solution)/shard_map/ppermute | solution.py:310
  29.6 3.7 %collective-permute-start.11 = (bf16[4,216,128]{2,1,0:T(8,128)(2,1)S(1)}, bf16[4,216,128]{2,1,0:T(8,128)(2,1)S(1)}, u32[]{:S(2)}, u32[]{:S(2)}) collective-permute-start(bf16[4,216,128]{2,1,0:T(8,128)(2,1)S(1)} %collective-permute-done.9.refs_7_.refs_2_), channel_id=1, source_target_pairs={{0,1},{1,0},{2,3},{3,2},{4,5},{5,4},{6,7},{7,6},{8,9},{9,8},{10,11... | collective-permute-start | bytes 663560 | tf_op jit(solution)/shard_map/ppermute | solution.py:310
  32.8 3.5 %collective-permute-start.14 = (bf16[8,216,128]{2,1,0:T(8,128)(2,1)S(1)}, bf16[8,216,128]{2,1,0:T(8,128)(2,1)S(1)}, u32[]{:S(2)}, u32[]{:S(2)}) collective-permute-start(bf16[8,216,128]{2,1,0:T(8,128)(2,1)S(1)} %get-tuple-element.52), channel_id=1, source_target_pairs={{0,1},{1,0},{2,3},{3,2},{4,5},{5,4},{6,7},{7,6},{8,9},{9,8},{10,11... | collective-permute-start | bytes 1327112 | tf_op jit(solution)/shard_map/ppermute | solution.py:310
  36.2 1.9 %collective-permute-start.12 = (bf16[8,216,128]{2,1,0:T(8,128)(2,1)S(1)}, bf16[8,216,128]{2,1,0:T(8,128)(2,1)S(1)}, u32[]{:S(2)}, u32[]{:S(2)}) collective-permute-start(bf16[8,216,128]{2,1,0:T(8,128)(2,1)S(1)} %get-tuple-element.48), channel_id=1, source_target_pairs={{0,1},{1,0},{2,3},{3,2},{4,5},{5,4},{6,7},{7,6},{8,9},{9,8},{10,11... | collective-permute-start | bytes 1327112 | tf_op jit(solution)/shard_map/ppermute | solution.py:310
  36.4 6.0 %collective-permute-start.15 = (bf16[4,216,128]{2,1,0:T(8,128)(2,1)S(1)}, bf16[4,216,128]{2,1,0:T(8,128)(2,1)S(1)}, u32[]{:S(2)}, u32[]{:S(2)}) collective-permute-start(bf16[4,216,128]{2,1,0:T(8,128)(2,1)S(1)} %get-tuple-element.54), channel_id=1, source_target_pairs={{0,2},{1,5},{2,0},{3,7},{4,6},{5,1},{6,4},{7,3},{8,10},{9,13},{10,... | collective-permute-start | bytes 663560 | tf_op jit(solution)/shard_map/ppermute | solution.py:315
  38.1 6.6 %collective-permute-start.13 = (bf16[4,216,128]{2,1,0:T(8,128)(2,1)S(1)}, bf16[4,216,128]{2,1,0:T(8,128)(2,1)S(1)}, u32[]{:S(2)}, u32[]{:S(2)}) collective-permute-start(bf16[4,216,128]{2,1,0:T(8,128)(2,1)S(1)} %get-tuple-element.50.refs_3_), channel_id=1, source_target_pairs={{0,2},{1,5},{2,0},{3,7},{4,6},{5,1},{6,4},{7,3},{8,10},{9,13},{10,... | collective-permute-start | bytes 663560 | tf_op jit(solution)/shard_map/ppermute | solution.py:315
  42.4 4.8 %collective-permute-start.17 = (bf16[2,216,128]{2,1,0:T(8,128)(2,1)S(1)}, bf16[2,216,128]{2,1,0:T(8,128)(2,1)S(1)}, u32[]{:S(2)}, u32[]{:S(2)}) collective-permute-start(bf16[2,216,128]{2,1,0:T(8,128)(2,1)S(1)} %get-tuple-element.55.refs_3_), channel_id=1, source_target_pairs={{0,4},{1,3},{2,6},{3,1},{4,0},{5,7},{6,2},{7,5},{8,12},{9,11},{10,... | collective-permute-start | bytes 331784 | tf_op jit(solution)/shard_map/ppermute | solution.py:315
  44.8 4.8 %collective-permute-start.16 = (bf16[2,216,128]{2,1,0:T(8,128)(2,1)S(1)}, bf16[2,216,128]{2,1,0:T(8,128)(2,1)S(1)}, u32[]{:S(2)}, u32[]{:S(2)}) collective-permute-start(bf16[2,216,128]{2,1,0:T(8,128)(2,1)S(1)} %get-tuple-element.57.refs_3_), channel_id=1, source_target_pairs={{0,4},{1,3},{2,6},{3,1},{4,0},{5,7},{6,2},{7,5},{8,12},{9,11},{10,... | collective-permute-start | bytes 331784 | tf_op jit(solution)/shard_map/ppermute | solution.py:315
  49.6 5.7 %collective-permute-start.18 = (bf16[1,216,128]{2,1,0:T(8,128)(2,1)S(1)}, bf16[1,216,128]{2,1,0:T(8,128)(2,1)S(1)}, u32[]{:S(2)}, u32[]{:S(2)}) collective-permute-start(bf16[1,216,128]{2,1,0:T(8,128)(2,1)S(1)} %get-tuple-element.60.refs_2_), channel_id=1, source_target_pairs={{0,8},{1,9},{2,10},{3,11},{4,12},{5,13},{6,14},{7,15},{8,0},{9,1},... | collective-permute-start | bytes 165896 | tf_op jit(solution)/shard_map/ppermute | solution.py:310
  50.3 6.2 %collective-permute-start.19 = (bf16[1,216,128]{2,1,0:T(8,128)(2,1)S(1)}, bf16[1,216,128]{2,1,0:T(8,128)(2,1)S(1)}, u32[]{:S(2)}, u32[]{:S(2)}) collective-permute-start(bf16[1,216,128]{2,1,0:T(8,128)(2,1)S(1)} %get-tuple-element.59.refs_3_), channel_id=1, source_target_pairs={{0,8},{1,9},{2,10},{3,11},{4,12},{5,13},{6,14},{7,15},{8,0},{9,1},... | collective-permute-start | bytes 165896 | tf_op jit(solution)/shard_map/ppermute | solution.py:310

commit v3 on v2

--- a/solution.py
+++ b/solution.py
@@ -80,52 +80,53 @@
     lax.fori_loop(0, planes + 2, transposed, 0)
 
 
-def load_kernel(f_hbm, g_hbm, first_hbm, second_hbm, *refs):
-    f_ref, g_ref, first_ref, second_ref, sems = refs
-    moves = [
+def copy_all(moves, sems):
+    copies = [
         pltpu.make_async_copy(source, target, sems.at[at])
-        for at, (source, target) in enumerate(
-            (
-                (first_hbm, first_ref.at[0]),
-                (second_hbm, second_ref.at[0]),
-                (f_hbm, f_ref),
-                (g_hbm, g_ref),
-            )
-        )
+        for at, (source, target) in enumerate(moves)
     ]
-    for move in moves:
-        move.start()
-    for move in moves:
-        move.wait()
-
-
-def edges_kernel(me_ref, f_ref, g_ref, core_ref, chip_ref):
-    planes = f_ref.shape[0]
+    for copy in copies:
+        copy.start()
+    for copy in copies:
+        copy.wait()
+
+
+def load_kernel(f_hbm, g_hbm, f_ref, g_ref, sems):
+    copy_all(((f_hbm, f_ref), (g_hbm, g_ref)), sems)
+
+
+def load_shards_kernel(first_hbm, second_hbm, shards_ref, sems):
+    copy_all(((first_hbm, shards_ref.at[0]), (second_hbm, shards_ref.at[1])), sems)
+
+
+def edges_kernel(me_ref, f_hbm, g_hbm, core_ref, chip_ref, sems):
+    planes = f_hbm.shape[0]
     odd = me_ref[0] % 2
-    for ref, low in ((core_ref, odd == 1), (chip_ref, odd == 0)):
-        ref[0:2] = f_ref[pl.ds(jnp.where(low, 0, planes - 2), 2)]
-        ref[2:3] = g_ref[pl.ds(jnp.where(low, 0, planes - 1), 1)]
-
-
-def loaded(features, first, second, cotangent):
-    args = [
-        pltpu.with_memory_space_constraint(a, pltpu.HBM)
-        for a in (features, cotangent, first, second)
-    ]
+    moves = []
+    for ref, low in ((chip_ref, odd == 0), (core_ref, odd == 1)):
+        moves.append((f_hbm.at[pl.ds(jnp.where(low, 0, planes - 2), 2)], ref.at[pl.ds(0, 2)]))
+        moves.append((g_hbm.at[pl.ds(jnp.where(low, 0, planes - 1), 1)], ref.at[pl.ds(2, 1)]))
+    copy_all(moves, sems)
+
+
+def from_hbm(kernel, name, outs, args, scalars=(), wait_for=()):
+    args = [pltpu.with_memory_space_constraint(a, pltpu.HBM) for a in args]
+    first, last = len(scalars) + len(args), len(scalars) + len(args) + len(wait_for)
+
+    def body(*refs):
+        kernel(*refs[:first], *refs[last:])
+
+    spaces = [pltpu.SMEM] * len(scalars) + [pltpu.HBM] * len(args) + [pl.ANY] * len(wait_for)
     return pl.pallas_call(
-        load_kernel,
-        out_shape=[
-            like(features.shape, BF16),
-            like(cotangent.shape, BF16),
-            like((1, *first.shape), BF16),
-            like((1, *second.shape), BF16),
-        ],
-        in_specs=[pl.BlockSpec(memory_space=pltpu.HBM) for _ in args],
-        out_specs=[pl.BlockSpec(memory_space=pltpu.VMEM) for _ in range(4)],
-        scratch_shapes=[pltpu.SemaphoreType.DMA((len(args),))],
-        name="load",
+        body,
+        out_shape=outs,
+        in_specs=[pl.BlockSpec(memory_space=space) for space in spaces],
+        out_specs=[pl.BlockSpec(memory_space=pltpu.VMEM) for _ in outs],
+        scratch_shapes=[pltpu.SemaphoreType.DMA((4,))],
+        name=name,
         compiler_params=pltpu.CompilerParams(vmem_limit_bytes=LIMIT),
-    )(*args)
+        cost_estimate=pl.CostEstimate(flops=1000, bytes_accessed=0, transcendentals=0),
+    )(*scalars, *args, *wait_for)
 
 
 def join_kernel(*refs):
@@ -184,18 +185,18 @@
     return jnp.where(core == 0, 4, 2), jnp.where(core == 0, 2, 4)
 
 
-def assemble(me, pieces, dst):
+def assemble(bank, me, pieces, dst):
     rows = pieces[0].shape[1]
     near, far = near_far(me % 2)
-    for piece, start, side in zip(
-        pieces, (me, me ^ far, me ^ 1, me ^ 1 ^ near), (near, near, far, far)
-    ):
-        for at, owner in enumerate((start, start ^ 8, start ^ side, start ^ 8 ^ side)):
-            dst[pl.ds(pl.multiple_of(owner * rows, 8), rows)] = piece[at]
-
-
-def assemble_in_order(me, pieces, dst):
-    dst[...] = pieces[0][...]
+    starts = (me, me ^ 8, me ^ far, me ^ 8 ^ far)
+    starts += tuple(start ^ 1 for start in (me, me ^ 8, me ^ near, me ^ 8 ^ near))
+    for at, (piece, start) in enumerate(zip(pieces, starts)):
+        for next_to, owner in enumerate((start, start ^ (near if at < 4 else far))):
+            dst[pl.ds(pl.multiple_of(owner * rows, 8), rows)] = piece[2 * next_to + bank]
+
+
+def assemble_in_order(bank, me, pieces, dst):
+    dst[...] = pieces[bank][...]
 
 
 def split_terms(me, total_ref, send_ref, keep_ref):
@@ -213,7 +214,7 @@
     bank_ref, hidden_ref, slope_ref, send_ref, keep_ref, total_ref = out_refs
     me = me_ref[0]
     planes, height, width, channels = hidden_ref.shape
-    place(me, piece_refs, bank_ref)
+    place(0, me, piece_refs, bank_ref)
     active, slope = gelu_parts(conv_rows(xf_ref, 1, planes, bank_ref))
     slope_ref[...] = slope.T
     hidden = active.astype(BF16)
@@ -236,7 +237,7 @@
     channels = slope_ref.shape[0]
     planes, _, _, cells = gt_ref.shape
     planes -= 2
-    place(me, piece_refs, bank_ref)
+    place(1, me, piece_refs, bank_ref)
     back = jnp.concatenate(
         [bank_ref[tap * channels : (tap + 1) * channels] for tap in reversed(range(27))], axis=1
     )
@@ -338,12 +339,20 @@
     place = me if direct else jnp.zeros((1,), jnp.int32)
     order = assemble if direct else assemble_in_order
 
-    features, cotangent, first_shard, second_shard = loaded(
-        features, filters_first, filters_second, cotangent
-    )
     edge = like((3, height, width, channels), BF16)
-    to_core, to_chip = local_call(
-        edges_kernel, "edges", [edge, edge], [me, features, cotangent], scalars=1
+    to_core, to_chip = from_hbm(edges_kernel, "edges", [edge, edge], [features, cotangent], [me])
+    (own,) = from_hbm(
+        load_shards_kernel,
+        "load_shards",
+        [like((2, rows, channels), BF16)],
+        [filters_first, filters_second],
+    )
+    features, cotangent = from_hbm(
+        load_kernel,
+        "load",
+        [like(features.shape, BF16), like(cotangent.shape, BF16)],
+        [features, cotangent],
+        wait_for=[to_chip],
     )
     from_core = swap(to_core, count, 1)
     next_chip = [(i, i + 1 if i % 2 else i - 1) for i in range(1, count - 1)]
@@ -361,33 +370,24 @@
     )
     wait_for = []
     if direct:
-        far = [swap(shard, count, 8) for shard in (filters_first, filters_second)]
-        two_first = joined([first_shard, far[0]], "first_two", [from_chip])
-        near_first = swap_mixed(two_first, count, 4, 2)
-        two_second = joined([second_shard, far[1]], "second_two")
-        near_second = swap_mixed(two_second, count, 4, 2)
-        four_first = joined([two_first, near_first], "first_four", [two_second, xf])
-        cross_first = swap_mixed(four_first, count, 2, 4)
-        four_second = joined([two_second, near_second], "second_four")
-        cross_second = swap_mixed(four_second, count, 2, 4)
-        wait_for = [cross_second]
-        first = [four_first, cross_first, swap(four_first, count, 1), swap(cross_first, count, 1)]
-        second = [
-            four_second,
-            cross_second,
-            swap(four_second, count, 1),
-            swap(cross_second, count, 1),
+        far = swap(own, count, 8)
+        near = swap_mixed(own, count, 4, 2)
+        close = joined([own, near], "own_and_near", [])
+        cross = swap_mixed(close, count, 2, 4)
+        near = swap_mixed(far, count, 4, 2)
+        away = joined([far, near], "far_and_near", [xf])
+        cross_away = swap_mixed(away, count, 2, 4)
+        pieces = [close, away, cross, cross_away]
+        pieces += [swap(piece, count, 1) for piece in pieces]
+    else:
+        pieces = [
+            lax.all_gather(shard, "slab", axis=0, tiled=True)
+            for shard in (filters_first, filters_second)
         ]
-    else:
-        first, second = (
-            [lax.all_gather(shard, "slab", axis=0, tiled=True)]
-            for shard in (filters_first, filters_second)
-        )
-
     terms = [like((8, shard_rows, channels), BF16), like((8, shard_rows, channels), F32)]
     total = pltpu.VMEM((taps, channels), F32)
     bank, hidden, slope, send_second, keep_second = local_call(
-        functools.partial(first_kernel, len(first), order),
+        functools.partial(first_kernel, len(pieces), order),
         "hidden_and_second_grad",
         [
             like((taps, channels), BF16),
@@ -395,16 +395,16 @@
             like((channels, cells), F32),
             *terms,
         ],
-        [place, *first, xf, xg],
+        [place, *pieces, xf, xg],
         scratch=[total],
         scalars=1,
         wait_for=wait_for,
     )
     bank_second, send_first, keep_first = local_call(
-        functools.partial(second_kernel, len(second), order),
+        functools.partial(second_kernel, len(pieces), order),
         "first_grad",
         [like((taps, channels), BF16), *terms],
-        [place, *second, xf, gt, slope],
+        [place, *pieces, xf, gt, slope],
         scratch=[total],
         scalars=1,
     )

time: 57.4 us -> 55.2 us (0.962)
  waiting for transfers between devices: 24.7 us -> 18 us
  starting transfers between devices: 18.1 us -> 20.7 us
  Pallas kernels: 13.6 us -> 15.4 us
    ppermute x11 -> x10, waiting for transfers between devices: 9.05 us -> 2.82 us  [swap(): lax.ppermute(value, 'slab', [(i, i ^ distance) for i in range(count)])]
    ppermute x8, starting transfers between devices: 5.95 us -> 8.12 us  [swap_mixed(): return lax.ppermute(value, 'slab', pairs)]
    pallas_call x1 -> x3, Pallas kernels: 1.13 us -> 2.97 us  [from_hbm(): pl.pallas_call(body, out_shape=outs, in_specs=[pl.BlockSpec(memory_space=...]
    ppermute x11 -> x10, starting transfers between devices: 11.5 us -> 11.9 us  [swap(): lax.ppermute(value, 'slab', [(i, i ^ distance) for i in range(count)])]
    pallas_call x17 -> x14, Pallas kernels: 12.5 us -> 12.5 us  [local_call(): pl.pallas_call(body, out_shape=list(outs), in_specs=[pl.BlockSpec(memory_...]
  transfers between devices with their start and end apart: 20 -> 19, of which waited for: 13 -> 10; matrix products, arithmetic and copies ran while one was open for 0% -> 0% of each run, Pallas kernels for 20% -> 19%
where the time goes in v3:
time: 55.2 us; the launch traced here: 55 us
  starting transfers between devices  20.7 us (38%)
  waiting for transfers between devices  18 us (33%)
  Pallas kernels  15.4 us (28%)
  between operations  0.73 us (1%)
    ppermute x8, waiting for transfers between devices, swap_mixed(): return lax.ppermute(value, 'slab', pairs)  15.2 us
    pallas_call x14, Pallas kernels, local_call(): pl.pallas_call(body, out_shape=list(outs), in_specs=[pl.BlockSpec(memory_...  12.5 us
    ppermute x10, starting transfers between devices, swap(): lax.ppermute(value, 'slab', [(i, i ^ distance) for i in range(count)])  11.9 us
    ppermute x8, starting transfers between devices, swap_mixed(): return lax.ppermute(value, 'slab', pairs)  8.12 us
    pallas_call x3, Pallas kernels, from_hbm(): pl.pallas_call(body, out_shape=outs, in_specs=[pl.BlockSpec(memory_space=...  2.97 us
    ppermute x10, waiting for transfers between devices, swap(): lax.ppermute(value, 'slab', [(i, i ^ distance) for i in range(count)])  2.82 us
  transfers between devices with their start and end apart: 19, of which 10 were waited for; matrix products, arithmetic and copies ran while one was open for 0% of the time, Pallas kernels for 19%

profile of v3, /device:TPU:0, one launch (start us, length us, event | category | flops | bytes accessed | tf_op | source)
XLA Modules:
  0.0 55.0 jit_solution(13497690486005539546)
XLA Ops:
  0.6 0.9 %load_shards.1.refs_0_ = bf16[2,216,128]{2,1,0:T(8,128)(2,1)S(1)} custom-call(bf16[216,128]{1,0:T(8,128)(2,1)} %refs_0_.3, bf16[216,128]{1,0:T(8,128)(2,1)} %refs_1_.5), custom_call_target="tpu_custom_call" | custom-call | flops 1000 | tf_op jit(solution)/shard_map/load_shards/pallas_call | solution.py:120
  1.5 4.1 %collective-permute-start.3 = (bf16[2,216,128]{2,1,0:T(8,128)(2,1)S(1)}, bf16[2,216,128]{2,1,0:T(8,128)(2,1)S(1)}, u32[]{:S(2)}, u32[]{:S(2)}) collective-permute-start(bf16[2,216,128]{2,1,0:T(8,128)(2,1)S(1)} %load_shards.1.refs_0_), channel_id=1, source_target_pairs={{0,8},{1,9},{2,10},{3,11},{4,12},{5,13},{6,14},{7,15},{8,0},{9,1},... | collective-permute-start | bytes 331784 | tf_op jit(solution)/shard_map/ppermute | solution.py:311
  5.6 1.0 %edges.1 = (bf16[3,16,16,128]{3,2,1,0:T(8,128)(2,1)S(1)}, bf16[3,16,16,128]{3,2,1,0:T(8,128)(2,1)S(1)}) custom-call(s32[1]{0:T(128)} %bitcast.refs_0_, bf16[4,16,16,128]{3,2,1,0:T(8,128)(2,1)} %refs_0_.2, bf16[4,16,16,128]{3,2,1,0:T(8,128)(2,1)} %refs_1_.4), custom_call_target="tpu_custom_call" | custom-call | flops 1000 | tf_op jit(solution)/shard_map/edges/pallas_call | solution.py:120
  6.7 0.7 %collective-permute-start.1 = (bf16[3,16,16,128]{3,2,1,0:T(8,128)(2,1)S(1)}, bf16[3,16,16,128]{3,2,1,0:T(8,128)(2,1)S(1)}, u32[]{:S(2)}, u32[]{:S(2)}) collective-permute-start(bf16[3,16,16,128]{3,2,1,0:T(8,128)(2,1)S(1)} %get-tuple-element.32.refs_2_), channel_id=1, source_target_pairs={{1,2},{2,1},{3,4},{4,3},{5,6},{6,5},{7,8},{8,7},{9,10},{10,9},{11,... | collective-permute-start | bytes 589832 | tf_op jit(solution)/shard_map/ppermute | solution.py:359
  7.3 2.9 %collective-permute-start = (bf16[3,16,16,128]{3,2,1,0:T(8,128)(2,1)S(1)}, bf16[3,16,16,128]{3,2,1,0:T(8,128)(2,1)S(1)}, u32[]{:S(2)}, u32[]{:S(2)}) collective-permute-start(bf16[3,16,16,128]{3,2,1,0:T(8,128)(2,1)S(1)} %get-tuple-element.35), channel_id=1, source_target_pairs={{0,1},{1,0},{2,3},{3,2},{4,5},{5,4},{6,7},{7,6},{8,9},{9,8},{10,11... | collective-permute-start | bytes 589832 | tf_op jit(solution)/shard_map/ppermute | solution.py:311
  10.3 1.6 %collective-permute-start.2 = (bf16[2,216,128]{2,1,0:T(8,128)(2,1)S(1)}, bf16[2,216,128]{2,1,0:T(8,128)(2,1)S(1)}, u32[]{:S(2)}, u32[]{:S(2)}) collective-permute-start(bf16[2,216,128]{2,1,0:T(8,128)(2,1)S(1)} %load_shards.1.refs_0_), channel_id=1, source_target_pairs={{0,4},{1,3},{2,6},{3,1},{4,0},{5,7},{6,2},{7,5},{8,12},{9,11},{10,... | collective-permute-start | bytes 331784 | tf_op jit(solution)/shard_map/ppermute | solution.py:316
  11.9 0.0 collective-permute-done.3.refs_0_
  11.9 0.5 collective-permute-start.4
  12.3 1.1 %load.1 = (bf16[4,16,16,128]{3,2,1,0:T(8,128)(2,1)S(1)}, bf16[4,16,16,128]{3,2,1,0:T(8,128)(2,1)S(1)}) custom-call(bf16[4,16,16,128]{3,2,1,0:T(8,128)(2,1)} %refs_0_.2, bf16[4,16,16,128]{3,2,1,0:T(8,128)(2,1)} %refs_1_.4, bf16[3,16,16,128]{3,2,1,0:T(8,128)(2,1)S(1)} %get-tuple-element.32.refs_2_), custom_call_target="tpu_custom_call" | custom-call | flops 1000 | tf_op jit(solution)/shard_map/load/pallas_call | solution.py:120
  13.4 2.2 %collective-permute-done.2.refs_1_ = bf16[2,216,128]{2,1,0:T(8,128)(2,1)S(1)} collective-permute-done((bf16[2,216,128]{2,1,0:T(8,128)(2,1)S(1)}, bf16[2,216,128]{2,1,0:T(8,128)(2,1)S(1)}, u32[]{:S(2)}, u32[]{:S(2)}) %collective-permute-start.2) | collective-permute-done | bytes 110624 | tf_op jit(solution)/shard_map/ppermute | solution.py:316
  15.6 1.0 %collective-permute-start.5 = (bf16[4,216,128]{2,1,0:T(8,128)(2,1)S(1)}, bf16[4,216,128]{2,1,0:T(8,128)(2,1)S(1)}, u32[]{:S(2)}, u32[]{:S(2)}) collective-permute-start(bf16[4,216,128]{2,1,0:T(8,128)(2,1)S(1)} %own_and_near.1.refs_1_), channel_id=1, source_target_pairs={{0,2},{1,5},{2,0},{3,7},{4,6},{5,1},{6,4},{7,3},{8,10},{9,13},{10,... | collective-permute-start | bytes 663560 | tf_op jit(solution)/shard_map/ppermute | solution.py:316
  16.6 0.0 collective-permute-done.1.refs_4_
  16.6 0.0 collective-permute-done.refs_3_
  16.6 1.9 %shifted_planes.1 = (bf16[8,18,16,384]{3,2,1,0:T(8,128)(2,1)S(1)}, bf16[6,18,16,384]{3,2,1,0:T(8,128)(2,1)S(1)}, bf16[6,9,128,256]{3,2,1,0:T(8,128)(2,1)S(1)}) custom-call(s32[1]{0:T(128)} %bitcast.refs_0_, bf16[4,16,16,128]{3,2,1,0:T(8,128)(2,1)S(1)} %get-tuple-element.33.refs_1_, bf16[4,16,16,128]{3,2,1,0:T(8,128)(2,1)S(1)} %get-tuple-element.34.refs_2_, ...), custom_call_target="tpu_custom_call" | custom-call | flops 1000 | tf_op jit(solution)/shard_map/shifted_planes/pallas_call | solution.py:31
  18.6 0.0 collective-permute-done.4.refs_1_
  18.6 1.1 %collective-permute-start.6 = (bf16[4,216,128]{2,1,0:T(8,128)(2,1)S(1)}, bf16[4,216,128]{2,1,0:T(8,128)(2,1)S(1)}, u32[]{:S(2)}, u32[]{:S(2)}) collective-permute-start(bf16[4,216,128]{2,1,0:T(8,128)(2,1)S(1)} %far_and_near.1.refs_2_), channel_id=1, source_target_pairs={{0,2},{1,5},{2,0},{3,7},{4,6},{5,1},{6,4},{7,3},{8,10},{9,13},{10,... | collective-permute-start | bytes 663560 | tf_op jit(solution)/shard_map/ppermute | solution.py:316
  19.7 0.6 %collective-permute-start.7 = (bf16[4,216,128]{2,1,0:T(8,128)(2,1)S(1)}, bf16[4,216,128]{2,1,0:T(8,128)(2,1)S(1)}, u32[]{:S(2)}, u32[]{:S(2)}) collective-permute-start(bf16[4,216,128]{2,1,0:T(8,128)(2,1)S(1)} %own_and_near.1.refs_1_), channel_id=1, source_target_pairs={{0,1},{1,0},{2,3},{3,2},{4,5},{5,4},{6,7},{7,6},{8,9},{9,8},{10,11... | collective-permute-start | bytes 663560 | tf_op jit(solution)/shard_map/ppermute | solution.py:311
  20.3 0.1 collective-permute-start.8
  20.4 1.2 %collective-permute-done.5.refs_3_ = bf16[4,216,128]{2,1,0:T(8,128)(2,1)S(1)} collective-permute-done((bf16[4,216,128]{2,1,0:T(8,128)(2,1)S(1)}, bf16[4,216,128]{2,1,0:T(8,128)(2,1)S(1)}, u32[]{:S(2)}, u32[]{:S(2)}) %collective-permute-start.5) | collective-permute-done | bytes 221216 | tf_op jit(solution)/shard_map/ppermute | solution.py:316
  21.6 0.1 collective-permute-start.9
  21.7 2.9 %collective-permute-done.6.refs_4_ = bf16[4,216,128]{2,1,0:T(8,128)(2,1)S(1)} collective-permute-done((bf16[4,216,128]{2,1,0:T(8,128)(2,1)S(1)}, bf16[4,216,128]{2,1,0:T(8,128)(2,1)S(1)}, u32[]{:S(2)}, u32[]{:S(2)}) %collective-permute-start.6) | collective-permute-done | bytes 221216 | tf_op jit(solution)/shard_map/ppermute | solution.py:316
  24.6 0.4 collective-permute-start.10
  25.0 0.0 collective-permute-done.7.refs_5_
  25.0 0.0 collective-permute-done.8.refs_6_
  25.0 0.0 collective-permute-done.9.refs_7_
  25.1 1.1 %collective-permute-done.10.refs_8_ = bf16[4,216,128]{2,1,0:T(8,128)(2,1)S(1)} collective-permute-done((bf16[4,216,128]{2,1,0:T(8,128)(2,1)S(1)}, bf16[4,216,128]{2,1,0:T(8,128)(2,1)S(1)}, u32[]{:S(2)}, u32[]{:S(2)}) %collective-permute-start.10) | collective-permute-done | bytes 221216 | tf_op jit(solution)/shard_map/ppermute | solution.py:311
  26.1 3.1 %hidden_and_second_grad.1 = (bf16[3456,128]{1,0:T(8,128)(2,1)S(1)}, bf16[4,16,16,128]{3,2,1,0:T(8,128)(2,1)S(1)}, f32[128,1024]{1,0:T(8,128)S(1)}, bf16[8,216,128]{2,1,0:T(8,128)(2,1)S(1)}, f32[8,216,128]{2,1,0:T(8,128)S(1)}) custom-call(s32[1]{0:T(128)} %bitcast.refs_0_, bf16[4,216,128]{2,1,0:T(8,128)(2,1)S(1)} %own_and_near.1.refs_1_, ...), custom_call_target="tpu_custom_call" | custom-call | flops 1000 | tf_op jit(solution)/shard_map/hidden_and_second_grad/pallas_call | solution.py:31
  29.3 0.4 collective-permute-start.13
  29.7 2.8 %first_grad.1 = (bf16[3456,128]{1,0:T(8,128)(2,1)S(1)}, bf16[8,216,128]{2,1,0:T(8,128)(2,1)S(1)}, f32[8,216,128]{2,1,0:T(8,128)S(1)}) custom-call(s32[1]{0:T(128)} %bitcast.refs_0_, bf16[4,216,128]{2,1,0:T(8,128)(2,1)S(1)} %own_and_near.1.refs_1_, bf16[4,216,128]{2,1,0:T(8,128)(2,1)S(1)} %far_and_near.1.refs_2_, ...), custom_call_target="tpu_custom_call" | custom-call | flops 1000 | tf_op jit(solution)/shard_map/first_grad/pallas_call | solution.py:31
  32.5 0.2 collective-permute-start.11
  32.7 0.0 collective-permute-done.13.refs_2_
  32.7 0.1 second_pair.1
  32.8 1.5 %collective-permute-start.14 = (bf16[4,216,128]{2,1,0:T(8,128)(2,1)S(1)}, bf16[4,216,128]{2,1,0:T(8,128)(2,1)S(1)}, u32[]{:S(2)}, u32[]{:S(2)}) collective-permute-start(bf16[4,216,128]{2,1,0:T(8,128)(2,1)S(1)} %get-tuple-element.50), channel_id=1, source_target_pairs={{0,2},{1,5},{2,0},{3,7},{4,6},{5,1},{6,4},{7,3},{8,10},{9,13},{10,... | collective-permute-start | bytes 663560 | tf_op jit(solution)/shard_map/ppermute | solution.py:316
  34.3 1.3 %hidden_planes.1.refs_3_.refs_0_ = bf16[6,18,16,384]{3,2,1,0:T(8,128)(2,1)S(1)} custom-call(s32[1]{0:T(128)} %bitcast.refs_0_, bf16[8,18,16,384]{3,2,1,0:T(8,128)(2,1)S(1)} %get-tuple-element.36.refs_2_.refs_9_.refs_1_, bf16[3456,128]{1,0:T(8,128)(2,1)S(1)} %get-tuple-element.38.refs_2_, bf16[4,16,16,128]{3,2,1,0:T(8,128)(2,1)S(1)} %get-tuple-element.39.refs_3_, ...), custom_call_target="tpu_custom_call" | custom-call | flops 1000 | tf_op jit(solution)/shard_map/hidden_planes/pallas_call | solution.py:31
  35.7 0.0 collective-permute-done.11.refs_2_
  35.7 0.1 first_pair.1
  35.8 0.7 %collective-permute-start.12 = (bf16[4,216,128]{2,1,0:T(8,128)(2,1)S(1)}, bf16[4,216,128]{2,1,0:T(8,128)(2,1)S(1)}, u32[]{:S(2)}, u32[]{:S(2)}) collective-permute-start(bf16[4,216,128]{2,1,0:T(8,128)(2,1)S(1)} %get-tuple-element.46.refs_3_), channel_id=1, source_target_pairs={{0,2},{1,5},{2,0},{3,7},{4,6},{5,1},{6,4},{7,3},{8,10},{9,13},{10,... | collective-permute-start | bytes 663560 | tf_op jit(solution)/shard_map/ppermute | solution.py:316
  36.5 2.4 %collective-permute-done.14.refs_2_ = bf16[4,216,128]{2,1,0:T(8,128)(2,1)S(1)} collective-permute-done((bf16[4,216,128]{2,1,0:T(8,128)(2,1)S(1)}, bf16[4,216,128]{2,1,0:T(8,128)(2,1)S(1)}, u32[]{:S(2)}, u32[]{:S(2)}) %collective-permute-start.14) | collective-permute-done | bytes 221216 | tf_op jit(solution)/shard_map/ppermute | solution.py:316
  38.8 0.1 second_near.1
  38.9 1.2 %collective-permute-start.16 = (bf16[2,216,128]{2,1,0:T(8,128)(2,1)S(1)}, bf16[2,216,128]{2,1,0:T(8,128)(2,1)S(1)}, u32[]{:S(2)}, u32[]{:S(2)}) collective-permute-start(bf16[2,216,128]{2,1,0:T(8,128)(2,1)S(1)} %get-tuple-element.51.refs_3_), channel_id=1, source_target_pairs={{0,4},{1,3},{2,6},{3,1},{4,0},{5,7},{6,2},{7,5},{8,12},{9,11},{10,... | collective-permute-start | bytes 331784 | tf_op jit(solution)/shard_map/ppermute | solution.py:316
  40.1 2.4 %collective-permute-done.12.refs_2_ = bf16[4,216,128]{2,1,0:T(8,128)(2,1)S(1)} collective-permute-done((bf16[4,216,128]{2,1,0:T(8,128)(2,1)S(1)}, bf16[4,216,128]{2,1,0:T(8,128)(2,1)S(1)}, u32[]{:S(2)}, u32[]{:S(2)}) %collective-permute-start.12) | collective-permute-done | bytes 221216 | tf_op jit(solution)/shard_map/ppermute | solution.py:316
  42.5 0.1 first_near.1
  42.5 0.6 %collective-permute-start.15 = (bf16[2,216,128]{2,1,0:T(8,128)(2,1)S(1)}, bf16[2,216,128]{2,1,0:T(8,128)(2,1)S(1)}, u32[]{:S(2)}, u32[]{:S(2)}) collective-permute-start(bf16[2,216,128]{2,1,0:T(8,128)(2,1)S(1)} %get-tuple-element.53.refs_3_), channel_id=1, source_target_pairs={{0,4},{1,3},{2,6},{3,1},{4,0},{5,7},{6,2},{7,5},{8,12},{9,11},{10,... | collective-permute-start | bytes 331784 | tf_op jit(solution)/shard_map/ppermute | solution.py:316
  43.1 0.6 %collective-permute-done.16.refs_2_ = bf16[2,216,128]{2,1,0:T(8,128)(2,1)S(1)} collective-permute-done((bf16[2,216,128]{2,1,0:T(8,128)(2,1)S(1)}, bf16[2,216,128]{2,1,0:T(8,128)(2,1)S(1)}, u32[]{:S(2)}, u32[]{:S(2)}) %collective-permute-start.16) | collective-permute-done | bytes 110624 | tf_op jit(solution)/shard_map/ppermute | solution.py:316
  43.7 3.6 %collective-permute-done.15.refs_2_ = bf16[2,216,128]{2,1,0:T(8,128)(2,1)S(1)} collective-permute-done((bf16[2,216,128]{2,1,0:T(8,128)(2,1)S(1)}, bf16[2,216,128]{2,1,0:T(8,128)(2,1)S(1)}, u32[]{:S(2)}, u32[]{:S(2)}) %collective-permute-start.15) | collective-permute-done | bytes 110624 | tf_op jit(solution)/shard_map/ppermute | solution.py:316
  47.4 0.4 collective-permute-start.17
  47.8 2.6 %collective-permute-start.18 = (bf16[1,216,128]{2,1,0:T(8,128)(2,1)S(1)}, bf16[1,216,128]{2,1,0:T(8,128)(2,1)S(1)}, u32[]{:S(2)}, u32[]{:S(2)}) collective-permute-start(bf16[1,216,128]{2,1,0:T(8,128)(2,1)S(1)} %get-tuple-element.55.refs_3_), channel_id=1, source_target_pairs={{0,8},{1,9},{2,10},{3,11},{4,12},{5,13},{6,14},{7,15},{8,0},{9,1},... | collective-permute-start | bytes 165896 | tf_op jit(solution)/shard_map/ppermute | solution.py:311
  50.4 2.2 %output_conv.1 = bf16[4,16,16,128]{3,2,1,0:T(8,128)(2,1)} custom-call(bf16[6,18,16,384]{3,2,1,0:T(8,128)(2,1)S(1)} %hidden_planes.1.refs_3_.refs_0_, bf16[3456,128]{1,0:T(8,128)(2,1)S(1)} %get-tuple-element.43.refs_1_, bf16[1,216,128]{2,1,0:T(8,128)(2,1)S(1)} %get-tuple-element.56.refs_2_), custom_call_target="tpu_custom_call" | custom-call | flops 1000 | tf_op jit(solution)/shard_map/output_conv/pallas_call | solution.py:31
  52.5 0.5 collective-permute-done.17.refs_1_
  53.1 1.2 %collective-permute-done.18.refs_3_ = bf16[1,216,128]{2,1,0:T(8,128)(2,1)S(1)} collective-permute-done((bf16[1,216,128]{2,1,0:T(8,128)(2,1)S(1)}, bf16[1,216,128]{2,1,0:T(8,128)(2,1)S(1)}, u32[]{:S(2)}, u32[]{:S(2)}) %collective-permute-start.18) | collective-permute-done | bytes 55328 | tf_op jit(solution)/shard_map/ppermute | solution.py:311
  54.2 0.7 %sum_last.1 = (f32[216,128]{1,0:T(8,128)}, f32[216,128]{1,0:T(8,128)}) custom-call(f32[1,216,128]{2,1,0:T(8,128)S(1)} %get-tuple-element.57.refs_0_, bf16[1,216,128]{2,1,0:T(8,128)(2,1)S(1)} %collective-permute-done.17.refs_1_, f32[1,216,128]{2,1,0:T(8,128)S(1)} %get-tuple-element.58.refs_2_, bf16[1,216,128]{2,1,0:T(8,128)(2,1)S(1)} %collective-permute-done.18.refs_3_), custom_call_target="tpu_custom_call" | custom-call | flops 1000 | tf_op jit(solution)/shard_map/sum_last/pallas_call | solution.py:31
  (4 shorter events, 0.1 us)
Async XLA Ops:
  1.5 10.3 %collective-permute-start.3 = (bf16[2,216,128]{2,1,0:T(8,128)(2,1)S(1)}, bf16[2,216,128]{2,1,0:T(8,128)(2,1)S(1)}, u32[]{:S(2)}, u32[]{:S(2)}) collective-permute-start(bf16[2,216,128]{2,1,0:T(8,128)(2,1)S(1)} %load_shards.1.refs_0_), channel_id=1, source_target_pairs={{0,8},{1,9},{2,10},{3,11},{4,12},{5,13},{6,14},{7,15},{8,0},{9,1},... | collective-permute-start | bytes 331784 | tf_op jit(solution)/shard_map/ppermute | solution.py:311
  6.7 10.0 %collective-permute-start.1 = (bf16[3,16,16,128]{3,2,1,0:T(8,128)(2,1)S(1)}, bf16[3,16,16,128]{3,2,1,0:T(8,128)(2,1)S(1)}, u32[]{:S(2)}, u32[]{:S(2)}) collective-permute-start(bf16[3,16,16,128]{3,2,1,0:T(8,128)(2,1)S(1)} %get-tuple-element.32.refs_2_), channel_id=1, source_target_pairs={{1,2},{2,1},{3,4},{4,3},{5,6},{6,5},{7,8},{8,7},{9,10},{10,9},{11,... | collective-permute-start | bytes 589832 | tf_op jit(solution)/shard_map/ppermute | solution.py:359
  7.3 9.3 %collective-permute-start = (bf16[3,16,16,128]{3,2,1,0:T(8,128)(2,1)S(1)}, bf16[3,16,16,128]{3,2,1,0:T(8,128)(2,1)S(1)}, u32[]{:S(2)}, u32[]{:S(2)}) collective-permute-start(bf16[3,16,16,128]{3,2,1,0:T(8,128)(2,1)S(1)} %get-tuple-element.35), channel_id=1, source_target_pairs={{0,1},{1,0},{2,3},{3,2},{4,5},{5,4},{6,7},{7,6},{8,9},{9,8},{10,11... | collective-permute-start | bytes 589832 | tf_op jit(solution)/shard_map/ppermute | solution.py:311
  10.3 5.3 %collective-permute-start.2 = (bf16[2,216,128]{2,1,0:T(8,128)(2,1)S(1)}, bf16[2,216,128]{2,1,0:T(8,128)(2,1)S(1)}, u32[]{:S(2)}, u32[]{:S(2)}) collective-permute-start(bf16[2,216,128]{2,1,0:T(8,128)(2,1)S(1)} %load_shards.1.refs_0_), channel_id=1, source_target_pairs={{0,4},{1,3},{2,6},{3,1},{4,0},{5,7},{6,2},{7,5},{8,12},{9,11},{10,... | collective-permute-start | bytes 331784 | tf_op jit(solution)/shard_map/ppermute | solution.py:316
  11.9 6.7 %collective-permute-start.4 = (bf16[2,216,128]{2,1,0:T(8,128)(2,1)S(1)}, bf16[2,216,128]{2,1,0:T(8,128)(2,1)S(1)}, u32[]{:S(2)}, u32[]{:S(2)}) collective-permute-start(bf16[2,216,128]{2,1,0:T(8,128)(2,1)S(1)} %collective-permute-done.3.refs_0_), channel_id=1, source_target_pairs={{0,4},{1,3},{2,6},{3,1},{4,0},{5,7},{6,2},{7,5},{8,12},{9,11},{10,... | collective-permute-start | bytes 331784 | tf_op jit(solution)/shard_map/ppermute | solution.py:316
  15.6 6.0 %collective-permute-start.5 = (bf16[4,216,128]{2,1,0:T(8,128)(2,1)S(1)}, bf16[4,216,128]{2,1,0:T(8,128)(2,1)S(1)}, u32[]{:S(2)}, u32[]{:S(2)}) collective-permute-start(bf16[4,216,128]{2,1,0:T(8,128)(2,1)S(1)} %own_and_near.1.refs_1_), channel_id=1, source_target_pairs={{0,2},{1,5},{2,0},{3,7},{4,6},{5,1},{6,4},{7,3},{8,10},{9,13},{10,... | collective-permute-start | bytes 663560 | tf_op jit(solution)/shard_map/ppermute | solution.py:316
  18.6 6.0 %collective-permute-start.6 = (bf16[4,216,128]{2,1,0:T(8,128)(2,1)S(1)}, bf16[4,216,128]{2,1,0:T(8,128)(2,1)S(1)}, u32[]{:S(2)}, u32[]{:S(2)}) collective-permute-start(bf16[4,216,128]{2,1,0:T(8,128)(2,1)S(1)} %far_and_near.1.refs_2_), channel_id=1, source_target_pairs={{0,2},{1,5},{2,0},{3,7},{4,6},{5,1},{6,4},{7,3},{8,10},{9,13},{10,... | collective-permute-start | bytes 663560 | tf_op jit(solution)/shard_map/ppermute | solution.py:316
  19.7 5.3 %collective-permute-start.7 = (bf16[4,216,128]{2,1,0:T(8,128)(2,1)S(1)}, bf16[4,216,128]{2,1,0:T(8,128)(2,1)S(1)}, u32[]{:S(2)}, u32[]{:S(2)}) collective-permute-start(bf16[4,216,128]{2,1,0:T(8,128)(2,1)S(1)} %own_and_near.1.refs_1_), channel_id=1, source_target_pairs={{0,1},{1,0},{2,3},{3,2},{4,5},{5,4},{6,7},{7,6},{8,9},{9,8},{10,11... | collective-permute-start | bytes 663560 | tf_op jit(solution)/shard_map/ppermute | solution.py:311
  20.3 4.7 %collective-permute-start.8 = (bf16[4,216,128]{2,1,0:T(8,128)(2,1)S(1)}, bf16[4,216,128]{2,1,0:T(8,128)(2,1)S(1)}, u32[]{:S(2)}, u32[]{:S(2)}) collective-permute-start(bf16[4,216,128]{2,1,0:T(8,128)(2,1)S(1)} %far_and_near.1.refs_2_), channel_id=1, source_target_pairs={{0,1},{1,0},{2,3},{3,2},{4,5},{5,4},{6,7},{7,6},{8,9},{9,8},{10,11... | collective-permute-start | bytes 663560 | tf_op jit(solution)/shard_map/ppermute | solution.py:311
  21.6 3.5 %collective-permute-start.9 = (bf16[4,216,128]{2,1,0:T(8,128)(2,1)S(1)}, bf16[4,216,128]{2,1,0:T(8,128)(2,1)S(1)}, u32[]{:S(2)}, u32[]{:S(2)}) collective-permute-start(bf16[4,216,128]{2,1,0:T(8,128)(2,1)S(1)} %collective-permute-done.5.refs_3_), channel_id=1, source_target_pairs={{0,1},{1,0},{2,3},{3,2},{4,5},{5,4},{6,7},{7,6},{8,9},{9,8},{10,11... | collective-permute-start | bytes 663560 | tf_op jit(solution)/shard_map/ppermute | solution.py:311
  24.6 1.5 %collective-permute-start.10 = (bf16[4,216,128]{2,1,0:T(8,128)(2,1)S(1)}, bf16[4,216,128]{2,1,0:T(8,128)(2,1)S(1)}, u32[]{:S(2)}, u32[]{:S(2)}) collective-permute-start(bf16[4,216,128]{2,1,0:T(8,128)(2,1)S(1)} %collective-permute-done.6.refs_4_), channel_id=1, source_target_pairs={{0,1},{1,0},{2,3},{3,2},{4,5},{5,4},{6,7},{7,6},{8,9},{9,8},{10,11... | collective-permute-start | bytes 663560 | tf_op jit(solution)/shard_map/ppermute | solution.py:311
  29.3 3.5 %collective-permute-start.13 = (bf16[8,216,128]{2,1,0:T(8,128)(2,1)S(1)}, bf16[8,216,128]{2,1,0:T(8,128)(2,1)S(1)}, u32[]{:S(2)}, u32[]{:S(2)}) collective-permute-start(bf16[8,216,128]{2,1,0:T(8,128)(2,1)S(1)} %get-tuple-element.48), channel_id=1, source_target_pairs={{0,1},{1,0},{2,3},{3,2},{4,5},{5,4},{6,7},{7,6},{8,9},{9,8},{10,11... | collective-permute-start | bytes 1327112 | tf_op jit(solution)/shard_map/ppermute | solution.py:311
  32.5 3.2 %collective-permute-start.11 = (bf16[8,216,128]{2,1,0:T(8,128)(2,1)S(1)}, bf16[8,216,128]{2,1,0:T(8,128)(2,1)S(1)}, u32[]{:S(2)}, u32[]{:S(2)}) collective-permute-start(bf16[8,216,128]{2,1,0:T(8,128)(2,1)S(1)} %get-tuple-element.44), channel_id=1, source_target_pairs={{0,1},{1,0},{2,3},{3,2},{4,5},{5,4},{6,7},{7,6},{8,9},{9,8},{10,11... | collective-permute-start | bytes 1327112 | tf_op jit(solution)/shard_map/ppermute | solution.py:311
  32.8 6.0 %collective-permute-start.14 = (bf16[4,216,128]{2,1,0:T(8,128)(2,1)S(1)}, bf16[4,216,128]{2,1,0:T(8,128)(2,1)S(1)}, u32[]{:S(2)}, u32[]{:S(2)}) collective-permute-start(bf16[4,216,128]{2,1,0:T(8,128)(2,1)S(1)} %get-tuple-element.50), channel_id=1, source_target_pairs={{0,2},{1,5},{2,0},{3,7},{4,6},{5,1},{6,4},{7,3},{8,10},{9,13},{10,... | collective-permute-start | bytes 663560 | tf_op jit(solution)/shard_map/ppermute | solution.py:316
  35.8 6.7 %collective-permute-start.12 = (bf16[4,216,128]{2,1,0:T(8,128)(2,1)S(1)}, bf16[4,216,128]{2,1,0:T(8,128)(2,1)S(1)}, u32[]{:S(2)}, u32[]{:S(2)}) collective-permute-start(bf16[4,216,128]{2,1,0:T(8,128)(2,1)S(1)} %get-tuple-element.46.refs_3_), channel_id=1, source_target_pairs={{0,2},{1,5},{2,0},{3,7},{4,6},{5,1},{6,4},{7,3},{8,10},{9,13},{10,... | collective-permute-start | bytes 663560 | tf_op jit(solution)/shard_map/ppermute | solution.py:316
  38.9 4.8 %collective-permute-start.16 = (bf16[2,216,128]{2,1,0:T(8,128)(2,1)S(1)}, bf16[2,216,128]{2,1,0:T(8,128)(2,1)S(1)}, u32[]{:S(2)}, u32[]{:S(2)}) collective-permute-start(bf16[2,216,128]{2,1,0:T(8,128)(2,1)S(1)} %get-tuple-element.51.refs_3_), channel_id=1, source_target_pairs={{0,4},{1,3},{2,6},{3,1},{4,0},{5,7},{6,2},{7,5},{8,12},{9,11},{10,... | collective-permute-start | bytes 331784 | tf_op jit(solution)/shard_map/ppermute | solution.py:316
  42.5 4.8 %collective-permute-start.15 = (bf16[2,216,128]{2,1,0:T(8,128)(2,1)S(1)}, bf16[2,216,128]{2,1,0:T(8,128)(2,1)S(1)}, u32[]{:S(2)}, u32[]{:S(2)}) collective-permute-start(bf16[2,216,128]{2,1,0:T(8,128)(2,1)S(1)} %get-tuple-element.53.refs_3_), channel_id=1, source_target_pairs={{0,4},{1,3},{2,6},{3,1},{4,0},{5,7},{6,2},{7,5},{8,12},{9,11},{10,... | collective-permute-start | bytes 331784 | tf_op jit(solution)/shard_map/ppermute | solution.py:316
  47.4 5.7 %collective-permute-start.17 = (bf16[1,216,128]{2,1,0:T(8,128)(2,1)S(1)}, bf16[1,216,128]{2,1,0:T(8,128)(2,1)S(1)}, u32[]{:S(2)}, u32[]{:S(2)}) collective-permute-start(bf16[1,216,128]{2,1,0:T(8,128)(2,1)S(1)} %get-tuple-element.56.refs_2_), channel_id=1, source_target_pairs={{0,8},{1,9},{2,10},{3,11},{4,12},{5,13},{6,14},{7,15},{8,0},{9,1},... | collective-permute-start | bytes 165896 | tf_op jit(solution)/shard_map/ppermute | solution.py:311
  47.8 6.5 %collective-permute-start.18 = (bf16[1,216,128]{2,1,0:T(8,128)(2,1)S(1)}, bf16[1,216,128]{2,1,0:T(8,128)(2,1)S(1)}, u32[]{:S(2)}, u32[]{:S(2)}) collective-permute-start(bf16[1,216,128]{2,1,0:T(8,128)(2,1)S(1)} %get-tuple-element.55.refs_3_), channel_id=1, source_target_pairs={{0,8},{1,9},{2,10},{3,11},{4,12},{5,13},{6,14},{7,15},{8,0},{9,1},... | collective-permute-start | bytes 165896 | tf_op jit(solution)/shard_map/ppermute | solution.py:311

commit v4 on v3

--- a/solution.py
+++ b/solution.py
@@ -274,37 +274,43 @@
     out_ref[...] = out.astype(BF16).reshape(out_ref.shape)
 
 
-def sum_half(bit, place, keep_ref, got_ref, send_ref, own_ref):
-    for at in range(own_ref.shape[0]):
-        mine, other = place(at, bit), place(at, 1 - bit)
-        own_ref[at] = keep_ref[mine] + got_ref[mine].astype(F32)
-        send_ref[at] = (keep_ref[other] + got_ref[other].astype(F32)).astype(BF16)
+def scatter_bits(me):
+    low = me % 2 == 0
+    y, z = (me // 2) % 2, (me // 4) % 2
+    return low, jnp.where(low, y, z), jnp.where(low, z, y), me // 8
 
 
 def sum_pair_kernel(me_ref, *refs):
-    me = me_ref[0]
-    core = me % 2
-    bit = jnp.where(core == 0, (me // 2) % 2, (me // 4) % 2)
-
-    def place(at, value):
-        return jnp.where(core == 0, 2 * at + value, at // 2 * 4 + 2 * value + at % 2)
-
-    sum_half(bit, place, *refs)
-
-
-def sum_near_kernel(me_ref, *refs):
-    me = me_ref[0]
-    bit = jnp.where(me % 2 == 0, (me // 4) % 2, (me // 2) % 2)
-    sum_half(bit, lambda at, value: 2 * at + value, *refs)
-
-
-def sum_far_kernel(me_ref, *refs):
-    sum_half(me_ref[0] // 8, lambda at, value: value, *refs)
-
-
-def sum_last_kernel(keep_first, got_first, keep_second, got_second, first_ref, second_ref):
-    first_ref[...] = keep_first[0] + got_first[0].astype(F32)
-    second_ref[...] = keep_second[0] + got_second[0].astype(F32)
+    keep_refs, got_refs, (far_send, send, far_own, own) = refs[:2], refs[2:4], refs[4:]
+    low, first, _, last = scatter_bits(me_ref[0])
+    for bank, (keep_ref, got_ref) in enumerate(zip(keep_refs, got_refs)):
+        for second in range(2):
+            at = 2 * bank + second
+            for side, send_ref, own_ref in ((1 - last, far_send, far_own), (last, send, own)):
+
+                def total(bit):
+                    k = 4 * side + jnp.where(low, 2 * second + bit, 2 * bit + second)
+                    return keep_ref[k] + got_ref[k].astype(F32)
+
+                own_ref[at] = total(first)
+                send_ref[at] = total(1 - first).astype(BF16)
+
+
+def sum_near_kernel(me_ref, own_ref, got_ref, send_ref, keep_ref):
+    _, _, second, _ = scatter_bits(me_ref[0])
+    for bank in range(2):
+        mine, other = 2 * bank + second, 2 * bank + 1 - second
+        keep_ref[bank] = own_ref[mine] + got_ref[mine].astype(F32)
+        send_ref[bank] = (own_ref[other] + got_ref[other].astype(F32)).astype(BF16)
+
+
+def sum_far_kernel(keep_ref, got_ref, send_ref):
+    send_ref[...] = (keep_ref[...] + got_ref[...].astype(F32)).astype(BF16)
+
+
+def sum_last_kernel(keep_ref, near_ref, far_ref, first_ref, second_ref):
+    for bank, ref in enumerate((first_ref, second_ref)):
+        ref[...] = keep_ref[bank] + near_ref[bank].astype(F32) + far_ref[bank].astype(F32)
 
 
 def swap(value, count, distance):
@@ -320,12 +326,6 @@
     depth = sum(part.shape[0] if part.ndim == 3 else 1 for part in parts)
     out = like((depth, *parts[0].shape[-2:]), BF16)
     return local_call(join_kernel, name, [out], parts, wait_for=wait_for)[0]
-
-
-def summed(kernel, name, me, keep, got, wait_for=()):
-    shape = (keep.shape[0] // 2, *keep.shape[1:])
-    outs = [like(shape, BF16), like(shape, F32)]
-    return local_call(kernel, name, outs, [me, keep, got], scalars=1, wait_for=wait_for)
 
 
 def shards(count, features, filters_first, filters_second, cotangent):
@@ -408,49 +408,58 @@
         scratch=[total],
         scalars=1,
     )
-    wait_for = []
+    wait_for = [keep_first]
     if direct:
-        got = swap(send_second, count, 1)
-        send_second, keep_second = summed(sum_pair_kernel, "second_pair", me, keep_second, got)
-        got_second = swap_mixed(send_second, count, 2, 4)
-        got = swap(send_first, count, 1)
+        got_second = swap(send_second, count, 1)
+        wait_for.append(got_second)
     (xh,) = local_call(
         functools.partial(hidden_kernel, count),
         "hidden_planes",
         [like((planes + 2, height + 2, width, 3 * channels), BF16)],
         [me, xf, bank, hidden],
         scalars=1,
-        wait_for=[keep_first],
-    )
+        wait_for=wait_for,
+    )
+    wait_for = []
     if direct:
-        send_first, keep_first = summed(sum_pair_kernel, "first_pair", me, keep_first, got, [xh])
-        got_first = swap_mixed(send_first, count, 2, 4)
-        send_second, keep_second = summed(
-            sum_near_kernel, "second_near", me, keep_second, got_second, [send_first]
-        )
-        got_second = swap_mixed(send_second, count, 4, 2)
-        send_first, keep_first = summed(
-            sum_near_kernel, "first_near", me, keep_first, got_first, [send_second]
-        )
-        got_first = swap_mixed(send_first, count, 4, 2)
-        send_second, keep_second = summed(
-            sum_far_kernel, "second_far", me, keep_second, got_second, [send_first]
-        )
-        got_second = swap(send_second, count, 8)
-        send_first, keep_first = summed(
-            sum_far_kernel, "first_far", me, keep_first, got_first, [send_second]
-        )
-        wait_for = [send_first]
+        blocks = [like((4, rows, channels), BF16)] * 2 + [like((4, rows, channels), F32)] * 2
+        far_send, send, far_own, own = local_call(
+            sum_pair_kernel,
+            "sum_pair",
+            blocks,
+            [
+                me,
+                keep_first,
+                keep_second,
+                swap(send_first, count, 1),
+                got_second,
+            ],
+            scalars=1,
+            wait_for=[xh],
+        )
+        halves = [like((2, rows, channels), BF16), like((2, rows, channels), F32)]
+        far_got = swap_mixed(far_send, count, 2, 4)
+        far_send, far_keep = local_call(
+            sum_near_kernel, "far_near", halves, [me, far_own, far_got], scalars=1
+        )
+        far_got = swap_mixed(far_send, count, 4, 2)
+        got = swap_mixed(send, count, 2, 4)
+        send, keep = local_call(
+            sum_near_kernel, "own_near", halves, [me, own, got], scalars=1, wait_for=[far_send]
+        )
+        got = swap_mixed(send, count, 4, 2)
+        (far_send,) = local_call(
+            sum_far_kernel, "far_last", halves[:1], [far_keep, far_got]
+        )
+        far_got = swap(far_send, count, 8)
+        wait_for = [far_send]
     (output,) = local_call(
         output_kernel, "output_conv", [like(features.shape, BF16)], [xh, bank_second], wait_for=wait_for
     )
     if direct:
         out = like((rows, channels), F32)
         grad_first, grad_second = local_call(
-            sum_last_kernel,
-            "sum_last",
-            [out, out],
-            [keep_first, swap(send_first, count, 8), keep_second, got_second],
+            sum_last_kernel, "sum_last", [out, out], [keep, got, far_got]
         )
     else:
         grad_first, grad_second = (

time: 55.2 us -> 53.4 us (0.967)
  starting transfers between devices: 20.7 us -> 19.1 us
    ppermute x10 -> x9, starting transfers between devices: 11.9 us -> 6.69 us  [swap(): lax.ppermute(value, 'slab', [(i, i ^ distance) for i in range(count)])]
    ppermute x8, starting transfers between devices: 8.12 us -> 11.8 us  [swap_mixed(): return lax.ppermute(value, 'slab', pairs)]
    ppermute x8, waiting for transfers between devices: 15.2 us -> 12.9 us  [swap_mixed(): return lax.ppermute(value, 'slab', pairs)]
    ppermute x10 -> x9, waiting for transfers between devices: 2.82 us -> 5.03 us  [swap(): lax.ppermute(value, 'slab', [(i, i ^ distance) for i in range(count)])]
    pallas_call x14 -> x12, Pallas kernels: 12.5 us -> 12.4 us  [local_call(): pl.pallas_call(body, out_shape=list(outs), in_specs=[pl.BlockSpec(memory_...]
  transfers between devices with their start and end apart: 19 -> 18, of which waited for: 10 -> 10; matrix products, arithmetic and copies ran while one was open for 0% -> 0% of each run, Pallas kernels for 19% -> 20%
where the time goes in v4:
time: 53.4 us; the launch traced here: 53.1 us
  starting transfers between devices  19.1 us (36%)
  waiting for transfers between devices  17.9 us (34%)
  Pallas kernels  15.4 us (29%)
  between operations  0.76 us (1%)
    ppermute x8, waiting for transfers between devices, swap_mixed(): return lax.ppermute(value, 'slab', pairs)  12.9 us
    pallas_call x12, Pallas kernels, local_call(): pl.pallas_call(body, out_shape=list(outs), in_specs=[pl.BlockSpec(memory_...  12.4 us
    ppermute x8, starting transfers between devices, swap_mixed(): return lax.ppermute(value, 'slab', pairs)  11.8 us
    ppermute x9, starting transfers between devices, swap(): lax.ppermute(value, 'slab', [(i, i ^ distance) for i in range(count)])  6.69 us
    ppermute x9, waiting for transfers between devices, swap(): lax.ppermute(value, 'slab', [(i, i ^ distance) for i in range(count)])  5.03 us
    pallas_call x3, Pallas kernels, from_hbm(): pl.pallas_call(body, out_shape=outs, in_specs=[pl.BlockSpec(memory_space=...  2.97 us
  transfers between devices with their start and end apart: 18, of which 10 were waited for; matrix products, arithmetic and copies ran while one was open for 0% of the time, Pallas kernels for 20%

profile of v4, /device:TPU:0, one launch (start us, length us, event | category | flops | bytes accessed | tf_op | source)
XLA Modules:
  0.0 53.1 jit_solution(17382524119507084160)
XLA Ops:
  0.6 0.9 %load_shards.1.refs_0_ = bf16[2,216,128]{2,1,0:T(8,128)(2,1)S(1)} custom-call(bf16[216,128]{1,0:T(8,128)(2,1)} %refs_0_.3, bf16[216,128]{1,0:T(8,128)(2,1)} %refs_1_.5), custom_call_target="tpu_custom_call" | custom-call | flops 1000 | tf_op jit(solution)/shard_map/load_shards/pallas_call | solution.py:120
  1.5 4.1 %collective-permute-start.3 = (bf16[2,216,128]{2,1,0:T(8,128)(2,1)S(1)}, bf16[2,216,128]{2,1,0:T(8,128)(2,1)S(1)}, u32[]{:S(2)}, u32[]{:S(2)}) collective-permute-start(bf16[2,216,128]{2,1,0:T(8,128)(2,1)S(1)} %load_shards.1.refs_0_), channel_id=1, source_target_pairs={{0,8},{1,9},{2,10},{3,11},{4,12},{5,13},{6,14},{7,15},{8,0},{9,1},... | collective-permute-start | bytes 331784 | tf_op jit(solution)/shard_map/ppermute | solution.py:317
  5.6 1.0 %edges.1 = (bf16[3,16,16,128]{3,2,1,0:T(8,128)(2,1)S(1)}, bf16[3,16,16,128]{3,2,1,0:T(8,128)(2,1)S(1)}) custom-call(s32[1]{0:T(128)} %bitcast.refs_0_, bf16[4,16,16,128]{3,2,1,0:T(8,128)(2,1)} %refs_0_.2, bf16[4,16,16,128]{3,2,1,0:T(8,128)(2,1)} %refs_1_.4), custom_call_target="tpu_custom_call" | custom-call | flops 1000 | tf_op jit(solution)/shard_map/edges/pallas_call | solution.py:120
  6.7 0.1 collective-permute-start
  6.7 0.7 %collective-permute-start.1 = (bf16[3,16,16,128]{3,2,1,0:T(8,128)(2,1)S(1)}, bf16[3,16,16,128]{3,2,1,0:T(8,128)(2,1)S(1)}, u32[]{:S(2)}, u32[]{:S(2)}) collective-permute-start(bf16[3,16,16,128]{3,2,1,0:T(8,128)(2,1)S(1)} %get-tuple-element.28.refs_2_), channel_id=1, source_target_pairs={{1,2},{2,1},{3,4},{4,3},{5,6},{6,5},{7,8},{8,7},{9,10},{10,9},{11,... | collective-permute-start | bytes 589832 | tf_op jit(solution)/shard_map/ppermute | solution.py:359
  7.4 4.4 %collective-permute-start.2 = (bf16[2,216,128]{2,1,0:T(8,128)(2,1)S(1)}, bf16[2,216,128]{2,1,0:T(8,128)(2,1)S(1)}, u32[]{:S(2)}, u32[]{:S(2)}) collective-permute-start(bf16[2,216,128]{2,1,0:T(8,128)(2,1)S(1)} %load_shards.1.refs_0_), channel_id=1, source_target_pairs={{0,4},{1,3},{2,6},{3,1},{4,0},{5,7},{6,2},{7,5},{8,12},{9,11},{10,... | collective-permute-start | bytes 331784 | tf_op jit(solution)/shard_map/ppermute | solution.py:322
  11.8 0.0 collective-permute-done.3.refs_0_
  11.8 0.1 collective-permute-start.4
  11.9 1.1 %load.1 = (bf16[4,16,16,128]{3,2,1,0:T(8,128)(2,1)S(1)}, bf16[4,16,16,128]{3,2,1,0:T(8,128)(2,1)S(1)}) custom-call(bf16[4,16,16,128]{3,2,1,0:T(8,128)(2,1)} %refs_0_.2, bf16[4,16,16,128]{3,2,1,0:T(8,128)(2,1)} %refs_1_.4, bf16[3,16,16,128]{3,2,1,0:T(8,128)(2,1)S(1)} %get-tuple-element.28.refs_2_), custom_call_target="tpu_custom_call" | custom-call | flops 1000 | tf_op jit(solution)/shard_map/load/pallas_call | solution.py:120
  13.0 3.6 %collective-permute-done.2.refs_1_ = bf16[2,216,128]{2,1,0:T(8,128)(2,1)S(1)} collective-permute-done((bf16[2,216,128]{2,1,0:T(8,128)(2,1)S(1)}, bf16[2,216,128]{2,1,0:T(8,128)(2,1)S(1)}, u32[]{:S(2)}, u32[]{:S(2)}) %collective-permute-start.2) | collective-permute-done | bytes 110624 | tf_op jit(solution)/shard_map/ppermute | solution.py:322
  16.6 0.1 collective-permute-start.5
  16.7 0.0 collective-permute-done.refs_3_
  16.7 0.0 collective-permute-done.1.refs_4_
  16.7 1.9 %shifted_planes.1 = (bf16[8,18,16,384]{3,2,1,0:T(8,128)(2,1)S(1)}, bf16[6,18,16,384]{3,2,1,0:T(8,128)(2,1)S(1)}, bf16[6,9,128,256]{3,2,1,0:T(8,128)(2,1)S(1)}) custom-call(s32[1]{0:T(128)} %bitcast.refs_0_, bf16[4,16,16,128]{3,2,1,0:T(8,128)(2,1)S(1)} %get-tuple-element.29.refs_1_, bf16[4,16,16,128]{3,2,1,0:T(8,128)(2,1)S(1)} %get-tuple-element.30.refs_2_, ...), custom_call_target="tpu_custom_call" | custom-call | flops 1000 | tf_op jit(solution)/shard_map/shifted_planes/pallas_call | solution.py:31
  18.6 0.0 collective-permute-done.4.refs_1_
  18.7 2.1 %collective-permute-start.6 = (bf16[4,216,128]{2,1,0:T(8,128)(2,1)S(1)}, bf16[4,216,128]{2,1,0:T(8,128)(2,1)S(1)}, u32[]{:S(2)}, u32[]{:S(2)}) collective-permute-start(bf16[4,216,128]{2,1,0:T(8,128)(2,1)S(1)} %far_and_near.1.refs_2_), channel_id=1, source_target_pairs={{0,2},{1,5},{2,0},{3,7},{4,6},{5,1},{6,4},{7,3},{8,10},{9,13},{10,... | collective-permute-start | bytes 663560 | tf_op jit(solution)/shard_map/ppermute | solution.py:322
  20.7 0.7 %collective-permute-start.7 = (bf16[4,216,128]{2,1,0:T(8,128)(2,1)S(1)}, bf16[4,216,128]{2,1,0:T(8,128)(2,1)S(1)}, u32[]{:S(2)}, u32[]{:S(2)}) collective-permute-start(bf16[4,216,128]{2,1,0:T(8,128)(2,1)S(1)} %own_and_near.1.refs_1_), channel_id=1, source_target_pairs={{0,1},{1,0},{2,3},{3,2},{4,5},{5,4},{6,7},{7,6},{8,9},{9,8},{10,11... | collective-permute-start | bytes 663560 | tf_op jit(solution)/shard_map/ppermute | solution.py:317
  21.4 0.0 collective-permute-start.8
  21.4 1.2 %collective-permute-done.5.refs_3_ = bf16[4,216,128]{2,1,0:T(8,128)(2,1)S(1)} collective-permute-done((bf16[4,216,128]{2,1,0:T(8,128)(2,1)S(1)}, bf16[4,216,128]{2,1,0:T(8,128)(2,1)S(1)}, u32[]{:S(2)}, u32[]{:S(2)}) %collective-permute-start.5) | collective-permute-done | bytes 221216 | tf_op jit(solution)/shard_map/ppermute | solution.py:322
  22.6 0.0 collective-permute-start.9
  22.6 2.4 %collective-permute-done.6.refs_4_ = bf16[4,216,128]{2,1,0:T(8,128)(2,1)S(1)} collective-permute-done((bf16[4,216,128]{2,1,0:T(8,128)(2,1)S(1)}, bf16[4,216,128]{2,1,0:T(8,128)(2,1)S(1)}, u32[]{:S(2)}, u32[]{:S(2)}) %collective-permute-start.6) | collective-permute-done | bytes 221216 | tf_op jit(solution)/shard_map/ppermute | solution.py:322
  25.0 0.1 collective-permute-start.10
  25.1 0.0 collective-permute-done.7.refs_5_
  25.1 0.0 collective-permute-done.8.refs_6_
  25.1 0.0 collective-permute-done.9.refs_7_
  25.1 1.3 %collective-permute-done.10.refs_8_ = bf16[4,216,128]{2,1,0:T(8,128)(2,1)S(1)} collective-permute-done((bf16[4,216,128]{2,1,0:T(8,128)(2,1)S(1)}, bf16[4,216,128]{2,1,0:T(8,128)(2,1)S(1)}, u32[]{:S(2)}, u32[]{:S(2)}) %collective-permute-start.10) | collective-permute-done | bytes 221216 | tf_op jit(solution)/shard_map/ppermute | solution.py:317
  26.4 3.1 %hidden_and_second_grad.1 = (bf16[3456,128]{1,0:T(8,128)(2,1)S(1)}, bf16[4,16,16,128]{3,2,1,0:T(8,128)(2,1)S(1)}, f32[128,1024]{1,0:T(8,128)S(1)}, bf16[8,216,128]{2,1,0:T(8,128)(2,1)S(1)}, f32[8,216,128]{2,1,0:T(8,128)S(1)}) custom-call(s32[1]{0:T(128)} %bitcast.refs_0_, bf16[4,216,128]{2,1,0:T(8,128)(2,1)S(1)} %own_and_near.1.refs_1_, ...), custom_call_target="tpu_custom_call" | custom-call | flops 1000 | tf_op jit(solution)/shard_map/hidden_and_second_grad/pallas_call | solution.py:31
  29.6 0.2 collective-permute-start.11
  29.8 2.8 %first_grad.1 = (bf16[3456,128]{1,0:T(8,128)(2,1)S(1)}, bf16[8,216,128]{2,1,0:T(8,128)(2,1)S(1)}, f32[8,216,128]{2,1,0:T(8,128)S(1)}) custom-call(s32[1]{0:T(128)} %bitcast.refs_0_, bf16[4,216,128]{2,1,0:T(8,128)(2,1)S(1)} %own_and_near.1.refs_1_, bf16[4,216,128]{2,1,0:T(8,128)(2,1)S(1)} %far_and_near.1.refs_2_, ...), custom_call_target="tpu_custom_call" | custom-call | flops 1000 | tf_op jit(solution)/shard_map/first_grad/pallas_call | solution.py:31
  32.6 0.5 collective-permute-start.12
  33.0 0.0 collective-permute-done.11.refs_5_.refs_4_
  33.0 1.3 %hidden_planes.1.refs_5_.refs_0_ = bf16[6,18,16,384]{3,2,1,0:T(8,128)(2,1)S(1)} custom-call(s32[1]{0:T(128)} %bitcast.refs_0_, bf16[8,18,16,384]{3,2,1,0:T(8,128)(2,1)S(1)} %get-tuple-element.32.refs_2_.refs_9_.refs_1_, bf16[3456,128]{1,0:T(8,128)(2,1)S(1)} %get-tuple-element.34.refs_2_, bf16[4,16,16,128]{3,2,1,0:T(8,128)(2,1)S(1)} %get-tuple-element.35.refs_3_, ...), custom_call_target="tpu_custom_call" | custom-call | flops 1000 | tf_op jit(solution)/shard_map/hidden_planes/pallas_call | solution.py:31
  34.4 0.1 collective-permute-done.12.refs_3_
  34.5 0.2 sum_pair.1
  34.6 1.8 %collective-permute-start.13 = (bf16[4,216,128]{2,1,0:T(8,128)(2,1)S(1)}, bf16[4,216,128]{2,1,0:T(8,128)(2,1)S(1)}, u32[]{:S(2)}, u32[]{:S(2)}) collective-permute-start(bf16[4,216,128]{2,1,0:T(8,128)(2,1)S(1)} %get-tuple-element.44), channel_id=1, source_target_pairs={{0,2},{1,5},{2,0},{3,7},{4,6},{5,1},{6,4},{7,3},{8,10},{9,13},{10,... | collective-permute-start | bytes 663560 | tf_op jit(solution)/shard_map/ppermute | solution.py:322
  36.4 0.3 collective-permute-start.15
  36.7 3.9 %collective-permute-done.13.refs_2_ = bf16[4,216,128]{2,1,0:T(8,128)(2,1)S(1)} collective-permute-done((bf16[4,216,128]{2,1,0:T(8,128)(2,1)S(1)}, bf16[4,216,128]{2,1,0:T(8,128)(2,1)S(1)}, u32[]{:S(2)}, u32[]{:S(2)}) %collective-permute-start.13) | collective-permute-done | bytes 221216 | tf_op jit(solution)/shard_map/ppermute | solution.py:322
  40.7 1.4 %collective-permute-start.14 = (bf16[2,216,128]{2,1,0:T(8,128)(2,1)S(1)}, bf16[2,216,128]{2,1,0:T(8,128)(2,1)S(1)}, u32[]{:S(2)}, u32[]{:S(2)}) collective-permute-start(bf16[2,216,128]{2,1,0:T(8,128)(2,1)S(1)} %get-tuple-element.46.refs_3_), channel_id=1, source_target_pairs={{0,4},{1,3},{2,6},{3,1},{4,0},{5,7},{6,2},{7,5},{8,12},{9,11},{10,... | collective-permute-start | bytes 331784 | tf_op jit(solution)/shard_map/ppermute | solution.py:322
  42.1 1.0 %collective-permute-done.15.refs_2_ = bf16[4,216,128]{2,1,0:T(8,128)(2,1)S(1)} collective-permute-done((bf16[4,216,128]{2,1,0:T(8,128)(2,1)S(1)}, bf16[4,216,128]{2,1,0:T(8,128)(2,1)S(1)}, u32[]{:S(2)}, u32[]{:S(2)}) %collective-permute-start.15) | collective-permute-done | bytes 221216 | tf_op jit(solution)/shard_map/ppermute | solution.py:322
  43.1 0.1 own_near.1
  43.2 1.6 %collective-permute-start.16 = (bf16[2,216,128]{2,1,0:T(8,128)(2,1)S(1)}, bf16[2,216,128]{2,1,0:T(8,128)(2,1)S(1)}, u32[]{:S(2)}, u32[]{:S(2)}) collective-permute-start(bf16[2,216,128]{2,1,0:T(8,128)(2,1)S(1)} %get-tuple-element.50), channel_id=1, source_target_pairs={{0,4},{1,3},{2,6},{3,1},{4,0},{5,7},{6,2},{7,5},{8,12},{9,11},{10,... | collective-permute-start | bytes 331784 | tf_op jit(solution)/shard_map/ppermute | solution.py:322
  44.8 0.7 %collective-permute-done.14.refs_1_ = bf16[2,216,128]{2,1,0:T(8,128)(2,1)S(1)} collective-permute-done((bf16[2,216,128]{2,1,0:T(8,128)(2,1)S(1)}, bf16[2,216,128]{2,1,0:T(8,128)(2,1)S(1)}, u32[]{:S(2)}, u32[]{:S(2)}) %collective-permute-start.14) | collective-permute-done | bytes 110624 | tf_op jit(solution)/shard_map/ppermute | solution.py:322
  45.5 1.0 %collective-permute-start.17 = (bf16[2,216,128]{2,1,0:T(8,128)(2,1)S(1)}, bf16[2,216,128]{2,1,0:T(8,128)(2,1)S(1)}, u32[]{:S(2)}, u32[]{:S(2)}) collective-permute-start(bf16[2,216,128]{2,1,0:T(8,128)(2,1)S(1)} %far_last.1.refs_2_), channel_id=1, source_target_pairs={{0,8},{1,9},{2,10},{3,11},{4,12},{5,13},{6,14},{7,15},{8,0},{9,1},... | collective-permute-start | bytes 331784 | tf_op jit(solution)/shard_map/ppermute | solution.py:317
  46.5 2.2 %output_conv.1 = bf16[4,16,16,128]{3,2,1,0:T(8,128)(2,1)} custom-call(bf16[6,18,16,384]{3,2,1,0:T(8,128)(2,1)S(1)} %hidden_planes.1.refs_5_.refs_0_, bf16[3456,128]{1,0:T(8,128)(2,1)S(1)} %get-tuple-element.40.refs_1_, bf16[2,216,128]{2,1,0:T(8,128)(2,1)S(1)} %far_last.1.refs_2_), custom_call_target="tpu_custom_call" | custom-call | flops 1000 | tf_op jit(solution)/shard_map/output_conv/pallas_call | solution.py:31
  48.7 0.1 collective-permute-done.16.refs_1_
  48.8 3.6 %collective-permute-done.17.refs_2_ = bf16[2,216,128]{2,1,0:T(8,128)(2,1)S(1)} collective-permute-done((bf16[2,216,128]{2,1,0:T(8,128)(2,1)S(1)}, bf16[2,216,128]{2,1,0:T(8,128)(2,1)S(1)}, u32[]{:S(2)}, u32[]{:S(2)}) %collective-permute-start.17) | collective-permute-done | bytes 110624 | tf_op jit(solution)/shard_map/ppermute | solution.py:317
  52.4 0.7 %sum_last.1 = (f32[216,128]{1,0:T(8,128)}, f32[216,128]{1,0:T(8,128)}) custom-call(f32[2,216,128]{2,1,0:T(8,128)S(1)} %get-tuple-element.49.refs_0_, bf16[2,216,128]{2,1,0:T(8,128)(2,1)S(1)} %collective-permute-done.16.refs_1_, bf16[2,216,128]{2,1,0:T(8,128)(2,1)S(1)} %collective-permute-done.17.refs_2_), custom_call_target="tpu_custom_call" | custom-call | flops 1000 | tf_op jit(solution)/shard_map/sum_last/pallas_call | solution.py:31
  (4 shorter events, 0.1 us)
Async XLA Ops:
  1.5 10.3 %collective-permute-start.3 = (bf16[2,216,128]{2,1,0:T(8,128)(2,1)S(1)}, bf16[2,216,128]{2,1,0:T(8,128)(2,1)S(1)}, u32[]{:S(2)}, u32[]{:S(2)}) collective-permute-start(bf16[2,216,128]{2,1,0:T(8,128)(2,1)S(1)} %load_shards.1.refs_0_), channel_id=1, source_target_pairs={{0,8},{1,9},{2,10},{3,11},{4,12},{5,13},{6,14},{7,15},{8,0},{9,1},... | collective-permute-start | bytes 331784 | tf_op jit(solution)/shard_map/ppermute | solution.py:317
  6.7 10.0 %collective-permute-start = (bf16[3,16,16,128]{3,2,1,0:T(8,128)(2,1)S(1)}, bf16[3,16,16,128]{3,2,1,0:T(8,128)(2,1)S(1)}, u32[]{:S(2)}, u32[]{:S(2)}) collective-permute-start(bf16[3,16,16,128]{3,2,1,0:T(8,128)(2,1)S(1)} %get-tuple-element.31), channel_id=1, source_target_pairs={{0,1},{1,0},{2,3},{3,2},{4,5},{5,4},{6,7},{7,6},{8,9},{9,8},{10,11... | collective-permute-start | bytes 589832 | tf_op jit(solution)/shard_map/ppermute | solution.py:317
  6.7 9.9 %collective-permute-start.1 = (bf16[3,16,16,128]{3,2,1,0:T(8,128)(2,1)S(1)}, bf16[3,16,16,128]{3,2,1,0:T(8,128)(2,1)S(1)}, u32[]{:S(2)}, u32[]{:S(2)}) collective-permute-start(bf16[3,16,16,128]{3,2,1,0:T(8,128)(2,1)S(1)} %get-tuple-element.28.refs_2_), channel_id=1, source_target_pairs={{1,2},{2,1},{3,4},{4,3},{5,6},{6,5},{7,8},{8,7},{9,10},{10,9},{11,... | collective-permute-start | bytes 589832 | tf_op jit(solution)/shard_map/ppermute | solution.py:359
  7.4 9.2 %collective-permute-start.2 = (bf16[2,216,128]{2,1,0:T(8,128)(2,1)S(1)}, bf16[2,216,128]{2,1,0:T(8,128)(2,1)S(1)}, u32[]{:S(2)}, u32[]{:S(2)}) collective-permute-start(bf16[2,216,128]{2,1,0:T(8,128)(2,1)S(1)} %load_shards.1.refs_0_), channel_id=1, source_target_pairs={{0,4},{1,3},{2,6},{3,1},{4,0},{5,7},{6,2},{7,5},{8,12},{9,11},{10,... | collective-permute-start | bytes 331784 | tf_op jit(solution)/shard_map/ppermute | solution.py:322
  11.8 6.8 %collective-permute-start.4 = (bf16[2,216,128]{2,1,0:T(8,128)(2,1)S(1)}, bf16[2,216,128]{2,1,0:T(8,128)(2,1)S(1)}, u32[]{:S(2)}, u32[]{:S(2)}) collective-permute-start(bf16[2,216,128]{2,1,0:T(8,128)(2,1)S(1)} %collective-permute-done.3.refs_0_), channel_id=1, source_target_pairs={{0,4},{1,3},{2,6},{3,1},{4,0},{5,7},{6,2},{7,5},{8,12},{9,11},{10,... | collective-permute-start | bytes 331784 | tf_op jit(solution)/shard_map/ppermute | solution.py:322
  16.6 6.0 %collective-permute-start.5 = (bf16[4,216,128]{2,1,0:T(8,128)(2,1)S(1)}, bf16[4,216,128]{2,1,0:T(8,128)(2,1)S(1)}, u32[]{:S(2)}, u32[]{:S(2)}) collective-permute-start(bf16[4,216,128]{2,1,0:T(8,128)(2,1)S(1)} %own_and_near.1.refs_1_), channel_id=1, source_target_pairs={{0,2},{1,5},{2,0},{3,7},{4,6},{5,1},{6,4},{7,3},{8,10},{9,13},{10,... | collective-permute-start | bytes 663560 | tf_op jit(solution)/shard_map/ppermute | solution.py:322
  18.7 6.3 %collective-permute-start.6 = (bf16[4,216,128]{2,1,0:T(8,128)(2,1)S(1)}, bf16[4,216,128]{2,1,0:T(8,128)(2,1)S(1)}, u32[]{:S(2)}, u32[]{:S(2)}) collective-permute-start(bf16[4,216,128]{2,1,0:T(8,128)(2,1)S(1)} %far_and_near.1.refs_2_), channel_id=1, source_target_pairs={{0,2},{1,5},{2,0},{3,7},{4,6},{5,1},{6,4},{7,3},{8,10},{9,13},{10,... | collective-permute-start | bytes 663560 | tf_op jit(solution)/shard_map/ppermute | solution.py:322
  20.7 4.4 %collective-permute-start.7 = (bf16[4,216,128]{2,1,0:T(8,128)(2,1)S(1)}, bf16[4,216,128]{2,1,0:T(8,128)(2,1)S(1)}, u32[]{:S(2)}, u32[]{:S(2)}) collective-permute-start(bf16[4,216,128]{2,1,0:T(8,128)(2,1)S(1)} %own_and_near.1.refs_1_), channel_id=1, source_target_pairs={{0,1},{1,0},{2,3},{3,2},{4,5},{5,4},{6,7},{7,6},{8,9},{9,8},{10,11... | collective-permute-start | bytes 663560 | tf_op jit(solution)/shard_map/ppermute | solution.py:317
  21.4 3.7 %collective-permute-start.8 = (bf16[4,216,128]{2,1,0:T(8,128)(2,1)S(1)}, bf16[4,216,128]{2,1,0:T(8,128)(2,1)S(1)}, u32[]{:S(2)}, u32[]{:S(2)}) collective-permute-start(bf16[4,216,128]{2,1,0:T(8,128)(2,1)S(1)} %far_and_near.1.refs_2_), channel_id=1, source_target_pairs={{0,1},{1,0},{2,3},{3,2},{4,5},{5,4},{6,7},{7,6},{8,9},{9,8},{10,11... | collective-permute-start | bytes 663560 | tf_op jit(solution)/shard_map/ppermute | solution.py:317
  22.6 2.5 %collective-permute-start.9 = (bf16[4,216,128]{2,1,0:T(8,128)(2,1)S(1)}, bf16[4,216,128]{2,1,0:T(8,128)(2,1)S(1)}, u32[]{:S(2)}, u32[]{:S(2)}) collective-permute-start(bf16[4,216,128]{2,1,0:T(8,128)(2,1)S(1)} %collective-permute-done.5.refs_3_), channel_id=1, source_target_pairs={{0,1},{1,0},{2,3},{3,2},{4,5},{5,4},{6,7},{7,6},{8,9},{9,8},{10,11... | collective-permute-start | bytes 663560 | tf_op jit(solution)/shard_map/ppermute | solution.py:317
  25.0 1.5 %collective-permute-start.10 = (bf16[4,216,128]{2,1,0:T(8,128)(2,1)S(1)}, bf16[4,216,128]{2,1,0:T(8,128)(2,1)S(1)}, u32[]{:S(2)}, u32[]{:S(2)}) collective-permute-start(bf16[4,216,128]{2,1,0:T(8,128)(2,1)S(1)} %collective-permute-done.6.refs_4_), channel_id=1, source_target_pairs={{0,1},{1,0},{2,3},{3,2},{4,5},{5,4},{6,7},{7,6},{8,9},{9,8},{10,11... | collective-permute-start | bytes 663560 | tf_op jit(solution)/shard_map/ppermute | solution.py:317
  29.6 3.5 %collective-permute-start.11 = (bf16[8,216,128]{2,1,0:T(8,128)(2,1)S(1)}, bf16[8,216,128]{2,1,0:T(8,128)(2,1)S(1)}, u32[]{:S(2)}, u32[]{:S(2)}) collective-permute-start(bf16[8,216,128]{2,1,0:T(8,128)(2,1)S(1)} %get-tuple-element.39), channel_id=1, source_target_pairs={{0,1},{1,0},{2,3},{3,2},{4,5},{5,4},{6,7},{7,6},{8,9},{9,8},{10,11... | collective-permute-start | bytes 1327112 | tf_op jit(solution)/shard_map/ppermute | solution.py:317
  32.6 1.9 %collective-permute-start.12 = (bf16[8,216,128]{2,1,0:T(8,128)(2,1)S(1)}, bf16[8,216,128]{2,1,0:T(8,128)(2,1)S(1)}, u32[]{:S(2)}, u32[]{:S(2)}) collective-permute-start(bf16[8,216,128]{2,1,0:T(8,128)(2,1)S(1)} %get-tuple-element.42), channel_id=1, source_target_pairs={{0,1},{1,0},{2,3},{3,2},{4,5},{5,4},{6,7},{7,6},{8,9},{9,8},{10,11... | collective-permute-start | bytes 1327112 | tf_op jit(solution)/shard_map/ppermute | solution.py:317
  34.6 6.0 %collective-permute-start.13 = (bf16[4,216,128]{2,1,0:T(8,128)(2,1)S(1)}, bf16[4,216,128]{2,1,0:T(8,128)(2,1)S(1)}, u32[]{:S(2)}, u32[]{:S(2)}) collective-permute-start(bf16[4,216,128]{2,1,0:T(8,128)(2,1)S(1)} %get-tuple-element.44), channel_id=1, source_target_pairs={{0,2},{1,5},{2,0},{3,7},{4,6},{5,1},{6,4},{7,3},{8,10},{9,13},{10,... | collective-permute-start | bytes 663560 | tf_op jit(solution)/shard_map/ppermute | solution.py:322
  36.4 6.7 %collective-permute-start.15 = (bf16[4,216,128]{2,1,0:T(8,128)(2,1)S(1)}, bf16[4,216,128]{2,1,0:T(8,128)(2,1)S(1)}, u32[]{:S(2)}, u32[]{:S(2)}) collective-permute-start(bf16[4,216,128]{2,1,0:T(8,128)(2,1)S(1)} %get-tuple-element.48), channel_id=1, source_target_pairs={{0,2},{1,5},{2,0},{3,7},{4,6},{5,1},{6,4},{7,3},{8,10},{9,13},{10,... | collective-permute-start | bytes 663560 | tf_op jit(solution)/shard_map/ppermute | solution.py:322
  40.7 4.8 %collective-permute-start.14 = (bf16[2,216,128]{2,1,0:T(8,128)(2,1)S(1)}, bf16[2,216,128]{2,1,0:T(8,128)(2,1)S(1)}, u32[]{:S(2)}, u32[]{:S(2)}) collective-permute-start(bf16[2,216,128]{2,1,0:T(8,128)(2,1)S(1)} %get-tuple-element.46.refs_3_), channel_id=1, source_target_pairs={{0,4},{1,3},{2,6},{3,1},{4,0},{5,7},{6,2},{7,5},{8,12},{9,11},{10,... | collective-permute-start | bytes 331784 | tf_op jit(solution)/shard_map/ppermute | solution.py:322
  43.2 5.7 %collective-permute-start.16 = (bf16[2,216,128]{2,1,0:T(8,128)(2,1)S(1)}, bf16[2,216,128]{2,1,0:T(8,128)(2,1)S(1)}, u32[]{:S(2)}, u32[]{:S(2)}) collective-permute-start(bf16[2,216,128]{2,1,0:T(8,128)(2,1)S(1)} %get-tuple-element.50), channel_id=1, source_target_pairs={{0,4},{1,3},{2,6},{3,1},{4,0},{5,7},{6,2},{7,5},{8,12},{9,11},{10,... | collective-permute-start | bytes 331784 | tf_op jit(solution)/shard_map/ppermute | solution.py:322
  45.5 6.9 %collective-permute-start.17 = (bf16[2,216,128]{2,1,0:T(8,128)(2,1)S(1)}, bf16[2,216,128]{2,1,0:T(8,128)(2,1)S(1)}, u32[]{:S(2)}, u32[]{:S(2)}) collective-permute-start(bf16[2,216,128]{2,1,0:T(8,128)(2,1)S(1)} %far_last.1.refs_2_), channel_id=1, source_target_pairs={{0,8},{1,9},{2,10},{3,11},{4,12},{5,13},{6,14},{7,15},{8,0},{9,1},... | collective-permute-start | bytes 331784 | tf_op jit(solution)/shard_map/ppermute | solution.py:317

commit v5 on v4

--- a/solution.py
+++ b/solution.py
@@ -59,15 +59,26 @@
         )
 
 
-def prepare_kernel(me_ref, f_ref, g_ref, core_ref, chip_ref, xf_ref, xg_ref, gt_ref):
-    planes, height, width, channels = f_ref.shape
+def sides(me_ref, core_ref, chip_ref, own):
     odd = me_ref[0] % 2
-    for ref, below in ((core_ref, odd), (chip_ref, 1 - odd)):
+    for ref, below in ((core_ref, odd == 1), (chip_ref, odd == 0)):
+        yield ref, lambda p, count: jnp.where(below, p, own + count + p)
+
+
+def features_kernel(me_ref, f_ref, core_ref, chip_ref, xf_ref):
+    planes = f_ref.shape[0]
+    for ref, place in sides(me_ref, core_ref, chip_ref, planes):
         for p in range(2):
-            write_shifted(xf_ref, jnp.where(below == 1, p, planes + 2 + p), ref[p])
-        write_shifted(xg_ref, jnp.where(below == 1, 0, planes + 1), ref[2])
+            write_shifted(xf_ref, place(p, 2), ref[p])
     for p in range(planes):
         write_shifted(xf_ref, p + 2, f_ref[p])
+
+
+def cotangent_kernel(me_ref, g_ref, core_ref, chip_ref, xg_ref, gt_ref):
+    planes, height, width, channels = g_ref.shape
+    for ref, place in sides(me_ref, core_ref, chip_ref, planes):
+        write_shifted(xg_ref, place(0, 1), ref[2])
+    for p in range(planes):
         write_shifted(xg_ref, p + 1, g_ref[p])
 
     def transposed(p, _):
@@ -95,14 +106,11 @@
     copy_all(((f_hbm, f_ref), (g_hbm, g_ref)), sems)
 
 
-def load_shards_kernel(first_hbm, second_hbm, shards_ref, sems):
-    copy_all(((first_hbm, shards_ref.at[0]), (second_hbm, shards_ref.at[1])), sems)
-
-
-def edges_kernel(me_ref, f_hbm, g_hbm, core_ref, chip_ref, sems):
+def first_load_kernel(me_ref, f_hbm, g_hbm, first_hbm, second_hbm, *refs):
+    shards_ref, core_ref, chip_ref, sems = refs
     planes = f_hbm.shape[0]
     odd = me_ref[0] % 2
-    moves = []
+    moves = [(first_hbm, shards_ref.at[0]), (second_hbm, shards_ref.at[1])]
     for ref, low in ((chip_ref, odd == 0), (core_ref, odd == 1)):
         moves.append((f_hbm.at[pl.ds(jnp.where(low, 0, planes - 2), 2)], ref.at[pl.ds(0, 2)]))
         moves.append((g_hbm.at[pl.ds(jnp.where(low, 0, planes - 1), 1)], ref.at[pl.ds(2, 1)]))
@@ -122,7 +130,7 @@
         out_shape=outs,
         in_specs=[pl.BlockSpec(memory_space=space) for space in spaces],
         out_specs=[pl.BlockSpec(memory_space=pltpu.VMEM) for _ in outs],
-        scratch_shapes=[pltpu.SemaphoreType.DMA((4,))],
+        scratch_shapes=[pltpu.SemaphoreType.DMA((6,))],
         name=name,
         compiler_params=pltpu.CompilerParams(vmem_limit_bytes=LIMIT),
         cost_estimate=pl.CostEstimate(flops=1000, bytes_accessed=0, transcendentals=0),
@@ -340,12 +348,12 @@
     order = assemble if direct else assemble_in_order
 
     edge = like((3, height, width, channels), BF16)
-    to_core, to_chip = from_hbm(edges_kernel, "edges", [edge, edge], [features, cotangent], [me])
-    (own,) = from_hbm(
-        load_shards_kernel,
-        "load_shards",
-        [like((2, rows, channels), BF16)],
-        [filters_first, filters_second],
+    own, to_core, to_chip = from_hbm(
+        first_load_kernel,
+        "load_shards_and_edges",
+        [like((2, rows, channels), BF16), edge, edge],
+        [features, cotangent, filters_first, filters_second],
+        [me],
     )
     features, cotangent = from_hbm(
         load_kernel,
@@ -357,15 +365,12 @@
     from_core = swap(to_core, count, 1)
     next_chip = [(i, i + 1 if i % 2 else i - 1) for i in range(1, count - 1)]
     from_chip = lax.ppermute(to_chip, "slab", next_chip)
-    xf, xg, gt = local_call(
-        prepare_kernel,
-        "shifted_planes",
-        [
-            like((planes + 4, height + 2, width, 3 * channels), BF16),
-            like((planes + 2, height + 2, width, 3 * channels), BF16),
-            like((planes + 2, 9, channels, height * width), BF16),
-        ],
-        [me, features, cotangent, from_core, from_chip],
+    edges = [from_core, from_chip]
+    (xf,) = local_call(
+        features_kernel,
+        "feature_planes",
+        [like((planes + 4, height + 2, width, 3 * channels), BF16)],
+        [me, features, *edges],
         scalars=1,
     )
     wait_for = []
@@ -377,6 +382,7 @@
         near = swap_mixed(far, count, 4, 2)
         away = joined([far, near], "far_and_near", [xf])
         cross_away = swap_mixed(away, count, 2, 4)
+        wait_for = [cross_away]
         pieces = [close, away, cross, cross_away]
         pieces += [swap(piece, count, 1) for piece in pieces]
     else:
@@ -384,6 +390,17 @@
             lax.all_gather(shard, "slab", axis=0, tiled=True)
             for shard in (filters_first, filters_second)
         ]
+    xg, gt = local_call(
+        cotangent_kernel,
+        "cotangent_planes",
+        [
+            like((planes + 2, height + 2, width, 3 * channels), BF16),
+            like((planes + 2, 9, channels, height * width), BF16),
+        ],
+        [me, cotangent, *edges],
+        scalars=1,
+        wait_for=wait_for,
+    )
     terms = [like((8, shard_rows, channels), BF16), like((8, shard_rows, channels), F32)]
     total = pltpu.VMEM((taps, channels), F32)
     bank, hidden, slope, send_second, keep_second = local_call(
@@ -398,7 +415,6 @@
         [place, *pieces, xf, xg],
         scratch=[total],
         scalars=1,
-        wait_for=wait_for,
     )
     bank_second, send_first, keep_first = local_call(
         functools.partial(second_kernel, len(pieces), order),

time: 53.4 us -> 52.8 us (0.989)
  waiting for transfers between devices: 17.9 us -> 20.1 us
  starting transfers between devices: 19.1 us -> 17.1 us
  Pallas kernels: 15.4 us -> 14.6 us
    ppermute x8, waiting for transfers between devices: 12.9 us -> 15.8 us  [swap_mixed(): return lax.ppermute(value, 'slab', pairs)]
    ppermute x8, starting transfers between devices: 11.8 us -> 9.31 us  [swap_mixed(): return lax.ppermute(value, 'slab', pairs)]
    ppermute x9, waiting for transfers between devices: 5.03 us -> 4.26 us  [swap(): lax.ppermute(value, 'slab', [(i, i ^ distance) for i in range(count)])]
    pallas_call x3 -> x2, Pallas kernels: 2.97 us -> 2.2 us  [from_hbm(): pl.pallas_call(body, out_shape=outs, in_specs=[pl.BlockSpec(memory_space=...]
    pallas_call x12 -> x13, Pallas kernels: 12.4 us -> 12.4 us  [local_call(): pl.pallas_call(body, out_shape=list(outs), in_specs=[pl.BlockSpec(memory_...]
  transfers between devices with their start and end apart: 18 -> 18, of which waited for: 10 -> 11; matrix products, arithmetic and copies ran while one was open for 0% -> 0% of each run, Pallas kernels for 20% -> 18%
where the time goes in v5:
time: 52.8 us; the launch traced here: 52.6 us
  waiting for transfers between devices  20.1 us (38%)
  starting transfers between devices  17.1 us (32%)
  Pallas kernels  14.6 us (28%)
  between operations  0.77 us (1%)
    ppermute x8, waiting for transfers between devices, swap_mixed(): return lax.ppermute(value, 'slab', pairs)  15.8 us
    pallas_call x13, Pallas kernels, local_call(): pl.pallas_call(body, out_shape=list(outs), in_specs=[pl.BlockSpec(memory_...  12.4 us
    ppermute x8, starting transfers between devices, swap_mixed(): return lax.ppermute(value, 'slab', pairs)  9.31 us
    ppermute x9, starting transfers between devices, swap(): lax.ppermute(value, 'slab', [(i, i ^ distance) for i in range(count)])  7.14 us
    ppermute x9, waiting for transfers between devices, swap(): lax.ppermute(value, 'slab', [(i, i ^ distance) for i in range(count)])  4.26 us
    pallas_call x2, Pallas kernels, from_hbm(): pl.pallas_call(body, out_shape=outs, in_specs=[pl.BlockSpec(memory_space=...  2.2 us
  transfers between devices with their start and end apart: 18, of which 11 were waited for; matrix products, arithmetic and copies ran while one was open for 0% of the time, Pallas kernels for 18%

profile of v5, /device:TPU:0, one launch (start us, length us, event | category | flops | bytes accessed | tf_op | source)
XLA Modules:
  0.0 52.6 jit_solution(16733893440388163291)
XLA Ops:
  0.6 1.1 %load_shards_and_edges.1 = (bf16[2,216,128]{2,1,0:T(8,128)(2,1)S(1)}, bf16[3,16,16,128]{3,2,1,0:T(8,128)(2,1)S(1)}, bf16[3,16,16,128]{3,2,1,0:T(8,128)(2,1)S(1)}) custom-call(s32[1]{0:T(128)} %bitcast.refs_0_, bf16[4,16,16,128]{3,2,1,0:T(8,128)(2,1)} %refs_0_.1, bf16[4,16,16,128]{3,2,1,0:T(8,128)(2,1)} %refs_1_.3, bf16[216,128]{1,0:T(8,128)(2,1)} %refs_3_.1, ...), custom_call_target="tpu_custom_call" | custom-call | flops 1000 | tf_op jit(solution)/shard_map/load_shards_and_edges/pallas_call | solution.py:128
  1.8 4.1 %collective-permute-start.3 = (bf16[2,216,128]{2,1,0:T(8,128)(2,1)S(1)}, bf16[2,216,128]{2,1,0:T(8,128)(2,1)S(1)}, u32[]{:S(2)}, u32[]{:S(2)}) collective-permute-start(bf16[2,216,128]{2,1,0:T(8,128)(2,1)S(1)} %get-tuple-element.31.refs_0_), channel_id=1, source_target_pairs={{0,8},{1,9},{2,10},{3,11},{4,12},{5,13},{6,14},{7,15},{8,0},{9,1},... | collective-permute-start | bytes 331784 | tf_op jit(solution)/shard_map/ppermute | solution.py:325
  5.9 0.0 collective-permute-start
  5.9 0.7 %collective-permute-start.1 = (bf16[3,16,16,128]{3,2,1,0:T(8,128)(2,1)S(1)}, bf16[3,16,16,128]{3,2,1,0:T(8,128)(2,1)S(1)}, u32[]{:S(2)}, u32[]{:S(2)}) collective-permute-start(bf16[3,16,16,128]{3,2,1,0:T(8,128)(2,1)S(1)} %get-tuple-element.28.refs_2_), channel_id=1, source_target_pairs={{1,2},{2,1},{3,4},{4,3},{5,6},{6,5},{7,8},{8,7},{9,10},{10,9},{11,... | collective-permute-start | bytes 589832 | tf_op jit(solution)/shard_map/ppermute | solution.py:367
  6.5 4.4 %collective-permute-start.2 = (bf16[2,216,128]{2,1,0:T(8,128)(2,1)S(1)}, bf16[2,216,128]{2,1,0:T(8,128)(2,1)S(1)}, u32[]{:S(2)}, u32[]{:S(2)}) collective-permute-start(bf16[2,216,128]{2,1,0:T(8,128)(2,1)S(1)} %get-tuple-element.31.refs_0_), channel_id=1, source_target_pairs={{0,4},{1,3},{2,6},{3,1},{4,0},{5,7},{6,2},{7,5},{8,12},{9,11},{10,... | collective-permute-start | bytes 331784 | tf_op jit(solution)/shard_map/ppermute | solution.py:330
  10.9 0.4 collective-permute-done.3.refs_0_
  11.3 0.7 %collective-permute-start.4 = (bf16[2,216,128]{2,1,0:T(8,128)(2,1)S(1)}, bf16[2,216,128]{2,1,0:T(8,128)(2,1)S(1)}, u32[]{:S(2)}, u32[]{:S(2)}) collective-permute-start(bf16[2,216,128]{2,1,0:T(8,128)(2,1)S(1)} %collective-permute-done.3.refs_0_), channel_id=1, source_target_pairs={{0,4},{1,3},{2,6},{3,1},{4,0},{5,7},{6,2},{7,5},{8,12},{9,11},{10,... | collective-permute-start | bytes 331784 | tf_op jit(solution)/shard_map/ppermute | solution.py:330
  12.0 1.1 %load.1 = (bf16[4,16,16,128]{3,2,1,0:T(8,128)(2,1)S(1)}, bf16[4,16,16,128]{3,2,1,0:T(8,128)(2,1)S(1)}) custom-call(bf16[4,16,16,128]{3,2,1,0:T(8,128)(2,1)} %refs_0_.1, bf16[4,16,16,128]{3,2,1,0:T(8,128)(2,1)} %refs_1_.3, bf16[3,16,16,128]{3,2,1,0:T(8,128)(2,1)S(1)} %get-tuple-element.28.refs_2_), custom_call_target="tpu_custom_call" | custom-call | flops 1000 | tf_op jit(solution)/shard_map/load/pallas_call | solution.py:128
  13.1 2.6 %collective-permute-done.2.refs_1_ = bf16[2,216,128]{2,1,0:T(8,128)(2,1)S(1)} collective-permute-done((bf16[2,216,128]{2,1,0:T(8,128)(2,1)S(1)}, bf16[2,216,128]{2,1,0:T(8,128)(2,1)S(1)}, u32[]{:S(2)}, u32[]{:S(2)}) %collective-permute-start.2) | collective-permute-done | bytes 110624 | tf_op jit(solution)/shard_map/ppermute | solution.py:330
  15.7 0.1 collective-permute-start.5
  15.8 0.0 collective-permute-done.refs_2_
  15.8 0.0 collective-permute-done.1.refs_3_
  15.8 0.4 feature_planes.1.refs_2_.refs_9_.refs_1_
  16.2 0.7 %collective-permute-done.4.refs_1_ = bf16[2,216,128]{2,1,0:T(8,128)(2,1)S(1)} collective-permute-done((bf16[2,216,128]{2,1,0:T(8,128)(2,1)S(1)}, bf16[2,216,128]{2,1,0:T(8,128)(2,1)S(1)}, u32[]{:S(2)}, u32[]{:S(2)}) %collective-permute-start.4) | collective-permute-done | bytes 110624 | tf_op jit(solution)/shard_map/ppermute | solution.py:330
  16.9 1.4 %collective-permute-start.6 = (bf16[4,216,128]{2,1,0:T(8,128)(2,1)S(1)}, bf16[4,216,128]{2,1,0:T(8,128)(2,1)S(1)}, u32[]{:S(2)}, u32[]{:S(2)}) collective-permute-start(bf16[4,216,128]{2,1,0:T(8,128)(2,1)S(1)} %far_and_near.1.refs_2_), channel_id=1, source_target_pairs={{0,2},{1,5},{2,0},{3,7},{4,6},{5,1},{6,4},{7,3},{8,10},{9,13},{10,... | collective-permute-start | bytes 663560 | tf_op jit(solution)/shard_map/ppermute | solution.py:330
  18.3 1.4 %collective-permute-start.7 = (bf16[4,216,128]{2,1,0:T(8,128)(2,1)S(1)}, bf16[4,216,128]{2,1,0:T(8,128)(2,1)S(1)}, u32[]{:S(2)}, u32[]{:S(2)}) collective-permute-start(bf16[4,216,128]{2,1,0:T(8,128)(2,1)S(1)} %own_and_near.1.refs_1_), channel_id=1, source_target_pairs={{0,1},{1,0},{2,3},{3,2},{4,5},{5,4},{6,7},{7,6},{8,9},{9,8},{10,11... | collective-permute-start | bytes 663560 | tf_op jit(solution)/shard_map/ppermute | solution.py:325
  19.7 0.0 collective-permute-start.8
  19.7 2.0 %collective-permute-done.5.refs_3_ = bf16[4,216,128]{2,1,0:T(8,128)(2,1)S(1)} collective-permute-done((bf16[4,216,128]{2,1,0:T(8,128)(2,1)S(1)}, bf16[4,216,128]{2,1,0:T(8,128)(2,1)S(1)}, u32[]{:S(2)}, u32[]{:S(2)}) %collective-permute-start.5) | collective-permute-done | bytes 221216 | tf_op jit(solution)/shard_map/ppermute | solution.py:330
  21.7 0.0 collective-permute-start.9
  21.7 2.4 %collective-permute-done.6.refs_4_ = bf16[4,216,128]{2,1,0:T(8,128)(2,1)S(1)} collective-permute-done((bf16[4,216,128]{2,1,0:T(8,128)(2,1)S(1)}, bf16[4,216,128]{2,1,0:T(8,128)(2,1)S(1)}, u32[]{:S(2)}, u32[]{:S(2)}) %collective-permute-start.6) | collective-permute-done | bytes 221216 | tf_op jit(solution)/shard_map/ppermute | solution.py:330
  24.1 0.0 collective-permute-start.10
  24.1 1.5 %cotangent_planes.1 = (bf16[6,18,16,384]{3,2,1,0:T(8,128)(2,1)S(1)}, bf16[6,9,128,256]{3,2,1,0:T(8,128)(2,1)S(1)}) custom-call(s32[1]{0:T(128)} %bitcast.refs_0_, bf16[4,16,16,128]{3,2,1,0:T(8,128)(2,1)S(1)} %get-tuple-element.32.refs_1_, bf16[3,16,16,128]{3,2,1,0:T(8,128)(2,1)S(1)} %collective-permute-done.refs_2_, ...), custom_call_target="tpu_custom_call" | custom-call | flops 1000 | tf_op jit(solution)/shard_map/cotangent_planes/pallas_call | solution.py:31
  25.6 0.0 collective-permute-done.7.refs_5_
  25.7 0.0 collective-permute-done.8.refs_6_
  25.7 0.0 collective-permute-done.9.refs_7_
  25.7 0.0 collective-permute-done.10.refs_8_
  25.7 3.2 %hidden_and_second_grad.1 = (bf16[3456,128]{1,0:T(8,128)(2,1)S(1)}, bf16[4,16,16,128]{3,2,1,0:T(8,128)(2,1)S(1)}, f32[128,1024]{1,0:T(8,128)S(1)}, bf16[8,216,128]{2,1,0:T(8,128)(2,1)S(1)}, f32[8,216,128]{2,1,0:T(8,128)S(1)}) custom-call(s32[1]{0:T(128)} %bitcast.refs_0_, bf16[4,216,128]{2,1,0:T(8,128)(2,1)S(1)} %own_and_near.1.refs_1_, ...), custom_call_target="tpu_custom_call" | custom-call | flops 1000 | tf_op jit(solution)/shard_map/hidden_and_second_grad/pallas_call | solution.py:31
  28.8 0.6 %collective-permute-start.11 = (bf16[8,216,128]{2,1,0:T(8,128)(2,1)S(1)}, bf16[8,216,128]{2,1,0:T(8,128)(2,1)S(1)}, u32[]{:S(2)}, u32[]{:S(2)}) collective-permute-start(bf16[8,216,128]{2,1,0:T(8,128)(2,1)S(1)} %get-tuple-element.39), channel_id=1, source_target_pairs={{0,1},{1,0},{2,3},{3,2},{4,5},{5,4},{6,7},{7,6},{8,9},{9,8},{10,11... | collective-permute-start | bytes 1327112 | tf_op jit(solution)/shard_map/ppermute | solution.py:325
  29.4 2.8 %first_grad.1 = (bf16[3456,128]{1,0:T(8,128)(2,1)S(1)}, bf16[8,216,128]{2,1,0:T(8,128)(2,1)S(1)}, f32[8,216,128]{2,1,0:T(8,128)S(1)}) custom-call(s32[1]{0:T(128)} %bitcast.refs_0_, bf16[4,216,128]{2,1,0:T(8,128)(2,1)S(1)} %own_and_near.1.refs_1_, bf16[4,216,128]{2,1,0:T(8,128)(2,1)S(1)} %far_and_near.1.refs_2_, ...), custom_call_target="tpu_custom_call" | custom-call | flops 1000 | tf_op jit(solution)/shard_map/first_grad/pallas_call | solution.py:31
  32.2 0.1 collective-permute-start.12
  32.3 0.0 collective-permute-done.11.refs_5_.refs_4_
  32.3 1.3 %hidden_planes.1.refs_5_.refs_0_ = bf16[6,18,16,384]{3,2,1,0:T(8,128)(2,1)S(1)} custom-call(s32[1]{0:T(128)} %bitcast.refs_0_, bf16[8,18,16,384]{3,2,1,0:T(8,128)(2,1)S(1)} %feature_planes.1.refs_2_.refs_9_.refs_1_, bf16[3456,128]{1,0:T(8,128)(2,1)S(1)} %get-tuple-element.34.refs_2_, bf16[4,16,16,128]{3,2,1,0:T(8,128)(2,1)S(1)} %get-tuple-element.35.refs_3_, ...), custom_call_target="tpu_custom_call" | custom-call | flops 1000 | tf_op jit(solution)/shard_map/hidden_planes/pallas_call | solution.py:31
  33.6 0.4 collective-permute-done.12.refs_3_
  34.1 0.2 sum_pair.1
  34.3 0.5 %collective-permute-start.13 = (bf16[4,216,128]{2,1,0:T(8,128)(2,1)S(1)}, bf16[4,216,128]{2,1,0:T(8,128)(2,1)S(1)}, u32[]{:S(2)}, u32[]{:S(2)}) collective-permute-start(bf16[4,216,128]{2,1,0:T(8,128)(2,1)S(1)} %get-tuple-element.44), channel_id=1, source_target_pairs={{0,2},{1,5},{2,0},{3,7},{4,6},{5,1},{6,4},{7,3},{8,10},{9,13},{10,... | collective-permute-start | bytes 663560 | tf_op jit(solution)/shard_map/ppermute | solution.py:330
  34.8 1.5 %collective-permute-start.15 = (bf16[4,216,128]{2,1,0:T(8,128)(2,1)S(1)}, bf16[4,216,128]{2,1,0:T(8,128)(2,1)S(1)}, u32[]{:S(2)}, u32[]{:S(2)}) collective-permute-start(bf16[4,216,128]{2,1,0:T(8,128)(2,1)S(1)} %get-tuple-element.48), channel_id=1, source_target_pairs={{0,2},{1,5},{2,0},{3,7},{4,6},{5,1},{6,4},{7,3},{8,10},{9,13},{10,... | collective-permute-start | bytes 663560 | tf_op jit(solution)/shard_map/ppermute | solution.py:330
  36.4 3.9 %collective-permute-done.13.refs_2_ = bf16[4,216,128]{2,1,0:T(8,128)(2,1)S(1)} collective-permute-done((bf16[4,216,128]{2,1,0:T(8,128)(2,1)S(1)}, bf16[4,216,128]{2,1,0:T(8,128)(2,1)S(1)}, u32[]{:S(2)}, u32[]{:S(2)}) %collective-permute-start.13) | collective-permute-done | bytes 221216 | tf_op jit(solution)/shard_map/ppermute | solution.py:330
  40.3 0.4 collective-permute-start.14
  40.8 2.2 %collective-permute-done.15.refs_2_ = bf16[4,216,128]{2,1,0:T(8,128)(2,1)S(1)} collective-permute-done((bf16[4,216,128]{2,1,0:T(8,128)(2,1)S(1)}, bf16[4,216,128]{2,1,0:T(8,128)(2,1)S(1)}, u32[]{:S(2)}, u32[]{:S(2)}) %collective-permute-start.15) | collective-permute-done | bytes 221216 | tf_op jit(solution)/shard_map/ppermute | solution.py:330
  43.0 0.1 own_near.1
  43.0 0.2 collective-permute-start.16
  43.2 1.9 %collective-permute-done.14.refs_1_ = bf16[2,216,128]{2,1,0:T(8,128)(2,1)S(1)} collective-permute-done((bf16[2,216,128]{2,1,0:T(8,128)(2,1)S(1)}, bf16[2,216,128]{2,1,0:T(8,128)(2,1)S(1)}, u32[]{:S(2)}, u32[]{:S(2)}) %collective-permute-start.14) | collective-permute-done | bytes 110624 | tf_op jit(solution)/shard_map/ppermute | solution.py:330
  45.2 1.0 %collective-permute-start.17 = (bf16[2,216,128]{2,1,0:T(8,128)(2,1)S(1)}, bf16[2,216,128]{2,1,0:T(8,128)(2,1)S(1)}, u32[]{:S(2)}, u32[]{:S(2)}) collective-permute-start(bf16[2,216,128]{2,1,0:T(8,128)(2,1)S(1)} %far_last.1.refs_2_), channel_id=1, source_target_pairs={{0,8},{1,9},{2,10},{3,11},{4,12},{5,13},{6,14},{7,15},{8,0},{9,1},... | collective-permute-start | bytes 331784 | tf_op jit(solution)/shard_map/ppermute | solution.py:325
  46.2 2.2 %output_conv.1 = bf16[4,16,16,128]{3,2,1,0:T(8,128)(2,1)} custom-call(bf16[6,18,16,384]{3,2,1,0:T(8,128)(2,1)S(1)} %hidden_planes.1.refs_5_.refs_0_, bf16[3456,128]{1,0:T(8,128)(2,1)S(1)} %get-tuple-element.40.refs_1_, bf16[2,216,128]{2,1,0:T(8,128)(2,1)S(1)} %far_last.1.refs_2_), custom_call_target="tpu_custom_call" | custom-call | flops 1000 | tf_op jit(solution)/shard_map/output_conv/pallas_call | solution.py:31
  48.4 0.1 collective-permute-done.16.refs_1_
  48.4 3.4 %collective-permute-done.17.refs_2_ = bf16[2,216,128]{2,1,0:T(8,128)(2,1)S(1)} collective-permute-done((bf16[2,216,128]{2,1,0:T(8,128)(2,1)S(1)}, bf16[2,216,128]{2,1,0:T(8,128)(2,1)S(1)}, u32[]{:S(2)}, u32[]{:S(2)}) %collective-permute-start.17) | collective-permute-done | bytes 110624 | tf_op jit(solution)/shard_map/ppermute | solution.py:325
  51.9 0.7 %sum_last.1 = (f32[216,128]{1,0:T(8,128)}, f32[216,128]{1,0:T(8,128)}) custom-call(f32[2,216,128]{2,1,0:T(8,128)S(1)} %get-tuple-element.49.refs_0_, bf16[2,216,128]{2,1,0:T(8,128)(2,1)S(1)} %collective-permute-done.16.refs_1_, bf16[2,216,128]{2,1,0:T(8,128)(2,1)S(1)} %collective-permute-done.17.refs_2_), custom_call_target="tpu_custom_call" | custom-call | flops 1000 | tf_op jit(solution)/shard_map/sum_last/pallas_call | solution.py:31
  (4 shorter events, 0.1 us)
Async XLA Ops:
  1.8 9.5 %collective-permute-start.3 = (bf16[2,216,128]{2,1,0:T(8,128)(2,1)S(1)}, bf16[2,216,128]{2,1,0:T(8,128)(2,1)S(1)}, u32[]{:S(2)}, u32[]{:S(2)}) collective-permute-start(bf16[2,216,128]{2,1,0:T(8,128)(2,1)S(1)} %get-tuple-element.31.refs_0_), channel_id=1, source_target_pairs={{0,8},{1,9},{2,10},{3,11},{4,12},{5,13},{6,14},{7,15},{8,0},{9,1},... | collective-permute-start | bytes 331784 | tf_op jit(solution)/shard_map/ppermute | solution.py:325
  5.9 10.0 %collective-permute-start = (bf16[3,16,16,128]{3,2,1,0:T(8,128)(2,1)S(1)}, bf16[3,16,16,128]{3,2,1,0:T(8,128)(2,1)S(1)}, u32[]{:S(2)}, u32[]{:S(2)}) collective-permute-start(bf16[3,16,16,128]{3,2,1,0:T(8,128)(2,1)S(1)} %get-tuple-element.30), channel_id=1, source_target_pairs={{0,1},{1,0},{2,3},{3,2},{4,5},{5,4},{6,7},{7,6},{8,9},{9,8},{10,11... | collective-permute-start | bytes 589832 | tf_op jit(solution)/shard_map/ppermute | solution.py:325
  5.9 10.0 %collective-permute-start.1 = (bf16[3,16,16,128]{3,2,1,0:T(8,128)(2,1)S(1)}, bf16[3,16,16,128]{3,2,1,0:T(8,128)(2,1)S(1)}, u32[]{:S(2)}, u32[]{:S(2)}) collective-permute-start(bf16[3,16,16,128]{3,2,1,0:T(8,128)(2,1)S(1)} %get-tuple-element.28.refs_2_), channel_id=1, source_target_pairs={{1,2},{2,1},{3,4},{4,3},{5,6},{6,5},{7,8},{8,7},{9,10},{10,9},{11,... | collective-permute-start | bytes 589832 | tf_op jit(solution)/shard_map/ppermute | solution.py:367
  6.5 9.2 %collective-permute-start.2 = (bf16[2,216,128]{2,1,0:T(8,128)(2,1)S(1)}, bf16[2,216,128]{2,1,0:T(8,128)(2,1)S(1)}, u32[]{:S(2)}, u32[]{:S(2)}) collective-permute-start(bf16[2,216,128]{2,1,0:T(8,128)(2,1)S(1)} %get-tuple-element.31.refs_0_), channel_id=1, source_target_pairs={{0,4},{1,3},{2,6},{3,1},{4,0},{5,7},{6,2},{7,5},{8,12},{9,11},{10,... | collective-permute-start | bytes 331784 | tf_op jit(solution)/shard_map/ppermute | solution.py:330
  11.3 5.6 %collective-permute-start.4 = (bf16[2,216,128]{2,1,0:T(8,128)(2,1)S(1)}, bf16[2,216,128]{2,1,0:T(8,128)(2,1)S(1)}, u32[]{:S(2)}, u32[]{:S(2)}) collective-permute-start(bf16[2,216,128]{2,1,0:T(8,128)(2,1)S(1)} %collective-permute-done.3.refs_0_), channel_id=1, source_target_pairs={{0,4},{1,3},{2,6},{3,1},{4,0},{5,7},{6,2},{7,5},{8,12},{9,11},{10,... | collective-permute-start | bytes 331784 | tf_op jit(solution)/shard_map/ppermute | solution.py:330
  15.7 6.0 %collective-permute-start.5 = (bf16[4,216,128]{2,1,0:T(8,128)(2,1)S(1)}, bf16[4,216,128]{2,1,0:T(8,128)(2,1)S(1)}, u32[]{:S(2)}, u32[]{:S(2)}) collective-permute-start(bf16[4,216,128]{2,1,0:T(8,128)(2,1)S(1)} %own_and_near.1.refs_1_), channel_id=1, source_target_pairs={{0,2},{1,5},{2,0},{3,7},{4,6},{5,1},{6,4},{7,3},{8,10},{9,13},{10,... | collective-permute-start | bytes 663560 | tf_op jit(solution)/shard_map/ppermute | solution.py:330
  16.9 7.2 %collective-permute-start.6 = (bf16[4,216,128]{2,1,0:T(8,128)(2,1)S(1)}, bf16[4,216,128]{2,1,0:T(8,128)(2,1)S(1)}, u32[]{:S(2)}, u32[]{:S(2)}) collective-permute-start(bf16[4,216,128]{2,1,0:T(8,128)(2,1)S(1)} %far_and_near.1.refs_2_), channel_id=1, source_target_pairs={{0,2},{1,5},{2,0},{3,7},{4,6},{5,1},{6,4},{7,3},{8,10},{9,13},{10,... | collective-permute-start | bytes 663560 | tf_op jit(solution)/shard_map/ppermute | solution.py:330
  18.3 7.3 %collective-permute-start.7 = (bf16[4,216,128]{2,1,0:T(8,128)(2,1)S(1)}, bf16[4,216,128]{2,1,0:T(8,128)(2,1)S(1)}, u32[]{:S(2)}, u32[]{:S(2)}) collective-permute-start(bf16[4,216,128]{2,1,0:T(8,128)(2,1)S(1)} %own_and_near.1.refs_1_), channel_id=1, source_target_pairs={{0,1},{1,0},{2,3},{3,2},{4,5},{5,4},{6,7},{7,6},{8,9},{9,8},{10,11... | collective-permute-start | bytes 663560 | tf_op jit(solution)/shard_map/ppermute | solution.py:325
  19.7 6.0 %collective-permute-start.8 = (bf16[4,216,128]{2,1,0:T(8,128)(2,1)S(1)}, bf16[4,216,128]{2,1,0:T(8,128)(2,1)S(1)}, u32[]{:S(2)}, u32[]{:S(2)}) collective-permute-start(bf16[4,216,128]{2,1,0:T(8,128)(2,1)S(1)} %far_and_near.1.refs_2_), channel_id=1, source_target_pairs={{0,1},{1,0},{2,3},{3,2},{4,5},{5,4},{6,7},{7,6},{8,9},{9,8},{10,11... | collective-permute-start | bytes 663560 | tf_op jit(solution)/shard_map/ppermute | solution.py:325
  21.7 3.9 %collective-permute-start.9 = (bf16[4,216,128]{2,1,0:T(8,128)(2,1)S(1)}, bf16[4,216,128]{2,1,0:T(8,128)(2,1)S(1)}, u32[]{:S(2)}, u32[]{:S(2)}) collective-permute-start(bf16[4,216,128]{2,1,0:T(8,128)(2,1)S(1)} %collective-permute-done.5.refs_3_), channel_id=1, source_target_pairs={{0,1},{1,0},{2,3},{3,2},{4,5},{5,4},{6,7},{7,6},{8,9},{9,8},{10,11... | collective-permute-start | bytes 663560 | tf_op jit(solution)/shard_map/ppermute | solution.py:325
  24.1 1.6 %collective-permute-start.10 = (bf16[4,216,128]{2,1,0:T(8,128)(2,1)S(1)}, bf16[4,216,128]{2,1,0:T(8,128)(2,1)S(1)}, u32[]{:S(2)}, u32[]{:S(2)}) collective-permute-start(bf16[4,216,128]{2,1,0:T(8,128)(2,1)S(1)} %collective-permute-done.6.refs_4_), channel_id=1, source_target_pairs={{0,1},{1,0},{2,3},{3,2},{4,5},{5,4},{6,7},{7,6},{8,9},{9,8},{10,11... | collective-permute-start | bytes 663560 | tf_op jit(solution)/shard_map/ppermute | solution.py:325
  28.8 3.5 %collective-permute-start.11 = (bf16[8,216,128]{2,1,0:T(8,128)(2,1)S(1)}, bf16[8,216,128]{2,1,0:T(8,128)(2,1)S(1)}, u32[]{:S(2)}, u32[]{:S(2)}) collective-permute-start(bf16[8,216,128]{2,1,0:T(8,128)(2,1)S(1)} %get-tuple-element.39), channel_id=1, source_target_pairs={{0,1},{1,0},{2,3},{3,2},{4,5},{5,4},{6,7},{7,6},{8,9},{9,8},{10,11... | collective-permute-start | bytes 1327112 | tf_op jit(solution)/shard_map/ppermute | solution.py:325
  32.2 1.9 %collective-permute-start.12 = (bf16[8,216,128]{2,1,0:T(8,128)(2,1)S(1)}, bf16[8,216,128]{2,1,0:T(8,128)(2,1)S(1)}, u32[]{:S(2)}, u32[]{:S(2)}) collective-permute-start(bf16[8,216,128]{2,1,0:T(8,128)(2,1)S(1)} %get-tuple-element.42), channel_id=1, source_target_pairs={{0,1},{1,0},{2,3},{3,2},{4,5},{5,4},{6,7},{7,6},{8,9},{9,8},{10,11... | collective-permute-start | bytes 1327112 | tf_op jit(solution)/shard_map/ppermute | solution.py:325
  34.3 6.0 %collective-permute-start.13 = (bf16[4,216,128]{2,1,0:T(8,128)(2,1)S(1)}, bf16[4,216,128]{2,1,0:T(8,128)(2,1)S(1)}, u32[]{:S(2)}, u32[]{:S(2)}) collective-permute-start(bf16[4,216,128]{2,1,0:T(8,128)(2,1)S(1)} %get-tuple-element.44), channel_id=1, source_target_pairs={{0,2},{1,5},{2,0},{3,7},{4,6},{5,1},{6,4},{7,3},{8,10},{9,13},{10,... | collective-permute-start | bytes 663560 | tf_op jit(solution)/shard_map/ppermute | solution.py:330
  34.8 8.1 %collective-permute-start.15 = (bf16[4,216,128]{2,1,0:T(8,128)(2,1)S(1)}, bf16[4,216,128]{2,1,0:T(8,128)(2,1)S(1)}, u32[]{:S(2)}, u32[]{:S(2)}) collective-permute-start(bf16[4,216,128]{2,1,0:T(8,128)(2,1)S(1)} %get-tuple-element.48), channel_id=1, source_target_pairs={{0,2},{1,5},{2,0},{3,7},{4,6},{5,1},{6,4},{7,3},{8,10},{9,13},{10,... | collective-permute-start | bytes 663560 | tf_op jit(solution)/shard_map/ppermute | solution.py:330
  40.3 4.8 %collective-permute-start.14 = (bf16[2,216,128]{2,1,0:T(8,128)(2,1)S(1)}, bf16[2,216,128]{2,1,0:T(8,128)(2,1)S(1)}, u32[]{:S(2)}, u32[]{:S(2)}) collective-permute-start(bf16[2,216,128]{2,1,0:T(8,128)(2,1)S(1)} %get-tuple-element.46.refs_3_), channel_id=1, source_target_pairs={{0,4},{1,3},{2,6},{3,1},{4,0},{5,7},{6,2},{7,5},{8,12},{9,11},{10,... | collective-permute-start | bytes 331784 | tf_op jit(solution)/shard_map/ppermute | solution.py:330
  43.0 5.4 %collective-permute-start.16 = (bf16[2,216,128]{2,1,0:T(8,128)(2,1)S(1)}, bf16[2,216,128]{2,1,0:T(8,128)(2,1)S(1)}, u32[]{:S(2)}, u32[]{:S(2)}) collective-permute-start(bf16[2,216,128]{2,1,0:T(8,128)(2,1)S(1)} %get-tuple-element.50), channel_id=1, source_target_pairs={{0,4},{1,3},{2,6},{3,1},{4,0},{5,7},{6,2},{7,5},{8,12},{9,11},{10,... | collective-permute-start | bytes 331784 | tf_op jit(solution)/shard_map/ppermute | solution.py:330
  45.2 6.7 %collective-permute-start.17 = (bf16[2,216,128]{2,1,0:T(8,128)(2,1)S(1)}, bf16[2,216,128]{2,1,0:T(8,128)(2,1)S(1)}, u32[]{:S(2)}, u32[]{:S(2)}) collective-permute-start(bf16[2,216,128]{2,1,0:T(8,128)(2,1)S(1)} %far_last.1.refs_2_), channel_id=1, source_target_pairs={{0,8},{1,9},{2,10},{3,11},{4,12},{5,13},{6,14},{7,15},{8,0},{9,1},... | collective-permute-start | bytes 331784 | tf_op jit(solution)/shard_map/ppermute | solution.py:325

commit v6 on v5

--- a/solution.py
+++ b/solution.py
@@ -288,28 +288,32 @@
     return low, jnp.where(low, y, z), jnp.where(low, z, y), me // 8
 
 
-def sum_pair_kernel(me_ref, *refs):
-    keep_refs, got_refs, (far_send, send, far_own, own) = refs[:2], refs[2:4], refs[4:]
+def sum_pair_kernel(me_ref, keep_ref, got_ref, *refs):
+    before, (far_send, far_own, send, own) = refs[:-4], refs[-4:]
     low, first, _, last = scatter_bits(me_ref[0])
-    for bank, (keep_ref, got_ref) in enumerate(zip(keep_refs, got_refs)):
-        for second in range(2):
-            at = 2 * bank + second
-            for side, send_ref, own_ref in ((1 - last, far_send, far_own), (last, send, own)):
-
-                def total(bit):
-                    k = 4 * side + jnp.where(low, 2 * second + bit, 2 * bit + second)
-                    return keep_ref[k] + got_ref[k].astype(F32)
-
-                own_ref[at] = total(first)
-                send_ref[at] = total(1 - first).astype(BF16)
-
-
-def sum_near_kernel(me_ref, own_ref, got_ref, send_ref, keep_ref):
+    if before:
+        for ref, earlier in zip((send, own), before):
+            ref[2:4] = earlier[...]
+    for second in range(2):
+        for side, send_ref, own_ref in ((1 - last, far_send, far_own), (last, send, own)):
+
+            def total(bit):
+                k = 4 * side + jnp.where(low, 2 * second + bit, 2 * bit + second)
+                return keep_ref[k] + got_ref[k].astype(F32)
+
+            own_ref[second] = total(first)
+            send_ref[second] = total(1 - first).astype(BF16)
+
+
+def sum_near_kernel(me_ref, own_ref, got_ref, *refs):
+    before, (send_ref, keep_ref) = refs[:-2], refs[-2:]
     _, _, second, _ = scatter_bits(me_ref[0])
-    for bank in range(2):
+    for bank in range(own_ref.shape[0] // 2):
         mine, other = 2 * bank + second, 2 * bank + 1 - second
         keep_ref[bank] = own_ref[mine] + got_ref[mine].astype(F32)
         send_ref[bank] = (own_ref[other] + got_ref[other].astype(F32)).astype(BF16)
+    for ref, earlier in zip((send_ref, keep_ref), before):
+        ref[1:2] = earlier[...]
 
 
 def sum_far_kernel(keep_ref, got_ref, send_ref):
@@ -424,10 +428,20 @@
         scratch=[total],
         scalars=1,
     )
+    def both(count):
+        return [like((count, rows, channels), BF16), like((count, rows, channels), F32)]
+
     wait_for = [keep_first]
     if direct:
-        got_second = swap(send_second, count, 1)
-        wait_for.append(got_second)
+        far_send, far_own_second, *own_second = local_call(
+            sum_pair_kernel,
+            "second_pair",
+            both(2) + both(2),
+            [me, keep_second, swap(send_second, count, 1)],
+            scalars=1,
+        )
+        far_got_second = swap_mixed(far_send, count, 2, 4)
+        wait_for.append(far_send)
     (xh,) = local_call(
         functools.partial(hidden_kernel, count),
         "hidden_planes",
@@ -438,34 +452,34 @@
     )
     wait_for = []
     if direct:
-        blocks = [like((4, rows, channels), BF16)] * 2 + [like((4, rows, channels), F32)] * 2
-        far_send, send, far_own, own = local_call(
+        far_send, far_own, send, own = local_call(
             sum_pair_kernel,
-            "sum_pair",
-            blocks,
-            [
-                me,
-                keep_first,
-                keep_second,
-                swap(send_first, count, 1),
-                got_second,
-            ],
+            "first_pair",
+            both(2) + both(4),
+            [me, keep_first, swap(send_first, count, 1), *own_second],
             scalars=1,
             wait_for=[xh],
         )
-        halves = [like((2, rows, channels), BF16), like((2, rows, channels), F32)]
         far_got = swap_mixed(far_send, count, 2, 4)
+        far_second = local_call(
+            sum_near_kernel,
+            "second_far_near",
+            both(1),
+            [me, far_own_second, far_got_second],
+            scalars=1,
+            wait_for=[far_send],
+        )
         far_send, far_keep = local_call(
-            sum_near_kernel, "far_near", halves, [me, far_own, far_got], scalars=1
+            sum_near_kernel, "first_far_near", both(2), [me, far_own, far_got, *far_second], scalars=1
         )
         far_got = swap_mixed(far_send, count, 4, 2)
         got = swap_mixed(send, count, 2, 4)
         send, keep = local_call(
-            sum_near_kernel, "own_near", halves, [me, own, got], scalars=1, wait_for=[far_send]
+            sum_near_kernel, "own_near", both(2), [me, own, got], scalars=1, wait_for=[far_send]
         )
         got = swap_mixed(send, count, 4, 2)
         (far_send,) = local_call(
-            sum_far_kernel, "far_last", halves[:1], [far_keep, far_got]
+            sum_far_kernel, "far_last", both(2)[:1], [far_keep, far_got]
         )
         far_got = swap(far_send, count, 8)
         wait_for = [far_send]

time: 52.8 us -> 52.6 us (level)
  waiting for transfers between devices: 20.1 us -> 13.1 us
  starting transfers between devices: 17.1 us -> 23.9 us
    ppermute x8 -> x9, waiting for transfers between devices: 15.8 us -> 10.7 us  [swap_mixed(): return lax.ppermute(value, 'slab', pairs)]
    ppermute x9, starting transfers between devices: 7.14 us -> 11.5 us  [swap(): lax.ppermute(value, 'slab', [(i, i ^ distance) for i in range(count)])]
    ppermute x8 -> x9, starting transfers between devices: 9.31 us -> 11.7 us  [swap_mixed(): return lax.ppermute(value, 'slab', pairs)]
    ppermute x9, waiting for transfers between devices: 4.26 us -> 2.42 us  [swap(): lax.ppermute(value, 'slab', [(i, i ^ distance) for i in range(count)])]
    pallas_call x13 -> x15, Pallas kernels: 12.4 us -> 12.5 us  [local_call(): pl.pallas_call(body, out_shape=list(outs), in_specs=[pl.BlockSpec(memory_...]
  transfers between devices with their start and end apart: 18 -> 19, of which waited for: 11 -> 7; matrix products, arithmetic and copies ran while one was open for 0% -> 0% of each run, Pallas kernels for 18% -> 19%
where the time goes in v6:
time: 52.6 us; the launch traced here: 52.5 us
  starting transfers between devices  23.9 us (45%)
  Pallas kernels  14.7 us (28%)
  waiting for transfers between devices  13.1 us (25%)
  between operations  0.77 us (1%)
    pallas_call x15, Pallas kernels, local_call(): pl.pallas_call(body, out_shape=list(outs), in_specs=[pl.BlockSpec(memory_...  12.5 us
    ppermute x9, starting transfers between devices, swap_mixed(): return lax.ppermute(value, 'slab', pairs)  11.7 us
    ppermute x9, starting transfers between devices, swap(): lax.ppermute(value, 'slab', [(i, i ^ distance) for i in range(count)])  11.5 us
    ppermute x9, waiting for transfers between devices, swap_mixed(): return lax.ppermute(value, 'slab', pairs)  10.7 us
    ppermute x9, waiting for transfers between devices, swap(): lax.ppermute(value, 'slab', [(i, i ^ distance) for i in range(count)])  2.42 us
    pallas_call x2, Pallas kernels, from_hbm(): pl.pallas_call(body, out_shape=outs, in_specs=[pl.BlockSpec(memory_space=...  2.2 us
  transfers between devices with their start and end apart: 19, of which 7 were waited for; matrix products, arithmetic and copies ran while one was open for 0% of the time, Pallas kernels for 19%

profile of v6, /device:TPU:0, one launch (start us, length us, event | category | flops | bytes accessed | tf_op | source)
XLA Modules:
  0.0 52.5 jit_solution(6050904395964263422)
XLA Ops:
  0.6 1.1 %load_shards_and_edges.1 = (bf16[2,216,128]{2,1,0:T(8,128)(2,1)S(1)}, bf16[3,16,16,128]{3,2,1,0:T(8,128)(2,1)S(1)}, bf16[3,16,16,128]{3,2,1,0:T(8,128)(2,1)S(1)}) custom-call(s32[1]{0:T(128)} %bitcast.refs_0_, bf16[4,16,16,128]{3,2,1,0:T(8,128)(2,1)} %refs_0_.1, bf16[4,16,16,128]{3,2,1,0:T(8,128)(2,1)} %refs_1_.3, bf16[216,128]{1,0:T(8,128)(2,1)} %refs_3_.1, ...), custom_call_target="tpu_custom_call" | custom-call | flops 1000 | tf_op jit(solution)/shard_map/load_shards_and_edges/pallas_call | solution.py:128
  1.8 4.1 %collective-permute-start.3 = (bf16[2,216,128]{2,1,0:T(8,128)(2,1)S(1)}, bf16[2,216,128]{2,1,0:T(8,128)(2,1)S(1)}, u32[]{:S(2)}, u32[]{:S(2)}) collective-permute-start(bf16[2,216,128]{2,1,0:T(8,128)(2,1)S(1)} %get-tuple-element.37.refs_0_), channel_id=1, source_target_pairs={{0,8},{1,9},{2,10},{3,11},{4,12},{5,13},{6,14},{7,15},{8,0},{9,1},... | collective-permute-start | bytes 331784 | tf_op jit(solution)/shard_map/ppermute | solution.py:329
  5.9 0.7 %collective-permute-start.1 = (bf16[3,16,16,128]{3,2,1,0:T(8,128)(2,1)S(1)}, bf16[3,16,16,128]{3,2,1,0:T(8,128)(2,1)S(1)}, u32[]{:S(2)}, u32[]{:S(2)}) collective-permute-start(bf16[3,16,16,128]{3,2,1,0:T(8,128)(2,1)S(1)} %get-tuple-element.34.refs_2_), channel_id=1, source_target_pairs={{1,2},{2,1},{3,4},{4,3},{5,6},{6,5},{7,8},{8,7},{9,10},{10,9},{11,... | collective-permute-start | bytes 589832 | tf_op jit(solution)/shard_map/ppermute | solution.py:371
  6.5 2.9 %collective-permute-start = (bf16[3,16,16,128]{3,2,1,0:T(8,128)(2,1)S(1)}, bf16[3,16,16,128]{3,2,1,0:T(8,128)(2,1)S(1)}, u32[]{:S(2)}, u32[]{:S(2)}) collective-permute-start(bf16[3,16,16,128]{3,2,1,0:T(8,128)(2,1)S(1)} %get-tuple-element.36), channel_id=1, source_target_pairs={{0,1},{1,0},{2,3},{3,2},{4,5},{5,4},{6,7},{7,6},{8,9},{9,8},{10,11... | collective-permute-start | bytes 589832 | tf_op jit(solution)/shard_map/ppermute | solution.py:329
  9.5 1.6 %collective-permute-start.2 = (bf16[2,216,128]{2,1,0:T(8,128)(2,1)S(1)}, bf16[2,216,128]{2,1,0:T(8,128)(2,1)S(1)}, u32[]{:S(2)}, u32[]{:S(2)}) collective-permute-start(bf16[2,216,128]{2,1,0:T(8,128)(2,1)S(1)} %get-tuple-element.37.refs_0_), channel_id=1, source_target_pairs={{0,4},{1,3},{2,6},{3,1},{4,0},{5,7},{6,2},{7,5},{8,12},{9,11},{10,... | collective-permute-start | bytes 331784 | tf_op jit(solution)/shard_map/ppermute | solution.py:334
  11.0 0.2 collective-permute-done.3.refs_0_
  11.3 0.7 %collective-permute-start.4 = (bf16[2,216,128]{2,1,0:T(8,128)(2,1)S(1)}, bf16[2,216,128]{2,1,0:T(8,128)(2,1)S(1)}, u32[]{:S(2)}, u32[]{:S(2)}) collective-permute-start(bf16[2,216,128]{2,1,0:T(8,128)(2,1)S(1)} %collective-permute-done.3.refs_0_), channel_id=1, source_target_pairs={{0,4},{1,3},{2,6},{3,1},{4,0},{5,7},{6,2},{7,5},{8,12},{9,11},{10,... | collective-permute-start | bytes 331784 | tf_op jit(solution)/shard_map/ppermute | solution.py:334
  12.0 1.1 %load.1 = (bf16[4,16,16,128]{3,2,1,0:T(8,128)(2,1)S(1)}, bf16[4,16,16,128]{3,2,1,0:T(8,128)(2,1)S(1)}) custom-call(bf16[4,16,16,128]{3,2,1,0:T(8,128)(2,1)} %refs_0_.1, bf16[4,16,16,128]{3,2,1,0:T(8,128)(2,1)} %refs_1_.3, bf16[3,16,16,128]{3,2,1,0:T(8,128)(2,1)S(1)} %get-tuple-element.34.refs_2_), custom_call_target="tpu_custom_call" | custom-call | flops 1000 | tf_op jit(solution)/shard_map/load/pallas_call | solution.py:128
  13.1 1.7 %collective-permute-done.2.refs_1_ = bf16[2,216,128]{2,1,0:T(8,128)(2,1)S(1)} collective-permute-done((bf16[2,216,128]{2,1,0:T(8,128)(2,1)S(1)}, bf16[2,216,128]{2,1,0:T(8,128)(2,1)S(1)}, u32[]{:S(2)}, u32[]{:S(2)}) %collective-permute-start.2) | collective-permute-done | bytes 110624 | tf_op jit(solution)/shard_map/ppermute | solution.py:334
  14.8 1.0 %collective-permute-start.5 = (bf16[4,216,128]{2,1,0:T(8,128)(2,1)S(1)}, bf16[4,216,128]{2,1,0:T(8,128)(2,1)S(1)}, u32[]{:S(2)}, u32[]{:S(2)}) collective-permute-start(bf16[4,216,128]{2,1,0:T(8,128)(2,1)S(1)} %own_and_near.1.refs_1_), channel_id=1, source_target_pairs={{0,2},{1,5},{2,0},{3,7},{4,6},{5,1},{6,4},{7,3},{8,10},{9,13},{10,... | collective-permute-start | bytes 663560 | tf_op jit(solution)/shard_map/ppermute | solution.py:334
  15.8 0.0 collective-permute-done.1.refs_3_
  15.8 0.0 collective-permute-done.refs_2_
  15.8 0.4 feature_planes.1.refs_2_.refs_9_.refs_1_
  16.2 0.0 collective-permute-done.4.refs_1_
  16.3 1.4 %collective-permute-start.6 = (bf16[4,216,128]{2,1,0:T(8,128)(2,1)S(1)}, bf16[4,216,128]{2,1,0:T(8,128)(2,1)S(1)}, u32[]{:S(2)}, u32[]{:S(2)}) collective-permute-start(bf16[4,216,128]{2,1,0:T(8,128)(2,1)S(1)} %far_and_near.1.refs_2_), channel_id=1, source_target_pairs={{0,2},{1,5},{2,0},{3,7},{4,6},{5,1},{6,4},{7,3},{8,10},{9,13},{10,... | collective-permute-start | bytes 663560 | tf_op jit(solution)/shard_map/ppermute | solution.py:334
  17.7 0.9 %collective-permute-start.7 = (bf16[4,216,128]{2,1,0:T(8,128)(2,1)S(1)}, bf16[4,216,128]{2,1,0:T(8,128)(2,1)S(1)}, u32[]{:S(2)}, u32[]{:S(2)}) collective-permute-start(bf16[4,216,128]{2,1,0:T(8,128)(2,1)S(1)} %own_and_near.1.refs_1_), channel_id=1, source_target_pairs={{0,1},{1,0},{2,3},{3,2},{4,5},{5,4},{6,7},{7,6},{8,9},{9,8},{10,11... | collective-permute-start | bytes 663560 | tf_op jit(solution)/shard_map/ppermute | solution.py:329
  18.6 0.0 collective-permute-start.8
  18.6 2.2 %collective-permute-done.5.refs_3_ = bf16[4,216,128]{2,1,0:T(8,128)(2,1)S(1)} collective-permute-done((bf16[4,216,128]{2,1,0:T(8,128)(2,1)S(1)}, bf16[4,216,128]{2,1,0:T(8,128)(2,1)S(1)}, u32[]{:S(2)}, u32[]{:S(2)}) %collective-permute-start.5) | collective-permute-done | bytes 221216 | tf_op jit(solution)/shard_map/ppermute | solution.py:334
  20.8 0.3 collective-permute-start.9
  21.0 2.1 %collective-permute-done.6.refs_4_ = bf16[4,216,128]{2,1,0:T(8,128)(2,1)S(1)} collective-permute-done((bf16[4,216,128]{2,1,0:T(8,128)(2,1)S(1)}, bf16[4,216,128]{2,1,0:T(8,128)(2,1)S(1)}, u32[]{:S(2)}, u32[]{:S(2)}) %collective-permute-start.6) | collective-permute-done | bytes 221216 | tf_op jit(solution)/shard_map/ppermute | solution.py:334
  23.2 0.1 collective-permute-start.10
  23.3 1.5 %cotangent_planes.1 = (bf16[6,18,16,384]{3,2,1,0:T(8,128)(2,1)S(1)}, bf16[6,9,128,256]{3,2,1,0:T(8,128)(2,1)S(1)}) custom-call(s32[1]{0:T(128)} %bitcast.refs_0_, bf16[4,16,16,128]{3,2,1,0:T(8,128)(2,1)S(1)} %get-tuple-element.38.refs_1_, bf16[3,16,16,128]{3,2,1,0:T(8,128)(2,1)S(1)} %collective-permute-done.refs_2_, ...), custom_call_target="tpu_custom_call" | custom-call | flops 1000 | tf_op jit(solution)/shard_map/cotangent_planes/pallas_call | solution.py:31
  24.8 0.0 collective-permute-done.7.refs_5_
  24.8 0.0 collective-permute-done.8.refs_6_
  24.8 0.0 collective-permute-done.9.refs_7_
  24.8 0.0 collective-permute-done.10.refs_8_
  24.8 3.2 %hidden_and_second_grad.1 = (bf16[3456,128]{1,0:T(8,128)(2,1)S(1)}, bf16[4,16,16,128]{3,2,1,0:T(8,128)(2,1)S(1)}, f32[128,1024]{1,0:T(8,128)S(1)}, bf16[8,216,128]{2,1,0:T(8,128)(2,1)S(1)}, f32[8,216,128]{2,1,0:T(8,128)S(1)}) custom-call(s32[1]{0:T(128)} %bitcast.refs_0_, bf16[4,216,128]{2,1,0:T(8,128)(2,1)S(1)} %own_and_near.1.refs_1_, ...), custom_call_target="tpu_custom_call" | custom-call | flops 1000 | tf_op jit(solution)/shard_map/hidden_and_second_grad/pallas_call | solution.py:31
  28.0 0.5 collective-permute-start.11
  28.5 2.8 %first_grad.1 = (bf16[3456,128]{1,0:T(8,128)(2,1)S(1)}, bf16[8,216,128]{2,1,0:T(8,128)(2,1)S(1)}, f32[8,216,128]{2,1,0:T(8,128)S(1)}) custom-call(s32[1]{0:T(128)} %bitcast.refs_0_, bf16[4,216,128]{2,1,0:T(8,128)(2,1)S(1)} %own_and_near.1.refs_1_, bf16[4,216,128]{2,1,0:T(8,128)(2,1)S(1)} %far_and_near.1.refs_2_, ...), custom_call_target="tpu_custom_call" | custom-call | flops 1000 | tf_op jit(solution)/shard_map/first_grad/pallas_call | solution.py:31
  31.3 0.2 collective-permute-start.12
  31.5 0.0 collective-permute-done.11.refs_2_
  31.5 0.1 second_pair.1
  31.6 1.8 %collective-permute-start.14 = (bf16[2,216,128]{2,1,0:T(8,128)(2,1)S(1)}, bf16[2,216,128]{2,1,0:T(8,128)(2,1)S(1)}, u32[]{:S(2)}, u32[]{:S(2)}) collective-permute-start(bf16[2,216,128]{2,1,0:T(8,128)(2,1)S(1)} %get-tuple-element.47.refs_5_), channel_id=1, source_target_pairs={{0,2},{1,5},{2,0},{3,7},{4,6},{5,1},{6,4},{7,3},{8,10},{9,13},{10,... | collective-permute-start | bytes 331784 | tf_op jit(solution)/shard_map/ppermute | solution.py:334
  33.4 1.3 %hidden_planes.1.refs_5_.refs_0_ = bf16[6,18,16,384]{3,2,1,0:T(8,128)(2,1)S(1)} custom-call(s32[1]{0:T(128)} %bitcast.refs_0_, bf16[8,18,16,384]{3,2,1,0:T(8,128)(2,1)S(1)} %feature_planes.1.refs_2_.refs_9_.refs_1_, bf16[3456,128]{1,0:T(8,128)(2,1)S(1)} %get-tuple-element.40.refs_2_, bf16[4,16,16,128]{3,2,1,0:T(8,128)(2,1)S(1)} %get-tuple-element.41.refs_3_, ...), custom_call_target="tpu_custom_call" | custom-call | flops 1000 | tf_op jit(solution)/shard_map/hidden_planes/pallas_call | solution.py:31
  34.7 0.0 collective-permute-done.12.refs_2_
  34.7 0.1 first_pair.1
  34.8 0.4 collective-permute-start.13
  35.2 1.7 %collective-permute-start.16 = (bf16[4,216,128]{2,1,0:T(8,128)(2,1)S(1)}, bf16[4,216,128]{2,1,0:T(8,128)(2,1)S(1)}, u32[]{:S(2)}, u32[]{:S(2)}) collective-permute-start(bf16[4,216,128]{2,1,0:T(8,128)(2,1)S(1)} %get-tuple-element.60), channel_id=1, source_target_pairs={{0,2},{1,5},{2,0},{3,7},{4,6},{5,1},{6,4},{7,3},{8,10},{9,13},{10,... | collective-permute-start | bytes 663560 | tf_op jit(solution)/shard_map/ppermute | solution.py:334
  36.9 0.0 collective-permute-done.14.refs_2_
  37.0 2.7 %collective-permute-done.13.refs_2_ = bf16[2,216,128]{2,1,0:T(8,128)(2,1)S(1)} collective-permute-done((bf16[2,216,128]{2,1,0:T(8,128)(2,1)S(1)}, bf16[2,216,128]{2,1,0:T(8,128)(2,1)S(1)}, u32[]{:S(2)}, u32[]{:S(2)}) %collective-permute-start.13) | collective-permute-done | bytes 110624 | tf_op jit(solution)/shard_map/ppermute | solution.py:334
  39.7 1.4 %collective-permute-start.15 = (bf16[2,216,128]{2,1,0:T(8,128)(2,1)S(1)}, bf16[2,216,128]{2,1,0:T(8,128)(2,1)S(1)}, u32[]{:S(2)}, u32[]{:S(2)}) collective-permute-start(bf16[2,216,128]{2,1,0:T(8,128)(2,1)S(1)} %get-tuple-element.58.refs_3_), channel_id=1, source_target_pairs={{0,4},{1,3},{2,6},{3,1},{4,0},{5,7},{6,2},{7,5},{8,12},{9,11},{10,... | collective-permute-start | bytes 331784 | tf_op jit(solution)/shard_map/ppermute | solution.py:334
  41.1 2.0 %collective-permute-done.16.refs_2_ = bf16[4,216,128]{2,1,0:T(8,128)(2,1)S(1)} collective-permute-done((bf16[4,216,128]{2,1,0:T(8,128)(2,1)S(1)}, bf16[4,216,128]{2,1,0:T(8,128)(2,1)S(1)}, u32[]{:S(2)}, u32[]{:S(2)}) %collective-permute-start.16) | collective-permute-done | bytes 221216 | tf_op jit(solution)/shard_map/ppermute | solution.py:334
  43.2 1.6 %collective-permute-start.17 = (bf16[2,216,128]{2,1,0:T(8,128)(2,1)S(1)}, bf16[2,216,128]{2,1,0:T(8,128)(2,1)S(1)}, u32[]{:S(2)}, u32[]{:S(2)}) collective-permute-start(bf16[2,216,128]{2,1,0:T(8,128)(2,1)S(1)} %get-tuple-element.62), channel_id=1, source_target_pairs={{0,4},{1,3},{2,6},{3,1},{4,0},{5,7},{6,2},{7,5},{8,12},{9,11},{10,... | collective-permute-start | bytes 331784 | tf_op jit(solution)/shard_map/ppermute | solution.py:334
  44.8 0.0 collective-permute-done.15.refs_1_
  44.9 2.6 %collective-permute-start.18 = (bf16[2,216,128]{2,1,0:T(8,128)(2,1)S(1)}, bf16[2,216,128]{2,1,0:T(8,128)(2,1)S(1)}, u32[]{:S(2)}, u32[]{:S(2)}) collective-permute-start(bf16[2,216,128]{2,1,0:T(8,128)(2,1)S(1)} %far_last.1.refs_2_), channel_id=1, source_target_pairs={{0,8},{1,9},{2,10},{3,11},{4,12},{5,13},{6,14},{7,15},{8,0},{9,1},... | collective-permute-start | bytes 331784 | tf_op jit(solution)/shard_map/ppermute | solution.py:329
  47.4 2.2 %output_conv.1 = bf16[4,16,16,128]{3,2,1,0:T(8,128)(2,1)} custom-call(bf16[6,18,16,384]{3,2,1,0:T(8,128)(2,1)S(1)} %hidden_planes.1.refs_5_.refs_0_, bf16[3456,128]{1,0:T(8,128)(2,1)S(1)} %get-tuple-element.48.refs_1_, bf16[2,216,128]{2,1,0:T(8,128)(2,1)S(1)} %far_last.1.refs_2_), custom_call_target="tpu_custom_call" | custom-call | flops 1000 | tf_op jit(solution)/shard_map/output_conv/pallas_call | solution.py:31
  49.6 0.0 collective-permute-done.17.refs_1_
  49.6 2.2 %collective-permute-done.18.refs_2_ = bf16[2,216,128]{2,1,0:T(8,128)(2,1)S(1)} collective-permute-done((bf16[2,216,128]{2,1,0:T(8,128)(2,1)S(1)}, bf16[2,216,128]{2,1,0:T(8,128)(2,1)S(1)}, u32[]{:S(2)}, u32[]{:S(2)}) %collective-permute-start.18) | collective-permute-done | bytes 110624 | tf_op jit(solution)/shard_map/ppermute | solution.py:329
  51.8 0.7 %sum_last.1 = (f32[216,128]{1,0:T(8,128)}, f32[216,128]{1,0:T(8,128)}) custom-call(f32[2,216,128]{2,1,0:T(8,128)S(1)} %get-tuple-element.61.refs_0_, bf16[2,216,128]{2,1,0:T(8,128)(2,1)S(1)} %collective-permute-done.17.refs_1_, bf16[2,216,128]{2,1,0:T(8,128)(2,1)S(1)} %collective-permute-done.18.refs_2_), custom_call_target="tpu_custom_call" | custom-call | flops 1000 | tf_op jit(solution)/shard_map/sum_last/pallas_call | solution.py:31
  (6 shorter events, 0.2 us)
Async XLA Ops:
  1.8 9.5 %collective-permute-start.3 = (bf16[2,216,128]{2,1,0:T(8,128)(2,1)S(1)}, bf16[2,216,128]{2,1,0:T(8,128)(2,1)S(1)}, u32[]{:S(2)}, u32[]{:S(2)}) collective-permute-start(bf16[2,216,128]{2,1,0:T(8,128)(2,1)S(1)} %get-tuple-element.37.refs_0_), channel_id=1, source_target_pairs={{0,8},{1,9},{2,10},{3,11},{4,12},{5,13},{6,14},{7,15},{8,0},{9,1},... | collective-permute-start | bytes 331784 | tf_op jit(solution)/shard_map/ppermute | solution.py:329
  5.9 10.0 %collective-permute-start.1 = (bf16[3,16,16,128]{3,2,1,0:T(8,128)(2,1)S(1)}, bf16[3,16,16,128]{3,2,1,0:T(8,128)(2,1)S(1)}, u32[]{:S(2)}, u32[]{:S(2)}) collective-permute-start(bf16[3,16,16,128]{3,2,1,0:T(8,128)(2,1)S(1)} %get-tuple-element.34.refs_2_), channel_id=1, source_target_pairs={{1,2},{2,1},{3,4},{4,3},{5,6},{6,5},{7,8},{8,7},{9,10},{10,9},{11,... | collective-permute-start | bytes 589832 | tf_op jit(solution)/shard_map/ppermute | solution.py:371
  6.5 9.3 %collective-permute-start = (bf16[3,16,16,128]{3,2,1,0:T(8,128)(2,1)S(1)}, bf16[3,16,16,128]{3,2,1,0:T(8,128)(2,1)S(1)}, u32[]{:S(2)}, u32[]{:S(2)}) collective-permute-start(bf16[3,16,16,128]{3,2,1,0:T(8,128)(2,1)S(1)} %get-tuple-element.36), channel_id=1, source_target_pairs={{0,1},{1,0},{2,3},{3,2},{4,5},{5,4},{6,7},{7,6},{8,9},{9,8},{10,11... | collective-permute-start | bytes 589832 | tf_op jit(solution)/shard_map/ppermute | solution.py:329
  9.5 5.3 %collective-permute-start.2 = (bf16[2,216,128]{2,1,0:T(8,128)(2,1)S(1)}, bf16[2,216,128]{2,1,0:T(8,128)(2,1)S(1)}, u32[]{:S(2)}, u32[]{:S(2)}) collective-permute-start(bf16[2,216,128]{2,1,0:T(8,128)(2,1)S(1)} %get-tuple-element.37.refs_0_), channel_id=1, source_target_pairs={{0,4},{1,3},{2,6},{3,1},{4,0},{5,7},{6,2},{7,5},{8,12},{9,11},{10,... | collective-permute-start | bytes 331784 | tf_op jit(solution)/shard_map/ppermute | solution.py:334
  11.3 4.9 %collective-permute-start.4 = (bf16[2,216,128]{2,1,0:T(8,128)(2,1)S(1)}, bf16[2,216,128]{2,1,0:T(8,128)(2,1)S(1)}, u32[]{:S(2)}, u32[]{:S(2)}) collective-permute-start(bf16[2,216,128]{2,1,0:T(8,128)(2,1)S(1)} %collective-permute-done.3.refs_0_), channel_id=1, source_target_pairs={{0,4},{1,3},{2,6},{3,1},{4,0},{5,7},{6,2},{7,5},{8,12},{9,11},{10,... | collective-permute-start | bytes 331784 | tf_op jit(solution)/shard_map/ppermute | solution.py:334
  14.8 6.0 %collective-permute-start.5 = (bf16[4,216,128]{2,1,0:T(8,128)(2,1)S(1)}, bf16[4,216,128]{2,1,0:T(8,128)(2,1)S(1)}, u32[]{:S(2)}, u32[]{:S(2)}) collective-permute-start(bf16[4,216,128]{2,1,0:T(8,128)(2,1)S(1)} %own_and_near.1.refs_1_), channel_id=1, source_target_pairs={{0,2},{1,5},{2,0},{3,7},{4,6},{5,1},{6,4},{7,3},{8,10},{9,13},{10,... | collective-permute-start | bytes 663560 | tf_op jit(solution)/shard_map/ppermute | solution.py:334
  16.3 6.9 %collective-permute-start.6 = (bf16[4,216,128]{2,1,0:T(8,128)(2,1)S(1)}, bf16[4,216,128]{2,1,0:T(8,128)(2,1)S(1)}, u32[]{:S(2)}, u32[]{:S(2)}) collective-permute-start(bf16[4,216,128]{2,1,0:T(8,128)(2,1)S(1)} %far_and_near.1.refs_2_), channel_id=1, source_target_pairs={{0,2},{1,5},{2,0},{3,7},{4,6},{5,1},{6,4},{7,3},{8,10},{9,13},{10,... | collective-permute-start | bytes 663560 | tf_op jit(solution)/shard_map/ppermute | solution.py:334
  17.7 7.1 %collective-permute-start.7 = (bf16[4,216,128]{2,1,0:T(8,128)(2,1)S(1)}, bf16[4,216,128]{2,1,0:T(8,128)(2,1)S(1)}, u32[]{:S(2)}, u32[]{:S(2)}) collective-permute-start(bf16[4,216,128]{2,1,0:T(8,128)(2,1)S(1)} %own_and_near.1.refs_1_), channel_id=1, source_target_pairs={{0,1},{1,0},{2,3},{3,2},{4,5},{5,4},{6,7},{7,6},{8,9},{9,8},{10,11... | collective-permute-start | bytes 663560 | tf_op jit(solution)/shard_map/ppermute | solution.py:329
  18.6 6.2 %collective-permute-start.8 = (bf16[4,216,128]{2,1,0:T(8,128)(2,1)S(1)}, bf16[4,216,128]{2,1,0:T(8,128)(2,1)S(1)}, u32[]{:S(2)}, u32[]{:S(2)}) collective-permute-start(bf16[4,216,128]{2,1,0:T(8,128)(2,1)S(1)} %far_and_near.1.refs_2_), channel_id=1, source_target_pairs={{0,1},{1,0},{2,3},{3,2},{4,5},{5,4},{6,7},{7,6},{8,9},{9,8},{10,11... | collective-permute-start | bytes 663560 | tf_op jit(solution)/shard_map/ppermute | solution.py:329
  20.8 4.0 %collective-permute-start.9 = (bf16[4,216,128]{2,1,0:T(8,128)(2,1)S(1)}, bf16[4,216,128]{2,1,0:T(8,128)(2,1)S(1)}, u32[]{:S(2)}, u32[]{:S(2)}) collective-permute-start(bf16[4,216,128]{2,1,0:T(8,128)(2,1)S(1)} %collective-permute-done.5.refs_3_), channel_id=1, source_target_pairs={{0,1},{1,0},{2,3},{3,2},{4,5},{5,4},{6,7},{7,6},{8,9},{9,8},{10,11... | collective-permute-start | bytes 663560 | tf_op jit(solution)/shard_map/ppermute | solution.py:329
  23.2 1.7 %collective-permute-start.10 = (bf16[4,216,128]{2,1,0:T(8,128)(2,1)S(1)}, bf16[4,216,128]{2,1,0:T(8,128)(2,1)S(1)}, u32[]{:S(2)}, u32[]{:S(2)}) collective-permute-start(bf16[4,216,128]{2,1,0:T(8,128)(2,1)S(1)} %collective-permute-done.6.refs_4_), channel_id=1, source_target_pairs={{0,1},{1,0},{2,3},{3,2},{4,5},{5,4},{6,7},{7,6},{8,9},{9,8},{10,11... | collective-permute-start | bytes 663560 | tf_op jit(solution)/shard_map/ppermute | solution.py:329
  28.0 3.5 %collective-permute-start.11 = (bf16[8,216,128]{2,1,0:T(8,128)(2,1)S(1)}, bf16[8,216,128]{2,1,0:T(8,128)(2,1)S(1)}, u32[]{:S(2)}, u32[]{:S(2)}) collective-permute-start(bf16[8,216,128]{2,1,0:T(8,128)(2,1)S(1)} %get-tuple-element.46), channel_id=1, source_target_pairs={{0,1},{1,0},{2,3},{3,2},{4,5},{5,4},{6,7},{7,6},{8,9},{9,8},{10,11... | collective-permute-start | bytes 1327112 | tf_op jit(solution)/shard_map/ppermute | solution.py:329
  31.3 3.4 %collective-permute-start.12 = (bf16[8,216,128]{2,1,0:T(8,128)(2,1)S(1)}, bf16[8,216,128]{2,1,0:T(8,128)(2,1)S(1)}, u32[]{:S(2)}, u32[]{:S(2)}) collective-permute-start(bf16[8,216,128]{2,1,0:T(8,128)(2,1)S(1)} %get-tuple-element.49), channel_id=1, source_target_pairs={{0,1},{1,0},{2,3},{3,2},{4,5},{5,4},{6,7},{7,6},{8,9},{9,8},{10,11... | collective-permute-start | bytes 1327112 | tf_op jit(solution)/shard_map/ppermute | solution.py:329
  31.6 5.3 %collective-permute-start.14 = (bf16[2,216,128]{2,1,0:T(8,128)(2,1)S(1)}, bf16[2,216,128]{2,1,0:T(8,128)(2,1)S(1)}, u32[]{:S(2)}, u32[]{:S(2)}) collective-permute-start(bf16[2,216,128]{2,1,0:T(8,128)(2,1)S(1)} %get-tuple-element.47.refs_5_), channel_id=1, source_target_pairs={{0,2},{1,5},{2,0},{3,7},{4,6},{5,1},{6,4},{7,3},{8,10},{9,13},{10,... | collective-permute-start | bytes 331784 | tf_op jit(solution)/shard_map/ppermute | solution.py:334
  34.8 4.8 %collective-permute-start.13 = (bf16[2,216,128]{2,1,0:T(8,128)(2,1)S(1)}, bf16[2,216,128]{2,1,0:T(8,128)(2,1)S(1)}, u32[]{:S(2)}, u32[]{:S(2)}) collective-permute-start(bf16[2,216,128]{2,1,0:T(8,128)(2,1)S(1)} %get-tuple-element.53.refs_3_), channel_id=1, source_target_pairs={{0,2},{1,5},{2,0},{3,7},{4,6},{5,1},{6,4},{7,3},{8,10},{9,13},{10,... | collective-permute-start | bytes 331784 | tf_op jit(solution)/shard_map/ppermute | solution.py:334
  35.2 7.9 %collective-permute-start.16 = (bf16[4,216,128]{2,1,0:T(8,128)(2,1)S(1)}, bf16[4,216,128]{2,1,0:T(8,128)(2,1)S(1)}, u32[]{:S(2)}, u32[]{:S(2)}) collective-permute-start(bf16[4,216,128]{2,1,0:T(8,128)(2,1)S(1)} %get-tuple-element.60), channel_id=1, source_target_pairs={{0,2},{1,5},{2,0},{3,7},{4,6},{5,1},{6,4},{7,3},{8,10},{9,13},{10,... | collective-permute-start | bytes 663560 | tf_op jit(solution)/shard_map/ppermute | solution.py:334
  39.7 5.1 %collective-permute-start.15 = (bf16[2,216,128]{2,1,0:T(8,128)(2,1)S(1)}, bf16[2,216,128]{2,1,0:T(8,128)(2,1)S(1)}, u32[]{:S(2)}, u32[]{:S(2)}) collective-permute-start(bf16[2,216,128]{2,1,0:T(8,128)(2,1)S(1)} %get-tuple-element.58.refs_3_), channel_id=1, source_target_pairs={{0,4},{1,3},{2,6},{3,1},{4,0},{5,7},{6,2},{7,5},{8,12},{9,11},{10,... | collective-permute-start | bytes 331784 | tf_op jit(solution)/shard_map/ppermute | solution.py:334
  43.2 6.4 %collective-permute-start.17 = (bf16[2,216,128]{2,1,0:T(8,128)(2,1)S(1)}, bf16[2,216,128]{2,1,0:T(8,128)(2,1)S(1)}, u32[]{:S(2)}, u32[]{:S(2)}) collective-permute-start(bf16[2,216,128]{2,1,0:T(8,128)(2,1)S(1)} %get-tuple-element.62), channel_id=1, source_target_pairs={{0,4},{1,3},{2,6},{3,1},{4,0},{5,7},{6,2},{7,5},{8,12},{9,11},{10,... | collective-permute-start | bytes 331784 | tf_op jit(solution)/shard_map/ppermute | solution.py:334
  44.9 6.9 %collective-permute-start.18 = (bf16[2,216,128]{2,1,0:T(8,128)(2,1)S(1)}, bf16[2,216,128]{2,1,0:T(8,128)(2,1)S(1)}, u32[]{:S(2)}, u32[]{:S(2)}) collective-permute-start(bf16[2,216,128]{2,1,0:T(8,128)(2,1)S(1)} %far_last.1.refs_2_), channel_id=1, source_target_pairs={{0,8},{1,9},{2,10},{3,11},{4,12},{5,13},{6,14},{7,15},{8,0},{9,1},... | collective-permute-start | bytes 331784 | tf_op jit(solution)/shard_map/ppermute | solution.py:329

commit v7 on v5

--- a/solution.py
+++ b/solution.py
@@ -74,12 +74,17 @@
         write_shifted(xf_ref, p + 2, f_ref[p])
 
 
-def cotangent_kernel(me_ref, g_ref, core_ref, chip_ref, xg_ref, gt_ref):
-    planes, height, width, channels = g_ref.shape
+def cotangent_kernel(me_ref, g_ref, core_ref, chip_ref, xg_ref):
+    planes = g_ref.shape[0]
     for ref, place in sides(me_ref, core_ref, chip_ref, planes):
         write_shifted(xg_ref, place(0, 1), ref[2])
     for p in range(planes):
         write_shifted(xg_ref, p + 1, g_ref[p])
+
+
+def transposed_kernel(xg_ref, gt_ref):
+    planes, _, channels, _ = gt_ref.shape
+    height, width = xg_ref.shape[1] - 2, xg_ref.shape[2]
 
     def transposed(p, _):
         for b in range(3):
@@ -88,7 +93,7 @@
                 gt_ref[p, b * 3 + c] = block.reshape(height * width, channels).T
         return 0
 
-    lax.fori_loop(0, planes + 2, transposed, 0)
+    lax.fori_loop(0, planes, transposed, 0)
 
 
 def copy_all(moves, sems):
@@ -172,8 +177,14 @@
         return sum(term(a, 1, taps[a]) for a in range(3))
     channels = taps[0].shape[1]
     middle = term(1, planes - 1, jnp.concatenate(taps[:2], axis=1))
-    late = term(2, planes - 2, taps[2])
-    ends = (term(0, 1, taps[0]), term(planes + 1, 1, taps[2]))
+    late = jnp.dot(
+        jnp.concatenate(
+            [window(ref, first + 2, planes - 2), window(ref, first + planes + 1, 1)], axis=0
+        ),
+        taps[2],
+        preferred_element_type=F32,
+    )
+    ends = (term(0, 1, taps[0]), late[(planes - 2) * cells :])
     last = term(planes, 1, jnp.concatenate(taps[1:], axis=1))
     parts = [[] for _ in range(planes)]
     parts[0].append(ends[0])
@@ -382,24 +393,30 @@
         near = swap_mixed(far, count, 4, 2)
         away = joined([far, near], "far_and_near", [xf])
         cross_away = swap_mixed(away, count, 2, 4)
-        wait_for = [cross_away]
+        wait_for = [cross, cross_away]
         pieces = [close, away, cross, cross_away]
-        pieces += [swap(piece, count, 1) for piece in pieces]
     else:
         pieces = [
             lax.all_gather(shard, "slab", axis=0, tiled=True)
             for shard in (filters_first, filters_second)
         ]
-    xg, gt = local_call(
+    (xg,) = local_call(
         cotangent_kernel,
         "cotangent_planes",
-        [
-            like((planes + 2, height + 2, width, 3 * channels), BF16),
-            like((planes + 2, 9, channels, height * width), BF16),
-        ],
+        [like((planes + 2, height + 2, width, 3 * channels), BF16)],
         [me, cotangent, *edges],
         scalars=1,
-        wait_for=wait_for,
+        wait_for=wait_for[:1],
+    )
+    if direct:
+        cross_sent = joined([cross], "cross", [xg])
+        pieces += [swap(piece, count, 1) for piece in (close, away, cross_sent, cross_away)]
+    (gt,) = local_call(
+        transposed_kernel,
+        "cotangent_windows",
+        [like((planes + 2, 9, channels, height * width), BF16)],
+        [xg],
+        wait_for=wait_for[1:],
     )
     terms = [like((8, shard_rows, channels), BF16), like((8, shard_rows, channels), F32)]
     total = pltpu.VMEM((taps, channels), F32)
@@ -415,6 +432,7 @@
         [place, *pieces, xf, xg],
         scratch=[total],
         scalars=1,
+        wait_for=[gt],
     )
     bank_second, send_first, keep_first = local_call(
         functools.partial(second_kernel, len(pieces), order),

time: 52.8 us -> 52.5 us (level)
  waiting for transfers between devices: 20.1 us -> 19 us
  starting transfers between devices: 17.1 us -> 18 us
    ppermute x8, waiting for transfers between devices: 15.8 us -> 14.5 us  [swap_mixed(): return lax.ppermute(value, 'slab', pairs)]
    ppermute x9, starting transfers between devices: 7.14 us -> 7.77 us  [swap(): lax.ppermute(value, 'slab', [(i, i ^ distance) for i in range(count)])]
    pallas_call x13 -> x15, Pallas kernels: 12.4 us -> 12.5 us  [local_call(): pl.pallas_call(body, out_shape=list(outs), in_specs=[pl.BlockSpec(memory_...]
where the time goes in v7:
time: 52.5 us; the launch traced here: 52.4 us
  waiting for transfers between devices  19 us (36%)
  starting transfers between devices  18 us (34%)
  Pallas kernels  14.7 us (28%)
  between operations  0.78 us (1%)
    ppermute x8, waiting for transfers between devices, swap_mixed(): return lax.ppermute(value, 'slab', pairs)  14.5 us
    pallas_call x15, Pallas kernels, local_call(): pl.pallas_call(body, out_shape=list(outs), in_specs=[pl.BlockSpec(memory_...  12.5 us
    ppermute x8, starting transfers between devices, swap_mixed(): return lax.ppermute(value, 'slab', pairs)  9.55 us
    ppermute x9, starting transfers between devices, swap(): lax.ppermute(value, 'slab', [(i, i ^ distance) for i in range(count)])  7.77 us
    ppermute x9, waiting for transfers between devices, swap(): lax.ppermute(value, 'slab', [(i, i ^ distance) for i in range(count)])  4.41 us
    pallas_call x2, Pallas kernels, from_hbm(): pl.pallas_call(body, out_shape=outs, in_specs=[pl.BlockSpec(memory_space=...  2.2 us
  transfers between devices with their start and end apart: 18, of which 11 were waited for; matrix products, arithmetic and copies ran while one was open for 0% of the time, Pallas kernels for 18%

profile of v7, /device:TPU:0, one launch (start us, length us, event | category | flops | bytes accessed | tf_op | source)
XLA Modules:
  0.0 52.4 jit_solution(530173000421368944)
XLA Ops:
  0.6 1.1 %load_shards_and_edges.1 = (bf16[2,216,128]{2,1,0:T(8,128)(2,1)S(1)}, bf16[3,16,16,128]{3,2,1,0:T(8,128)(2,1)S(1)}, bf16[3,16,16,128]{3,2,1,0:T(8,128)(2,1)S(1)}) custom-call(s32[1]{0:T(128)} %bitcast.refs_0_, bf16[4,16,16,128]{3,2,1,0:T(8,128)(2,1)} %refs_0_.1, bf16[4,16,16,128]{3,2,1,0:T(8,128)(2,1)} %refs_1_.3, bf16[216,128]{1,0:T(8,128)(2,1)} %refs_3_.1, ...), custom_call_target="tpu_custom_call" | custom-call | flops 1000 | tf_op jit(solution)/shard_map/load_shards_and_edges/pallas_call | solution.py:133
  1.8 4.1 %collective-permute-start.3 = (bf16[2,216,128]{2,1,0:T(8,128)(2,1)S(1)}, bf16[2,216,128]{2,1,0:T(8,128)(2,1)S(1)}, u32[]{:S(2)}, u32[]{:S(2)}) collective-permute-start(bf16[2,216,128]{2,1,0:T(8,128)(2,1)S(1)} %get-tuple-element.29.refs_0_), channel_id=1, source_target_pairs={{0,8},{1,9},{2,10},{3,11},{4,12},{5,13},{6,14},{7,15},{8,0},{9,1},... | collective-permute-start | bytes 331784 | tf_op jit(solution)/shard_map/ppermute | solution.py:336
  5.9 0.0 collective-permute-start
  5.9 0.7 %collective-permute-start.1 = (bf16[3,16,16,128]{3,2,1,0:T(8,128)(2,1)S(1)}, bf16[3,16,16,128]{3,2,1,0:T(8,128)(2,1)S(1)}, u32[]{:S(2)}, u32[]{:S(2)}) collective-permute-start(bf16[3,16,16,128]{3,2,1,0:T(8,128)(2,1)S(1)} %get-tuple-element.26.refs_2_), channel_id=1, source_target_pairs={{1,2},{2,1},{3,4},{4,3},{5,6},{6,5},{7,8},{8,7},{9,10},{10,9},{11,... | collective-permute-start | bytes 589832 | tf_op jit(solution)/shard_map/ppermute | solution.py:378
  6.5 4.4 %collective-permute-start.2 = (bf16[2,216,128]{2,1,0:T(8,128)(2,1)S(1)}, bf16[2,216,128]{2,1,0:T(8,128)(2,1)S(1)}, u32[]{:S(2)}, u32[]{:S(2)}) collective-permute-start(bf16[2,216,128]{2,1,0:T(8,128)(2,1)S(1)} %get-tuple-element.29.refs_0_), channel_id=1, source_target_pairs={{0,4},{1,3},{2,6},{3,1},{4,0},{5,7},{6,2},{7,5},{8,12},{9,11},{10,... | collective-permute-start | bytes 331784 | tf_op jit(solution)/shard_map/ppermute | solution.py:341
  10.9 0.4 collective-permute-done.3.refs_0_
  11.3 0.7 %collective-permute-start.4 = (bf16[2,216,128]{2,1,0:T(8,128)(2,1)S(1)}, bf16[2,216,128]{2,1,0:T(8,128)(2,1)S(1)}, u32[]{:S(2)}, u32[]{:S(2)}) collective-permute-start(bf16[2,216,128]{2,1,0:T(8,128)(2,1)S(1)} %collective-permute-done.3.refs_0_), channel_id=1, source_target_pairs={{0,4},{1,3},{2,6},{3,1},{4,0},{5,7},{6,2},{7,5},{8,12},{9,11},{10,... | collective-permute-start | bytes 331784 | tf_op jit(solution)/shard_map/ppermute | solution.py:341
  12.0 1.1 %load.1 = (bf16[4,16,16,128]{3,2,1,0:T(8,128)(2,1)S(1)}, bf16[4,16,16,128]{3,2,1,0:T(8,128)(2,1)S(1)}) custom-call(bf16[4,16,16,128]{3,2,1,0:T(8,128)(2,1)} %refs_0_.1, bf16[4,16,16,128]{3,2,1,0:T(8,128)(2,1)} %refs_1_.3, bf16[3,16,16,128]{3,2,1,0:T(8,128)(2,1)S(1)} %get-tuple-element.26.refs_2_), custom_call_target="tpu_custom_call" | custom-call | flops 1000 | tf_op jit(solution)/shard_map/load/pallas_call | solution.py:133
  13.1 2.6 %collective-permute-done.2.refs_1_ = bf16[2,216,128]{2,1,0:T(8,128)(2,1)S(1)} collective-permute-done((bf16[2,216,128]{2,1,0:T(8,128)(2,1)S(1)}, bf16[2,216,128]{2,1,0:T(8,128)(2,1)S(1)}, u32[]{:S(2)}, u32[]{:S(2)}) %collective-permute-start.2) | collective-permute-done | bytes 110624 | tf_op jit(solution)/shard_map/ppermute | solution.py:341
  15.7 0.1 collective-permute-start.5
  15.8 0.0 collective-permute-done.refs_2_
  15.8 0.0 collective-permute-done.1.refs_3_
  15.8 0.4 feature_planes.1.refs_2_.refs_9_.refs_1_
  16.2 0.7 %collective-permute-done.4.refs_1_ = bf16[2,216,128]{2,1,0:T(8,128)(2,1)S(1)} collective-permute-done((bf16[2,216,128]{2,1,0:T(8,128)(2,1)S(1)}, bf16[2,216,128]{2,1,0:T(8,128)(2,1)S(1)}, u32[]{:S(2)}, u32[]{:S(2)}) %collective-permute-start.4) | collective-permute-done | bytes 110624 | tf_op jit(solution)/shard_map/ppermute | solution.py:341
  16.9 1.4 %collective-permute-start.6 = (bf16[4,216,128]{2,1,0:T(8,128)(2,1)S(1)}, bf16[4,216,128]{2,1,0:T(8,128)(2,1)S(1)}, u32[]{:S(2)}, u32[]{:S(2)}) collective-permute-start(bf16[4,216,128]{2,1,0:T(8,128)(2,1)S(1)} %far_and_near.1.refs_2_), channel_id=1, source_target_pairs={{0,2},{1,5},{2,0},{3,7},{4,6},{5,1},{6,4},{7,3},{8,10},{9,13},{10,... | collective-permute-start | bytes 663560 | tf_op jit(solution)/shard_map/ppermute | solution.py:341
  18.3 1.4 %collective-permute-start.7 = (bf16[4,216,128]{2,1,0:T(8,128)(2,1)S(1)}, bf16[4,216,128]{2,1,0:T(8,128)(2,1)S(1)}, u32[]{:S(2)}, u32[]{:S(2)}) collective-permute-start(bf16[4,216,128]{2,1,0:T(8,128)(2,1)S(1)} %own_and_near.1.refs_1_), channel_id=1, source_target_pairs={{0,1},{1,0},{2,3},{3,2},{4,5},{5,4},{6,7},{7,6},{8,9},{9,8},{10,11... | collective-permute-start | bytes 663560 | tf_op jit(solution)/shard_map/ppermute | solution.py:336
  19.7 2.0 %collective-permute-done.5.refs_4_.refs_0_.refs_3_ = bf16[4,216,128]{2,1,0:T(8,128)(2,1)S(1)} collective-permute-done((bf16[4,216,128]{2,1,0:T(8,128)(2,1)S(1)}, bf16[4,216,128]{2,1,0:T(8,128)(2,1)S(1)}, u32[]{:S(2)}, u32[]{:S(2)}) %collective-permute-start.5) | collective-permute-done | bytes 221216 | tf_op jit(solution)/shard_map/ppermute | solution.py:341
  21.7 0.3 cotangent_planes.1.refs_1_.refs_0_.refs_10_
  22.0 0.1 collective-permute-start.8
  22.1 0.6 %collective-permute-start.9 = (bf16[4,216,128]{2,1,0:T(8,128)(2,1)S(1)}, bf16[4,216,128]{2,1,0:T(8,128)(2,1)S(1)}, u32[]{:S(2)}, u32[]{:S(2)}) collective-permute-start(bf16[4,216,128]{2,1,0:T(8,128)(2,1)S(1)} %cross.1), channel_id=1, source_target_pairs={{0,1},{1,0},{2,3},{3,2},{4,5},{5,4},{6,7},{7,6},{8,9},{9,8},{10,11... | collective-permute-start | bytes 663560 | tf_op jit(solution)/shard_map/ppermute | solution.py:336
  22.7 1.4 %collective-permute-done.6.refs_1_.refs_4_ = bf16[4,216,128]{2,1,0:T(8,128)(2,1)S(1)} collective-permute-done((bf16[4,216,128]{2,1,0:T(8,128)(2,1)S(1)}, bf16[4,216,128]{2,1,0:T(8,128)(2,1)S(1)}, u32[]{:S(2)}, u32[]{:S(2)}) %collective-permute-start.6) | collective-permute-done | bytes 221216 | tf_op jit(solution)/shard_map/ppermute | solution.py:341
  24.1 0.0 collective-permute-start.10
  24.1 1.2 %cotangent_windows.1.refs_11_.refs_10_ = bf16[6,9,128,256]{3,2,1,0:T(8,128)(2,1)S(1)} custom-call(bf16[6,18,16,384]{3,2,1,0:T(8,128)(2,1)S(1)} %cotangent_planes.1.refs_1_.refs_0_.refs_10_, bf16[4,216,128]{2,1,0:T(8,128)(2,1)S(1)} %collective-permute-done.6.refs_1_.refs_4_), custom_call_target="tpu_custom_call" | custom-call | flops 1000 | tf_op jit(solution)/shard_map/cotangent_windows/pallas_call | solution.py:31
  25.3 0.0 collective-permute-done.7.refs_5_
  25.4 0.0 collective-permute-done.8.refs_6_
  25.4 0.0 collective-permute-done.9.refs_7_
  25.4 0.2 collective-permute-done.10.refs_8_
  25.6 3.1 %hidden_and_second_grad.1 = (bf16[3456,128]{1,0:T(8,128)(2,1)S(1)}, bf16[4,16,16,128]{3,2,1,0:T(8,128)(2,1)S(1)}, f32[128,1024]{1,0:T(8,128)S(1)}, bf16[8,216,128]{2,1,0:T(8,128)(2,1)S(1)}, f32[8,216,128]{2,1,0:T(8,128)S(1)}) custom-call(s32[1]{0:T(128)} %bitcast.refs_0_, bf16[4,216,128]{2,1,0:T(8,128)(2,1)S(1)} %own_and_near.1.refs_1_, ...), custom_call_target="tpu_custom_call" | custom-call | flops 1000 | tf_op jit(solution)/shard_map/hidden_and_second_grad/pallas_call | solution.py:31
  28.7 0.4 collective-permute-start.11
  29.1 2.8 %first_grad.1 = (bf16[3456,128]{1,0:T(8,128)(2,1)S(1)}, bf16[8,216,128]{2,1,0:T(8,128)(2,1)S(1)}, f32[8,216,128]{2,1,0:T(8,128)S(1)}) custom-call(s32[1]{0:T(128)} %bitcast.refs_0_, bf16[4,216,128]{2,1,0:T(8,128)(2,1)S(1)} %own_and_near.1.refs_1_, bf16[4,216,128]{2,1,0:T(8,128)(2,1)S(1)} %far_and_near.1.refs_2_, ...), custom_call_target="tpu_custom_call" | custom-call | flops 1000 | tf_op jit(solution)/shard_map/first_grad/pallas_call | solution.py:31
  32.0 0.2 collective-permute-start.12
  32.2 0.0 collective-permute-done.11.refs_5_.refs_4_
  32.2 1.3 %hidden_planes.1.refs_5_.refs_0_ = bf16[6,18,16,384]{3,2,1,0:T(8,128)(2,1)S(1)} custom-call(s32[1]{0:T(128)} %bitcast.refs_0_, bf16[8,18,16,384]{3,2,1,0:T(8,128)(2,1)S(1)} %feature_planes.1.refs_2_.refs_9_.refs_1_, bf16[3456,128]{1,0:T(8,128)(2,1)S(1)} %get-tuple-element.31.refs_2_, bf16[4,16,16,128]{3,2,1,0:T(8,128)(2,1)S(1)} %get-tuple-element.32.refs_3_, ...), custom_call_target="tpu_custom_call" | custom-call | flops 1000 | tf_op jit(solution)/shard_map/hidden_planes/pallas_call | solution.py:31
  33.5 0.3 collective-permute-done.12.refs_3_
  33.8 0.2 sum_pair.1
  34.0 0.6 %collective-permute-start.13 = (bf16[4,216,128]{2,1,0:T(8,128)(2,1)S(1)}, bf16[4,216,128]{2,1,0:T(8,128)(2,1)S(1)}, u32[]{:S(2)}, u32[]{:S(2)}) collective-permute-start(bf16[4,216,128]{2,1,0:T(8,128)(2,1)S(1)} %get-tuple-element.40), channel_id=1, source_target_pairs={{0,2},{1,5},{2,0},{3,7},{4,6},{5,1},{6,4},{7,3},{8,10},{9,13},{10,... | collective-permute-start | bytes 663560 | tf_op jit(solution)/shard_map/ppermute | solution.py:341
  34.6 1.5 %collective-permute-start.15 = (bf16[4,216,128]{2,1,0:T(8,128)(2,1)S(1)}, bf16[4,216,128]{2,1,0:T(8,128)(2,1)S(1)}, u32[]{:S(2)}, u32[]{:S(2)}) collective-permute-start(bf16[4,216,128]{2,1,0:T(8,128)(2,1)S(1)} %get-tuple-element.44), channel_id=1, source_target_pairs={{0,2},{1,5},{2,0},{3,7},{4,6},{5,1},{6,4},{7,3},{8,10},{9,13},{10,... | collective-permute-start | bytes 663560 | tf_op jit(solution)/shard_map/ppermute | solution.py:341
  36.1 3.9 %collective-permute-done.13.refs_2_ = bf16[4,216,128]{2,1,0:T(8,128)(2,1)S(1)} collective-permute-done((bf16[4,216,128]{2,1,0:T(8,128)(2,1)S(1)}, bf16[4,216,128]{2,1,0:T(8,128)(2,1)S(1)}, u32[]{:S(2)}, u32[]{:S(2)}) %collective-permute-start.13) | collective-permute-done | bytes 221216 | tf_op jit(solution)/shard_map/ppermute | solution.py:341
  40.1 0.5 collective-permute-start.14
  40.6 2.1 %collective-permute-done.15.refs_2_ = bf16[4,216,128]{2,1,0:T(8,128)(2,1)S(1)} collective-permute-done((bf16[4,216,128]{2,1,0:T(8,128)(2,1)S(1)}, bf16[4,216,128]{2,1,0:T(8,128)(2,1)S(1)}, u32[]{:S(2)}, u32[]{:S(2)}) %collective-permute-start.15) | collective-permute-done | bytes 221216 | tf_op jit(solution)/shard_map/ppermute | solution.py:341
  42.6 0.1 own_near.1
  42.7 0.4 collective-permute-start.16
  43.1 1.8 %collective-permute-done.14.refs_1_ = bf16[2,216,128]{2,1,0:T(8,128)(2,1)S(1)} collective-permute-done((bf16[2,216,128]{2,1,0:T(8,128)(2,1)S(1)}, bf16[2,216,128]{2,1,0:T(8,128)(2,1)S(1)}, u32[]{:S(2)}, u32[]{:S(2)}) %collective-permute-start.14) | collective-permute-done | bytes 110624 | tf_op jit(solution)/shard_map/ppermute | solution.py:341
  44.9 1.0 %collective-permute-start.17 = (bf16[2,216,128]{2,1,0:T(8,128)(2,1)S(1)}, bf16[2,216,128]{2,1,0:T(8,128)(2,1)S(1)}, u32[]{:S(2)}, u32[]{:S(2)}) collective-permute-start(bf16[2,216,128]{2,1,0:T(8,128)(2,1)S(1)} %far_last.1.refs_2_), channel_id=1, source_target_pairs={{0,8},{1,9},{2,10},{3,11},{4,12},{5,13},{6,14},{7,15},{8,0},{9,1},... | collective-permute-start | bytes 331784 | tf_op jit(solution)/shard_map/ppermute | solution.py:336
  45.9 2.2 %output_conv.1 = bf16[4,16,16,128]{3,2,1,0:T(8,128)(2,1)} custom-call(bf16[6,18,16,384]{3,2,1,0:T(8,128)(2,1)S(1)} %hidden_planes.1.refs_5_.refs_0_, bf16[3456,128]{1,0:T(8,128)(2,1)S(1)} %get-tuple-element.36.refs_1_, bf16[2,216,128]{2,1,0:T(8,128)(2,1)S(1)} %far_last.1.refs_2_), custom_call_target="tpu_custom_call" | custom-call | flops 1000 | tf_op jit(solution)/shard_map/output_conv/pallas_call | solution.py:31
  48.1 0.0 collective-permute-done.16.refs_1_
  48.1 3.5 %collective-permute-done.17.refs_2_ = bf16[2,216,128]{2,1,0:T(8,128)(2,1)S(1)} collective-permute-done((bf16[2,216,128]{2,1,0:T(8,128)(2,1)S(1)}, bf16[2,216,128]{2,1,0:T(8,128)(2,1)S(1)}, u32[]{:S(2)}, u32[]{:S(2)}) %collective-permute-start.17) | collective-permute-done | bytes 110624 | tf_op jit(solution)/shard_map/ppermute | solution.py:336
  51.7 0.7 %sum_last.1 = (f32[216,128]{1,0:T(8,128)}, f32[216,128]{1,0:T(8,128)}) custom-call(f32[2,216,128]{2,1,0:T(8,128)S(1)} %get-tuple-element.45.refs_0_, bf16[2,216,128]{2,1,0:T(8,128)(2,1)S(1)} %collective-permute-done.16.refs_1_, bf16[2,216,128]{2,1,0:T(8,128)(2,1)S(1)} %collective-permute-done.17.refs_2_), custom_call_target="tpu_custom_call" | custom-call | flops 1000 | tf_op jit(solution)/shard_map/sum_last/pallas_call | solution.py:31
  (5 shorter events, 0.1 us)
Async XLA Ops:
  1.8 9.5 %collective-permute-start.3 = (bf16[2,216,128]{2,1,0:T(8,128)(2,1)S(1)}, bf16[2,216,128]{2,1,0:T(8,128)(2,1)S(1)}, u32[]{:S(2)}, u32[]{:S(2)}) collective-permute-start(bf16[2,216,128]{2,1,0:T(8,128)(2,1)S(1)} %get-tuple-element.29.refs_0_), channel_id=1, source_target_pairs={{0,8},{1,9},{2,10},{3,11},{4,12},{5,13},{6,14},{7,15},{8,0},{9,1},... | collective-permute-start | bytes 331784 | tf_op jit(solution)/shard_map/ppermute | solution.py:336
  5.9 10.0 %collective-permute-start = (bf16[3,16,16,128]{3,2,1,0:T(8,128)(2,1)S(1)}, bf16[3,16,16,128]{3,2,1,0:T(8,128)(2,1)S(1)}, u32[]{:S(2)}, u32[]{:S(2)}) collective-permute-start(bf16[3,16,16,128]{3,2,1,0:T(8,128)(2,1)S(1)} %get-tuple-element.28), channel_id=1, source_target_pairs={{0,1},{1,0},{2,3},{3,2},{4,5},{5,4},{6,7},{7,6},{8,9},{9,8},{10,11... | collective-permute-start | bytes 589832 | tf_op jit(solution)/shard_map/ppermute | solution.py:336
  5.9 10.0 %collective-permute-start.1 = (bf16[3,16,16,128]{3,2,1,0:T(8,128)(2,1)S(1)}, bf16[3,16,16,128]{3,2,1,0:T(8,128)(2,1)S(1)}, u32[]{:S(2)}, u32[]{:S(2)}) collective-permute-start(bf16[3,16,16,128]{3,2,1,0:T(8,128)(2,1)S(1)} %get-tuple-element.26.refs_2_), channel_id=1, source_target_pairs={{1,2},{2,1},{3,4},{4,3},{5,6},{6,5},{7,8},{8,7},{9,10},{10,9},{11,... | collective-permute-start | bytes 589832 | tf_op jit(solution)/shard_map/ppermute | solution.py:378
  6.5 9.2 %collective-permute-start.2 = (bf16[2,216,128]{2,1,0:T(8,128)(2,1)S(1)}, bf16[2,216,128]{2,1,0:T(8,128)(2,1)S(1)}, u32[]{:S(2)}, u32[]{:S(2)}) collective-permute-start(bf16[2,216,128]{2,1,0:T(8,128)(2,1)S(1)} %get-tuple-element.29.refs_0_), channel_id=1, source_target_pairs={{0,4},{1,3},{2,6},{3,1},{4,0},{5,7},{6,2},{7,5},{8,12},{9,11},{10,... | collective-permute-start | bytes 331784 | tf_op jit(solution)/shard_map/ppermute | solution.py:341
  11.3 5.6 %collective-permute-start.4 = (bf16[2,216,128]{2,1,0:T(8,128)(2,1)S(1)}, bf16[2,216,128]{2,1,0:T(8,128)(2,1)S(1)}, u32[]{:S(2)}, u32[]{:S(2)}) collective-permute-start(bf16[2,216,128]{2,1,0:T(8,128)(2,1)S(1)} %collective-permute-done.3.refs_0_), channel_id=1, source_target_pairs={{0,4},{1,3},{2,6},{3,1},{4,0},{5,7},{6,2},{7,5},{8,12},{9,11},{10,... | collective-permute-start | bytes 331784 | tf_op jit(solution)/shard_map/ppermute | solution.py:341
  15.7 6.0 %collective-permute-start.5 = (bf16[4,216,128]{2,1,0:T(8,128)(2,1)S(1)}, bf16[4,216,128]{2,1,0:T(8,128)(2,1)S(1)}, u32[]{:S(2)}, u32[]{:S(2)}) collective-permute-start(bf16[4,216,128]{2,1,0:T(8,128)(2,1)S(1)} %own_and_near.1.refs_1_), channel_id=1, source_target_pairs={{0,2},{1,5},{2,0},{3,7},{4,6},{5,1},{6,4},{7,3},{8,10},{9,13},{10,... | collective-permute-start | bytes 663560 | tf_op jit(solution)/shard_map/ppermute | solution.py:341
  16.9 7.2 %collective-permute-start.6 = (bf16[4,216,128]{2,1,0:T(8,128)(2,1)S(1)}, bf16[4,216,128]{2,1,0:T(8,128)(2,1)S(1)}, u32[]{:S(2)}, u32[]{:S(2)}) collective-permute-start(bf16[4,216,128]{2,1,0:T(8,128)(2,1)S(1)} %far_and_near.1.refs_2_), channel_id=1, source_target_pairs={{0,2},{1,5},{2,0},{3,7},{4,6},{5,1},{6,4},{7,3},{8,10},{9,13},{10,... | collective-permute-start | bytes 663560 | tf_op jit(solution)/shard_map/ppermute | solution.py:341
  18.3 7.0 %collective-permute-start.7 = (bf16[4,216,128]{2,1,0:T(8,128)(2,1)S(1)}, bf16[4,216,128]{2,1,0:T(8,128)(2,1)S(1)}, u32[]{:S(2)}, u32[]{:S(2)}) collective-permute-start(bf16[4,216,128]{2,1,0:T(8,128)(2,1)S(1)} %own_and_near.1.refs_1_), channel_id=1, source_target_pairs={{0,1},{1,0},{2,3},{3,2},{4,5},{5,4},{6,7},{7,6},{8,9},{9,8},{10,11... | collective-permute-start | bytes 663560 | tf_op jit(solution)/shard_map/ppermute | solution.py:336
  22.0 3.3 %collective-permute-start.8 = (bf16[4,216,128]{2,1,0:T(8,128)(2,1)S(1)}, bf16[4,216,128]{2,1,0:T(8,128)(2,1)S(1)}, u32[]{:S(2)}, u32[]{:S(2)}) collective-permute-start(bf16[4,216,128]{2,1,0:T(8,128)(2,1)S(1)} %far_and_near.1.refs_2_), channel_id=1, source_target_pairs={{0,1},{1,0},{2,3},{3,2},{4,5},{5,4},{6,7},{7,6},{8,9},{9,8},{10,11... | collective-permute-start | bytes 663560 | tf_op jit(solution)/shard_map/ppermute | solution.py:336
  22.1 3.2 %collective-permute-start.9 = (bf16[4,216,128]{2,1,0:T(8,128)(2,1)S(1)}, bf16[4,216,128]{2,1,0:T(8,128)(2,1)S(1)}, u32[]{:S(2)}, u32[]{:S(2)}) collective-permute-start(bf16[4,216,128]{2,1,0:T(8,128)(2,1)S(1)} %cross.1), channel_id=1, source_target_pairs={{0,1},{1,0},{2,3},{3,2},{4,5},{5,4},{6,7},{7,6},{8,9},{9,8},{10,11... | collective-permute-start | bytes 663560 | tf_op jit(solution)/shard_map/ppermute | solution.py:336
  24.1 1.5 %collective-permute-start.10 = (bf16[4,216,128]{2,1,0:T(8,128)(2,1)S(1)}, bf16[4,216,128]{2,1,0:T(8,128)(2,1)S(1)}, u32[]{:S(2)}, u32[]{:S(2)}) collective-permute-start(bf16[4,216,128]{2,1,0:T(8,128)(2,1)S(1)} %collective-permute-done.6.refs_1_.refs_4_), channel_id=1, source_target_pairs={{0,1},{1,0},{2,3},{3,2},{4,5},{5,4},{6,7},{7,6},{8,9},{9,8},{10,11... | collective-permute-start | bytes 663560 | tf_op jit(solution)/shard_map/ppermute | solution.py:336
  28.7 3.5 %collective-permute-start.11 = (bf16[8,216,128]{2,1,0:T(8,128)(2,1)S(1)}, bf16[8,216,128]{2,1,0:T(8,128)(2,1)S(1)}, u32[]{:S(2)}, u32[]{:S(2)}) collective-permute-start(bf16[8,216,128]{2,1,0:T(8,128)(2,1)S(1)} %get-tuple-element.35), channel_id=1, source_target_pairs={{0,1},{1,0},{2,3},{3,2},{4,5},{5,4},{6,7},{7,6},{8,9},{9,8},{10,11... | collective-permute-start | bytes 1327112 | tf_op jit(solution)/shard_map/ppermute | solution.py:336
  32.0 1.9 %collective-permute-start.12 = (bf16[8,216,128]{2,1,0:T(8,128)(2,1)S(1)}, bf16[8,216,128]{2,1,0:T(8,128)(2,1)S(1)}, u32[]{:S(2)}, u32[]{:S(2)}) collective-permute-start(bf16[8,216,128]{2,1,0:T(8,128)(2,1)S(1)} %get-tuple-element.38), channel_id=1, source_target_pairs={{0,1},{1,0},{2,3},{3,2},{4,5},{5,4},{6,7},{7,6},{8,9},{9,8},{10,11... | collective-permute-start | bytes 1327112 | tf_op jit(solution)/shard_map/ppermute | solution.py:336
  34.0 6.0 %collective-permute-start.13 = (bf16[4,216,128]{2,1,0:T(8,128)(2,1)S(1)}, bf16[4,216,128]{2,1,0:T(8,128)(2,1)S(1)}, u32[]{:S(2)}, u32[]{:S(2)}) collective-permute-start(bf16[4,216,128]{2,1,0:T(8,128)(2,1)S(1)} %get-tuple-element.40), channel_id=1, source_target_pairs={{0,2},{1,5},{2,0},{3,7},{4,6},{5,1},{6,4},{7,3},{8,10},{9,13},{10,... | collective-permute-start | bytes 663560 | tf_op jit(solution)/shard_map/ppermute | solution.py:341
  34.6 8.0 %collective-permute-start.15 = (bf16[4,216,128]{2,1,0:T(8,128)(2,1)S(1)}, bf16[4,216,128]{2,1,0:T(8,128)(2,1)S(1)}, u32[]{:S(2)}, u32[]{:S(2)}) collective-permute-start(bf16[4,216,128]{2,1,0:T(8,128)(2,1)S(1)} %get-tuple-element.44), channel_id=1, source_target_pairs={{0,2},{1,5},{2,0},{3,7},{4,6},{5,1},{6,4},{7,3},{8,10},{9,13},{10,... | collective-permute-start | bytes 663560 | tf_op jit(solution)/shard_map/ppermute | solution.py:341
  40.1 4.8 %collective-permute-start.14 = (bf16[2,216,128]{2,1,0:T(8,128)(2,1)S(1)}, bf16[2,216,128]{2,1,0:T(8,128)(2,1)S(1)}, u32[]{:S(2)}, u32[]{:S(2)}) collective-permute-start(bf16[2,216,128]{2,1,0:T(8,128)(2,1)S(1)} %get-tuple-element.42.refs_3_), channel_id=1, source_target_pairs={{0,4},{1,3},{2,6},{3,1},{4,0},{5,7},{6,2},{7,5},{8,12},{9,11},{10,... | collective-permute-start | bytes 331784 | tf_op jit(solution)/shard_map/ppermute | solution.py:341
  42.7 5.4 %collective-permute-start.16 = (bf16[2,216,128]{2,1,0:T(8,128)(2,1)S(1)}, bf16[2,216,128]{2,1,0:T(8,128)(2,1)S(1)}, u32[]{:S(2)}, u32[]{:S(2)}) collective-permute-start(bf16[2,216,128]{2,1,0:T(8,128)(2,1)S(1)} %get-tuple-element.46), channel_id=1, source_target_pairs={{0,4},{1,3},{2,6},{3,1},{4,0},{5,7},{6,2},{7,5},{8,12},{9,11},{10,... | collective-permute-start | bytes 331784 | tf_op jit(solution)/shard_map/ppermute | solution.py:341
  44.9 6.8 %collective-permute-start.17 = (bf16[2,216,128]{2,1,0:T(8,128)(2,1)S(1)}, bf16[2,216,128]{2,1,0:T(8,128)(2,1)S(1)}, u32[]{:S(2)}, u32[]{:S(2)}) collective-permute-start(bf16[2,216,128]{2,1,0:T(8,128)(2,1)S(1)} %far_last.1.refs_2_), channel_id=1, source_target_pairs={{0,8},{1,9},{2,10},{3,11},{4,12},{5,13},{6,14},{7,15},{8,0},{9,1},... | collective-permute-start | bytes 331784 | tf_op jit(solution)/shard_map/ppermute | solution.py:336

commit v8 on v6

--- a/solution.py
+++ b/solution.py
@@ -320,9 +320,13 @@
     send_ref[...] = (keep_ref[...] + got_ref[...].astype(F32)).astype(BF16)
 
 
-def sum_last_kernel(keep_ref, near_ref, far_ref, first_ref, second_ref):
+def sum_back_kernel(keep_ref, far_ref, out_ref):
+    out_ref[...] = keep_ref[...] + far_ref[...].astype(F32)
+
+
+def sum_last_kernel(keep_ref, near_ref, first_ref, second_ref):
     for bank, ref in enumerate((first_ref, second_ref)):
-        ref[...] = keep_ref[bank] + near_ref[bank].astype(F32) + far_ref[bank].astype(F32)
+        ref[...] = keep_ref[bank] + near_ref[bank].astype(F32)
 
 
 def swap(value, count, distance):
@@ -473,23 +477,22 @@
             sum_near_kernel, "first_far_near", both(2), [me, far_own, far_got, *far_second], scalars=1
         )
         far_got = swap_mixed(far_send, count, 4, 2)
+        (far_send,) = local_call(sum_far_kernel, "far_last", both(2)[:1], [far_keep, far_got])
+        far_got = swap(far_send, count, 8)
         got = swap_mixed(send, count, 2, 4)
         send, keep = local_call(
             sum_near_kernel, "own_near", both(2), [me, own, got], scalars=1, wait_for=[far_send]
         )
         got = swap_mixed(send, count, 4, 2)
-        (far_send,) = local_call(
-            sum_far_kernel, "far_last", both(2)[:1], [far_keep, far_got]
-        )
-        far_got = swap(far_send, count, 8)
-        wait_for = [far_send]
+        wait_for = [send]
     (output,) = local_call(
         output_kernel, "output_conv", [like(features.shape, BF16)], [xh, bank_second], wait_for=wait_for
     )
     if direct:
+        (keep,) = local_call(sum_back_kernel, "far_back", both(2)[1:], [keep, far_got])
         out = like((rows, channels), F32)
         grad_first, grad_second = local_call(
-            sum_last_kernel, "sum_last", [out, out], [keep, got, far_got]
+            sum_last_kernel, "sum_last", [out, out], [keep, got]
         )
     else:
         grad_first, grad_second = (

time: 52.6 us -> 52.6 us (level)
    ppermute x9, waiting for transfers between devices: 10.7 us -> 12.1 us  [swap_mixed(): return lax.ppermute(value, 'slab', pairs)]
    ppermute x9, waiting for transfers between devices: 2.42 us -> 1.27 us  [swap(): lax.ppermute(value, 'slab', [(i, i ^ distance) for i in range(count)])]
    ppermute x9, starting transfers between devices: 11.5 us -> 10.8 us  [swap(): lax.ppermute(value, 'slab', [(i, i ^ distance) for i in range(count)])]
    pallas_call x15 -> x16, Pallas kernels: 12.5 us -> 12.5 us  [local_call(): pl.pallas_call(body, out_shape=list(outs), in_specs=[pl.BlockSpec(memory_...]
where the time goes in v8:
time: 52.6 us; the launch traced here: 52.4 us
  starting transfers between devices  23.5 us (45%)
  Pallas kernels  14.7 us (28%)
  waiting for transfers between devices  13.4 us (25%)
  between operations  0.78 us (1%)
    pallas_call x16, Pallas kernels, local_call(): pl.pallas_call(body, out_shape=list(outs), in_specs=[pl.BlockSpec(memory_...  12.5 us
    ppermute x9, starting transfers between devices, swap_mixed(): return lax.ppermute(value, 'slab', pairs)  12.1 us
    ppermute x9, waiting for transfers between devices, swap_mixed(): return lax.ppermute(value, 'slab', pairs)  12.1 us
    ppermute x9, starting transfers between devices, swap(): lax.ppermute(value, 'slab', [(i, i ^ distance) for i in range(count)])  10.8 us
    pallas_call x2, Pallas kernels, from_hbm(): pl.pallas_call(body, out_shape=outs, in_specs=[pl.BlockSpec(memory_space=...  2.2 us
    ppermute x9, waiting for transfers between devices, swap(): lax.ppermute(value, 'slab', [(i, i ^ distance) for i in range(count)])  1.27 us
  transfers between devices with their start and end apart: 19, of which 7 were waited for; matrix products, arithmetic and copies ran while one was open for 0% of the time, Pallas kernels for 19%

profile of v8, /device:TPU:0, one launch (start us, length us, event | category | flops | bytes accessed | tf_op | source)
XLA Modules:
  0.0 52.4 jit_solution(406756434084297522)
XLA Ops:
  0.6 1.1 %load_shards_and_edges.1 = (bf16[2,216,128]{2,1,0:T(8,128)(2,1)S(1)}, bf16[3,16,16,128]{3,2,1,0:T(8,128)(2,1)S(1)}, bf16[3,16,16,128]{3,2,1,0:T(8,128)(2,1)S(1)}) custom-call(s32[1]{0:T(128)} %bitcast.refs_0_, bf16[4,16,16,128]{3,2,1,0:T(8,128)(2,1)} %refs_0_.1, bf16[4,16,16,128]{3,2,1,0:T(8,128)(2,1)} %refs_1_.3, bf16[216,128]{1,0:T(8,128)(2,1)} %refs_3_.1, ...), custom_call_target="tpu_custom_call" | custom-call | flops 1000 | tf_op jit(solution)/shard_map/load_shards_and_edges/pallas_call | solution.py:128
  1.8 4.1 %collective-permute-start.3 = (bf16[2,216,128]{2,1,0:T(8,128)(2,1)S(1)}, bf16[2,216,128]{2,1,0:T(8,128)(2,1)S(1)}, u32[]{:S(2)}, u32[]{:S(2)}) collective-permute-start(bf16[2,216,128]{2,1,0:T(8,128)(2,1)S(1)} %get-tuple-element.37.refs_0_), channel_id=1, source_target_pairs={{0,8},{1,9},{2,10},{3,11},{4,12},{5,13},{6,14},{7,15},{8,0},{9,1},... | collective-permute-start | bytes 331784 | tf_op jit(solution)/shard_map/ppermute | solution.py:333
  5.9 0.7 %collective-permute-start.1 = (bf16[3,16,16,128]{3,2,1,0:T(8,128)(2,1)S(1)}, bf16[3,16,16,128]{3,2,1,0:T(8,128)(2,1)S(1)}, u32[]{:S(2)}, u32[]{:S(2)}) collective-permute-start(bf16[3,16,16,128]{3,2,1,0:T(8,128)(2,1)S(1)} %get-tuple-element.34.refs_2_), channel_id=1, source_target_pairs={{1,2},{2,1},{3,4},{4,3},{5,6},{6,5},{7,8},{8,7},{9,10},{10,9},{11,... | collective-permute-start | bytes 589832 | tf_op jit(solution)/shard_map/ppermute | solution.py:375
  6.5 2.9 %collective-permute-start = (bf16[3,16,16,128]{3,2,1,0:T(8,128)(2,1)S(1)}, bf16[3,16,16,128]{3,2,1,0:T(8,128)(2,1)S(1)}, u32[]{:S(2)}, u32[]{:S(2)}) collective-permute-start(bf16[3,16,16,128]{3,2,1,0:T(8,128)(2,1)S(1)} %get-tuple-element.36), channel_id=1, source_target_pairs={{0,1},{1,0},{2,3},{3,2},{4,5},{5,4},{6,7},{7,6},{8,9},{9,8},{10,11... | collective-permute-start | bytes 589832 | tf_op jit(solution)/shard_map/ppermute | solution.py:333
  9.5 1.6 %collective-permute-start.2 = (bf16[2,216,128]{2,1,0:T(8,128)(2,1)S(1)}, bf16[2,216,128]{2,1,0:T(8,128)(2,1)S(1)}, u32[]{:S(2)}, u32[]{:S(2)}) collective-permute-start(bf16[2,216,128]{2,1,0:T(8,128)(2,1)S(1)} %get-tuple-element.37.refs_0_), channel_id=1, source_target_pairs={{0,4},{1,3},{2,6},{3,1},{4,0},{5,7},{6,2},{7,5},{8,12},{9,11},{10,... | collective-permute-start | bytes 331784 | tf_op jit(solution)/shard_map/ppermute | solution.py:338
  11.0 0.2 collective-permute-done.3.refs_0_
  11.3 0.7 %collective-permute-start.4 = (bf16[2,216,128]{2,1,0:T(8,128)(2,1)S(1)}, bf16[2,216,128]{2,1,0:T(8,128)(2,1)S(1)}, u32[]{:S(2)}, u32[]{:S(2)}) collective-permute-start(bf16[2,216,128]{2,1,0:T(8,128)(2,1)S(1)} %collective-permute-done.3.refs_0_), channel_id=1, source_target_pairs={{0,4},{1,3},{2,6},{3,1},{4,0},{5,7},{6,2},{7,5},{8,12},{9,11},{10,... | collective-permute-start | bytes 331784 | tf_op jit(solution)/shard_map/ppermute | solution.py:338
  12.0 1.1 %load.1 = (bf16[4,16,16,128]{3,2,1,0:T(8,128)(2,1)S(1)}, bf16[4,16,16,128]{3,2,1,0:T(8,128)(2,1)S(1)}) custom-call(bf16[4,16,16,128]{3,2,1,0:T(8,128)(2,1)} %refs_0_.1, bf16[4,16,16,128]{3,2,1,0:T(8,128)(2,1)} %refs_1_.3, bf16[3,16,16,128]{3,2,1,0:T(8,128)(2,1)S(1)} %get-tuple-element.34.refs_2_), custom_call_target="tpu_custom_call" | custom-call | flops 1000 | tf_op jit(solution)/shard_map/load/pallas_call | solution.py:128
  13.1 1.7 %collective-permute-done.2.refs_1_ = bf16[2,216,128]{2,1,0:T(8,128)(2,1)S(1)} collective-permute-done((bf16[2,216,128]{2,1,0:T(8,128)(2,1)S(1)}, bf16[2,216,128]{2,1,0:T(8,128)(2,1)S(1)}, u32[]{:S(2)}, u32[]{:S(2)}) %collective-permute-start.2) | collective-permute-done | bytes 110624 | tf_op jit(solution)/shard_map/ppermute | solution.py:338
  14.8 1.0 %collective-permute-start.5 = (bf16[4,216,128]{2,1,0:T(8,128)(2,1)S(1)}, bf16[4,216,128]{2,1,0:T(8,128)(2,1)S(1)}, u32[]{:S(2)}, u32[]{:S(2)}) collective-permute-start(bf16[4,216,128]{2,1,0:T(8,128)(2,1)S(1)} %own_and_near.1.refs_1_), channel_id=1, source_target_pairs={{0,2},{1,5},{2,0},{3,7},{4,6},{5,1},{6,4},{7,3},{8,10},{9,13},{10,... | collective-permute-start | bytes 663560 | tf_op jit(solution)/shard_map/ppermute | solution.py:338
  15.8 0.0 collective-permute-done.1.refs_3_
  15.8 0.0 collective-permute-done.refs_2_
  15.8 0.4 feature_planes.1.refs_2_.refs_9_.refs_1_
  16.2 0.0 collective-permute-done.4.refs_1_
  16.3 1.4 %collective-permute-start.6 = (bf16[4,216,128]{2,1,0:T(8,128)(2,1)S(1)}, bf16[4,216,128]{2,1,0:T(8,128)(2,1)S(1)}, u32[]{:S(2)}, u32[]{:S(2)}) collective-permute-start(bf16[4,216,128]{2,1,0:T(8,128)(2,1)S(1)} %far_and_near.1.refs_2_), channel_id=1, source_target_pairs={{0,2},{1,5},{2,0},{3,7},{4,6},{5,1},{6,4},{7,3},{8,10},{9,13},{10,... | collective-permute-start | bytes 663560 | tf_op jit(solution)/shard_map/ppermute | solution.py:338
  17.7 0.9 %collective-permute-start.7 = (bf16[4,216,128]{2,1,0:T(8,128)(2,1)S(1)}, bf16[4,216,128]{2,1,0:T(8,128)(2,1)S(1)}, u32[]{:S(2)}, u32[]{:S(2)}) collective-permute-start(bf16[4,216,128]{2,1,0:T(8,128)(2,1)S(1)} %own_and_near.1.refs_1_), channel_id=1, source_target_pairs={{0,1},{1,0},{2,3},{3,2},{4,5},{5,4},{6,7},{7,6},{8,9},{9,8},{10,11... | collective-permute-start | bytes 663560 | tf_op jit(solution)/shard_map/ppermute | solution.py:333
  18.6 0.0 collective-permute-start.8
  18.6 2.2 %collective-permute-done.5.refs_3_ = bf16[4,216,128]{2,1,0:T(8,128)(2,1)S(1)} collective-permute-done((bf16[4,216,128]{2,1,0:T(8,128)(2,1)S(1)}, bf16[4,216,128]{2,1,0:T(8,128)(2,1)S(1)}, u32[]{:S(2)}, u32[]{:S(2)}) %collective-permute-start.5) | collective-permute-done | bytes 221216 | tf_op jit(solution)/shard_map/ppermute | solution.py:338
  20.8 0.3 collective-permute-start.9
  21.0 2.1 %collective-permute-done.6.refs_4_ = bf16[4,216,128]{2,1,0:T(8,128)(2,1)S(1)} collective-permute-done((bf16[4,216,128]{2,1,0:T(8,128)(2,1)S(1)}, bf16[4,216,128]{2,1,0:T(8,128)(2,1)S(1)}, u32[]{:S(2)}, u32[]{:S(2)}) %collective-permute-start.6) | collective-permute-done | bytes 221216 | tf_op jit(solution)/shard_map/ppermute | solution.py:338
  23.2 0.1 collective-permute-start.10
  23.3 1.5 %cotangent_planes.1 = (bf16[6,18,16,384]{3,2,1,0:T(8,128)(2,1)S(1)}, bf16[6,9,128,256]{3,2,1,0:T(8,128)(2,1)S(1)}) custom-call(s32[1]{0:T(128)} %bitcast.refs_0_, bf16[4,16,16,128]{3,2,1,0:T(8,128)(2,1)S(1)} %get-tuple-element.38.refs_1_, bf16[3,16,16,128]{3,2,1,0:T(8,128)(2,1)S(1)} %collective-permute-done.refs_2_, ...), custom_call_target="tpu_custom_call" | custom-call | flops 1000 | tf_op jit(solution)/shard_map/cotangent_planes/pallas_call | solution.py:31
  24.8 0.0 collective-permute-done.7.refs_5_
  24.8 0.0 collective-permute-done.8.refs_6_
  24.8 0.0 collective-permute-done.9.refs_7_
  24.8 0.0 collective-permute-done.10.refs_8_
  24.8 3.2 %hidden_and_second_grad.1 = (bf16[3456,128]{1,0:T(8,128)(2,1)S(1)}, bf16[4,16,16,128]{3,2,1,0:T(8,128)(2,1)S(1)}, f32[128,1024]{1,0:T(8,128)S(1)}, bf16[8,216,128]{2,1,0:T(8,128)(2,1)S(1)}, f32[8,216,128]{2,1,0:T(8,128)S(1)}) custom-call(s32[1]{0:T(128)} %bitcast.refs_0_, bf16[4,216,128]{2,1,0:T(8,128)(2,1)S(1)} %own_and_near.1.refs_1_, ...), custom_call_target="tpu_custom_call" | custom-call | flops 1000 | tf_op jit(solution)/shard_map/hidden_and_second_grad/pallas_call | solution.py:31
  28.0 0.5 collective-permute-start.11
  28.5 2.8 %first_grad.1 = (bf16[3456,128]{1,0:T(8,128)(2,1)S(1)}, bf16[8,216,128]{2,1,0:T(8,128)(2,1)S(1)}, f32[8,216,128]{2,1,0:T(8,128)S(1)}) custom-call(s32[1]{0:T(128)} %bitcast.refs_0_, bf16[4,216,128]{2,1,0:T(8,128)(2,1)S(1)} %own_and_near.1.refs_1_, bf16[4,216,128]{2,1,0:T(8,128)(2,1)S(1)} %far_and_near.1.refs_2_, ...), custom_call_target="tpu_custom_call" | custom-call | flops 1000 | tf_op jit(solution)/shard_map/first_grad/pallas_call | solution.py:31
  31.3 0.2 collective-permute-start.12
  31.5 0.0 collective-permute-done.11.refs_2_
  31.5 0.1 second_pair.1
  31.6 1.8 %collective-permute-start.15 = (bf16[2,216,128]{2,1,0:T(8,128)(2,1)S(1)}, bf16[2,216,128]{2,1,0:T(8,128)(2,1)S(1)}, u32[]{:S(2)}, u32[]{:S(2)}) collective-permute-start(bf16[2,216,128]{2,1,0:T(8,128)(2,1)S(1)} %get-tuple-element.47.refs_5_), channel_id=1, source_target_pairs={{0,2},{1,5},{2,0},{3,7},{4,6},{5,1},{6,4},{7,3},{8,10},{9,13},{10,... | collective-permute-start | bytes 331784 | tf_op jit(solution)/shard_map/ppermute | solution.py:338
  33.4 1.3 %hidden_planes.1.refs_5_.refs_0_ = bf16[6,18,16,384]{3,2,1,0:T(8,128)(2,1)S(1)} custom-call(s32[1]{0:T(128)} %bitcast.refs_0_, bf16[8,18,16,384]{3,2,1,0:T(8,128)(2,1)S(1)} %feature_planes.1.refs_2_.refs_9_.refs_1_, bf16[3456,128]{1,0:T(8,128)(2,1)S(1)} %get-tuple-element.40.refs_2_, bf16[4,16,16,128]{3,2,1,0:T(8,128)(2,1)S(1)} %get-tuple-element.41.refs_3_, ...), custom_call_target="tpu_custom_call" | custom-call | flops 1000 | tf_op jit(solution)/shard_map/hidden_planes/pallas_call | solution.py:31
  34.7 0.0 collective-permute-done.12.refs_2_
  34.7 0.1 first_pair.1
  34.8 0.4 collective-permute-start.14
  35.2 1.7 %collective-permute-start.13 = (bf16[4,216,128]{2,1,0:T(8,128)(2,1)S(1)}, bf16[4,216,128]{2,1,0:T(8,128)(2,1)S(1)}, u32[]{:S(2)}, u32[]{:S(2)}) collective-permute-start(bf16[4,216,128]{2,1,0:T(8,128)(2,1)S(1)} %get-tuple-element.53), channel_id=1, source_target_pairs={{0,2},{1,5},{2,0},{3,7},{4,6},{5,1},{6,4},{7,3},{8,10},{9,13},{10,... | collective-permute-start | bytes 663560 | tf_op jit(solution)/shard_map/ppermute | solution.py:338
  36.9 0.0 collective-permute-done.15.refs_2_
  37.0 2.7 %collective-permute-done.14.refs_2_ = bf16[2,216,128]{2,1,0:T(8,128)(2,1)S(1)} collective-permute-done((bf16[2,216,128]{2,1,0:T(8,128)(2,1)S(1)}, bf16[2,216,128]{2,1,0:T(8,128)(2,1)S(1)}, u32[]{:S(2)}, u32[]{:S(2)}) %collective-permute-start.14) | collective-permute-done | bytes 110624 | tf_op jit(solution)/shard_map/ppermute | solution.py:338
  39.7 1.4 %collective-permute-start.16 = (bf16[2,216,128]{2,1,0:T(8,128)(2,1)S(1)}, bf16[2,216,128]{2,1,0:T(8,128)(2,1)S(1)}, u32[]{:S(2)}, u32[]{:S(2)}) collective-permute-start(bf16[2,216,128]{2,1,0:T(8,128)(2,1)S(1)} %get-tuple-element.60), channel_id=1, source_target_pairs={{0,4},{1,3},{2,6},{3,1},{4,0},{5,7},{6,2},{7,5},{8,12},{9,11},{10,... | collective-permute-start | bytes 331784 | tf_op jit(solution)/shard_map/ppermute | solution.py:338
  41.1 3.4 %collective-permute-done.16.refs_1_ = bf16[2,216,128]{2,1,0:T(8,128)(2,1)S(1)} collective-permute-done((bf16[2,216,128]{2,1,0:T(8,128)(2,1)S(1)}, bf16[2,216,128]{2,1,0:T(8,128)(2,1)S(1)}, u32[]{:S(2)}, u32[]{:S(2)}) %collective-permute-start.16) | collective-permute-done | bytes 110624 | tf_op jit(solution)/shard_map/ppermute | solution.py:338
  44.5 1.8 %collective-permute-start.17 = (bf16[2,216,128]{2,1,0:T(8,128)(2,1)S(1)}, bf16[2,216,128]{2,1,0:T(8,128)(2,1)S(1)}, u32[]{:S(2)}, u32[]{:S(2)}) collective-permute-start(bf16[2,216,128]{2,1,0:T(8,128)(2,1)S(1)} %far_last.1.refs_3_), channel_id=1, source_target_pairs={{0,8},{1,9},{2,10},{3,11},{4,12},{5,13},{6,14},{7,15},{8,0},{9,1},... | collective-permute-start | bytes 331784 | tf_op jit(solution)/shard_map/ppermute | solution.py:333
  46.3 0.0 collective-permute-done.13.refs_2_
  46.4 2.1 %collective-permute-start.18 = (bf16[2,216,128]{2,1,0:T(8,128)(2,1)S(1)}, bf16[2,216,128]{2,1,0:T(8,128)(2,1)S(1)}, u32[]{:S(2)}, u32[]{:S(2)}) collective-permute-start(bf16[2,216,128]{2,1,0:T(8,128)(2,1)S(1)} %get-tuple-element.61.refs_2_), channel_id=1, source_target_pairs={{0,4},{1,3},{2,6},{3,1},{4,0},{5,7},{6,2},{7,5},{8,12},{9,11},{10,... | collective-permute-start | bytes 331784 | tf_op jit(solution)/shard_map/ppermute | solution.py:338
  48.5 2.2 %output_conv.1 = bf16[4,16,16,128]{3,2,1,0:T(8,128)(2,1)} custom-call(bf16[6,18,16,384]{3,2,1,0:T(8,128)(2,1)S(1)} %hidden_planes.1.refs_5_.refs_0_, bf16[3456,128]{1,0:T(8,128)(2,1)S(1)} %get-tuple-element.48.refs_1_, bf16[2,216,128]{2,1,0:T(8,128)(2,1)S(1)} %get-tuple-element.61.refs_2_), custom_call_target="tpu_custom_call" | custom-call | flops 1000 | tf_op jit(solution)/shard_map/output_conv/pallas_call | solution.py:31
  50.6 1.0 %collective-permute-done.17.refs_1_ = bf16[2,216,128]{2,1,0:T(8,128)(2,1)S(1)} collective-permute-done((bf16[2,216,128]{2,1,0:T(8,128)(2,1)S(1)}, bf16[2,216,128]{2,1,0:T(8,128)(2,1)S(1)}, u32[]{:S(2)}, u32[]{:S(2)}) %collective-permute-start.17) | collective-permute-done | bytes 110624 | tf_op jit(solution)/shard_map/ppermute | solution.py:333
  51.7 0.0 collective-permute-done.18.refs_1_
  51.7 0.7 %sum_last.1 = (f32[216,128]{1,0:T(8,128)}, f32[216,128]{1,0:T(8,128)}) custom-call(f32[2,216,128]{2,1,0:T(8,128)S(1)} %far_back.1.refs_0_, bf16[2,216,128]{2,1,0:T(8,128)(2,1)S(1)} %collective-permute-done.18.refs_1_), custom_call_target="tpu_custom_call" | custom-call | flops 1000 | tf_op jit(solution)/shard_map/sum_last/pallas_call | solution.py:31
  (7 shorter events, 0.2 us)
Async XLA Ops:
  1.8 9.5 %collective-permute-start.3 = (bf16[2,216,128]{2,1,0:T(8,128)(2,1)S(1)}, bf16[2,216,128]{2,1,0:T(8,128)(2,1)S(1)}, u32[]{:S(2)}, u32[]{:S(2)}) collective-permute-start(bf16[2,216,128]{2,1,0:T(8,128)(2,1)S(1)} %get-tuple-element.37.refs_0_), channel_id=1, source_target_pairs={{0,8},{1,9},{2,10},{3,11},{4,12},{5,13},{6,14},{7,15},{8,0},{9,1},... | collective-permute-start | bytes 331784 | tf_op jit(solution)/shard_map/ppermute | solution.py:333
  5.9 10.0 %collective-permute-start.1 = (bf16[3,16,16,128]{3,2,1,0:T(8,128)(2,1)S(1)}, bf16[3,16,16,128]{3,2,1,0:T(8,128)(2,1)S(1)}, u32[]{:S(2)}, u32[]{:S(2)}) collective-permute-start(bf16[3,16,16,128]{3,2,1,0:T(8,128)(2,1)S(1)} %get-tuple-element.34.refs_2_), channel_id=1, source_target_pairs={{1,2},{2,1},{3,4},{4,3},{5,6},{6,5},{7,8},{8,7},{9,10},{10,9},{11,... | collective-permute-start | bytes 589832 | tf_op jit(solution)/shard_map/ppermute | solution.py:375
  6.5 9.3 %collective-permute-start = (bf16[3,16,16,128]{3,2,1,0:T(8,128)(2,1)S(1)}, bf16[3,16,16,128]{3,2,1,0:T(8,128)(2,1)S(1)}, u32[]{:S(2)}, u32[]{:S(2)}) collective-permute-start(bf16[3,16,16,128]{3,2,1,0:T(8,128)(2,1)S(1)} %get-tuple-element.36), channel_id=1, source_target_pairs={{0,1},{1,0},{2,3},{3,2},{4,5},{5,4},{6,7},{7,6},{8,9},{9,8},{10,11... | collective-permute-start | bytes 589832 | tf_op jit(solution)/shard_map/ppermute | solution.py:333
  9.5 5.3 %collective-permute-start.2 = (bf16[2,216,128]{2,1,0:T(8,128)(2,1)S(1)}, bf16[2,216,128]{2,1,0:T(8,128)(2,1)S(1)}, u32[]{:S(2)}, u32[]{:S(2)}) collective-permute-start(bf16[2,216,128]{2,1,0:T(8,128)(2,1)S(1)} %get-tuple-element.37.refs_0_), channel_id=1, source_target_pairs={{0,4},{1,3},{2,6},{3,1},{4,0},{5,7},{6,2},{7,5},{8,12},{9,11},{10,... | collective-permute-start | bytes 331784 | tf_op jit(solution)/shard_map/ppermute | solution.py:338
  11.3 4.9 %collective-permute-start.4 = (bf16[2,216,128]{2,1,0:T(8,128)(2,1)S(1)}, bf16[2,216,128]{2,1,0:T(8,128)(2,1)S(1)}, u32[]{:S(2)}, u32[]{:S(2)}) collective-permute-start(bf16[2,216,128]{2,1,0:T(8,128)(2,1)S(1)} %collective-permute-done.3.refs_0_), channel_id=1, source_target_pairs={{0,4},{1,3},{2,6},{3,1},{4,0},{5,7},{6,2},{7,5},{8,12},{9,11},{10,... | collective-permute-start | bytes 331784 | tf_op jit(solution)/shard_map/ppermute | solution.py:338
  14.8 6.0 %collective-permute-start.5 = (bf16[4,216,128]{2,1,0:T(8,128)(2,1)S(1)}, bf16[4,216,128]{2,1,0:T(8,128)(2,1)S(1)}, u32[]{:S(2)}, u32[]{:S(2)}) collective-permute-start(bf16[4,216,128]{2,1,0:T(8,128)(2,1)S(1)} %own_and_near.1.refs_1_), channel_id=1, source_target_pairs={{0,2},{1,5},{2,0},{3,7},{4,6},{5,1},{6,4},{7,3},{8,10},{9,13},{10,... | collective-permute-start | bytes 663560 | tf_op jit(solution)/shard_map/ppermute | solution.py:338
  16.3 6.9 %collective-permute-start.6 = (bf16[4,216,128]{2,1,0:T(8,128)(2,1)S(1)}, bf16[4,216,128]{2,1,0:T(8,128)(2,1)S(1)}, u32[]{:S(2)}, u32[]{:S(2)}) collective-permute-start(bf16[4,216,128]{2,1,0:T(8,128)(2,1)S(1)} %far_and_near.1.refs_2_), channel_id=1, source_target_pairs={{0,2},{1,5},{2,0},{3,7},{4,6},{5,1},{6,4},{7,3},{8,10},{9,13},{10,... | collective-permute-start | bytes 663560 | tf_op jit(solution)/shard_map/ppermute | solution.py:338
  17.7 7.1 %collective-permute-start.7 = (bf16[4,216,128]{2,1,0:T(8,128)(2,1)S(1)}, bf16[4,216,128]{2,1,0:T(8,128)(2,1)S(1)}, u32[]{:S(2)}, u32[]{:S(2)}) collective-permute-start(bf16[4,216,128]{2,1,0:T(8,128)(2,1)S(1)} %own_and_near.1.refs_1_), channel_id=1, source_target_pairs={{0,1},{1,0},{2,3},{3,2},{4,5},{5,4},{6,7},{7,6},{8,9},{9,8},{10,11... | collective-permute-start | bytes 663560 | tf_op jit(solution)/shard_map/ppermute | solution.py:333
  18.6 6.2 %collective-permute-start.8 = (bf16[4,216,128]{2,1,0:T(8,128)(2,1)S(1)}, bf16[4,216,128]{2,1,0:T(8,128)(2,1)S(1)}, u32[]{:S(2)}, u32[]{:S(2)}) collective-permute-start(bf16[4,216,128]{2,1,0:T(8,128)(2,1)S(1)} %far_and_near.1.refs_2_), channel_id=1, source_target_pairs={{0,1},{1,0},{2,3},{3,2},{4,5},{5,4},{6,7},{7,6},{8,9},{9,8},{10,11... | collective-permute-start | bytes 663560 | tf_op jit(solution)/shard_map/ppermute | solution.py:333
  20.8 4.0 %collective-permute-start.9 = (bf16[4,216,128]{2,1,0:T(8,128)(2,1)S(1)}, bf16[4,216,128]{2,1,0:T(8,128)(2,1)S(1)}, u32[]{:S(2)}, u32[]{:S(2)}) collective-permute-start(bf16[4,216,128]{2,1,0:T(8,128)(2,1)S(1)} %collective-permute-done.5.refs_3_), channel_id=1, source_target_pairs={{0,1},{1,0},{2,3},{3,2},{4,5},{5,4},{6,7},{7,6},{8,9},{9,8},{10,11... | collective-permute-start | bytes 663560 | tf_op jit(solution)/shard_map/ppermute | solution.py:333
  23.2 1.7 %collective-permute-start.10 = (bf16[4,216,128]{2,1,0:T(8,128)(2,1)S(1)}, bf16[4,216,128]{2,1,0:T(8,128)(2,1)S(1)}, u32[]{:S(2)}, u32[]{:S(2)}) collective-permute-start(bf16[4,216,128]{2,1,0:T(8,128)(2,1)S(1)} %collective-permute-done.6.refs_4_), channel_id=1, source_target_pairs={{0,1},{1,0},{2,3},{3,2},{4,5},{5,4},{6,7},{7,6},{8,9},{9,8},{10,11... | collective-permute-start | bytes 663560 | tf_op jit(solution)/shard_map/ppermute | solution.py:333
  28.0 3.5 %collective-permute-start.11 = (bf16[8,216,128]{2,1,0:T(8,128)(2,1)S(1)}, bf16[8,216,128]{2,1,0:T(8,128)(2,1)S(1)}, u32[]{:S(2)}, u32[]{:S(2)}) collective-permute-start(bf16[8,216,128]{2,1,0:T(8,128)(2,1)S(1)} %get-tuple-element.46), channel_id=1, source_target_pairs={{0,1},{1,0},{2,3},{3,2},{4,5},{5,4},{6,7},{7,6},{8,9},{9,8},{10,11... | collective-permute-start | bytes 1327112 | tf_op jit(solution)/shard_map/ppermute | solution.py:333
  31.3 3.4 %collective-permute-start.12 = (bf16[8,216,128]{2,1,0:T(8,128)(2,1)S(1)}, bf16[8,216,128]{2,1,0:T(8,128)(2,1)S(1)}, u32[]{:S(2)}, u32[]{:S(2)}) collective-permute-start(bf16[8,216,128]{2,1,0:T(8,128)(2,1)S(1)} %get-tuple-element.49), channel_id=1, source_target_pairs={{0,1},{1,0},{2,3},{3,2},{4,5},{5,4},{6,7},{7,6},{8,9},{9,8},{10,11... | collective-permute-start | bytes 1327112 | tf_op jit(solution)/shard_map/ppermute | solution.py:333
  31.6 5.3 %collective-permute-start.15 = (bf16[2,216,128]{2,1,0:T(8,128)(2,1)S(1)}, bf16[2,216,128]{2,1,0:T(8,128)(2,1)S(1)}, u32[]{:S(2)}, u32[]{:S(2)}) collective-permute-start(bf16[2,216,128]{2,1,0:T(8,128)(2,1)S(1)} %get-tuple-element.47.refs_5_), channel_id=1, source_target_pairs={{0,2},{1,5},{2,0},{3,7},{4,6},{5,1},{6,4},{7,3},{8,10},{9,13},{10,... | collective-permute-start | bytes 331784 | tf_op jit(solution)/shard_map/ppermute | solution.py:338
  34.8 4.8 %collective-permute-start.14 = (bf16[2,216,128]{2,1,0:T(8,128)(2,1)S(1)}, bf16[2,216,128]{2,1,0:T(8,128)(2,1)S(1)}, u32[]{:S(2)}, u32[]{:S(2)}) collective-permute-start(bf16[2,216,128]{2,1,0:T(8,128)(2,1)S(1)} %get-tuple-element.55.refs_3_), channel_id=1, source_target_pairs={{0,2},{1,5},{2,0},{3,7},{4,6},{5,1},{6,4},{7,3},{8,10},{9,13},{10,... | collective-permute-start | bytes 331784 | tf_op jit(solution)/shard_map/ppermute | solution.py:338
  35.2 11.1 %collective-permute-start.13 = (bf16[4,216,128]{2,1,0:T(8,128)(2,1)S(1)}, bf16[4,216,128]{2,1,0:T(8,128)(2,1)S(1)}, u32[]{:S(2)}, u32[]{:S(2)}) collective-permute-start(bf16[4,216,128]{2,1,0:T(8,128)(2,1)S(1)} %get-tuple-element.53), channel_id=1, source_target_pairs={{0,2},{1,5},{2,0},{3,7},{4,6},{5,1},{6,4},{7,3},{8,10},{9,13},{10,... | collective-permute-start | bytes 663560 | tf_op jit(solution)/shard_map/ppermute | solution.py:338
  39.7 4.8 %collective-permute-start.16 = (bf16[2,216,128]{2,1,0:T(8,128)(2,1)S(1)}, bf16[2,216,128]{2,1,0:T(8,128)(2,1)S(1)}, u32[]{:S(2)}, u32[]{:S(2)}) collective-permute-start(bf16[2,216,128]{2,1,0:T(8,128)(2,1)S(1)} %get-tuple-element.60), channel_id=1, source_target_pairs={{0,4},{1,3},{2,6},{3,1},{4,0},{5,7},{6,2},{7,5},{8,12},{9,11},{10,... | collective-permute-start | bytes 331784 | tf_op jit(solution)/shard_map/ppermute | solution.py:338
  44.5 7.1 %collective-permute-start.17 = (bf16[2,216,128]{2,1,0:T(8,128)(2,1)S(1)}, bf16[2,216,128]{2,1,0:T(8,128)(2,1)S(1)}, u32[]{:S(2)}, u32[]{:S(2)}) collective-permute-start(bf16[2,216,128]{2,1,0:T(8,128)(2,1)S(1)} %far_last.1.refs_3_), channel_id=1, source_target_pairs={{0,8},{1,9},{2,10},{3,11},{4,12},{5,13},{6,14},{7,15},{8,0},{9,1},... | collective-permute-start | bytes 331784 | tf_op jit(solution)/shard_map/ppermute | solution.py:333
  46.4 5.3 %collective-permute-start.18 = (bf16[2,216,128]{2,1,0:T(8,128)(2,1)S(1)}, bf16[2,216,128]{2,1,0:T(8,128)(2,1)S(1)}, u32[]{:S(2)}, u32[]{:S(2)}) collective-permute-start(bf16[2,216,128]{2,1,0:T(8,128)(2,1)S(1)} %get-tuple-element.61.refs_2_), channel_id=1, source_target_pairs={{0,4},{1,3},{2,6},{3,1},{4,0},{5,7},{6,2},{7,5},{8,12},{9,11},{10,... | collective-permute-start | bytes 331784 | tf_op jit(solution)/shard_map/ppermute | solution.py:338
